TPU v7x, 1024 devices: a whole 4x4x32 slice. The times are simulated.
1024 devices in a mesh: dp: 32 (over z), expert: 32 (over y, x, core).
Axes of the slice: x: 4, y: 4, z: 32, core: 2. Of those that a mesh axis runs over, the one named last changes fastest.
Arguments:
- tokens: bfloat16 [32768, 4096], P('dp', 'expert'), may hold values from -6 to 6
- cotangent: bfloat16 [32768, 4096], P('dp', 'expert'), may hold values from -6 to 6
- expert_ids: int32 [32768, 8], P('dp'), may hold values from 0 to 127, all different within a row; in each aligned block of 1024 rows (0 to 1023, 1024 to 2047, ...) at most 128 rows name the same one
- gate_values: float32 [32768, 8], P('dp'), may hold values from 0.05 to 0.5
- gate_proj: bfloat16 [6144, 4096], P('expert'), may hold values from -0.09375 to 0.09375
- up_proj: bfloat16 [6144, 4096], P('expert'), may hold values from -0.09375 to 0.09375
- down_proj: bfloat16 [6144, 4096], P('expert'), may hold values from -0.15625 to 0.15625
- probe: bfloat16 [6144, 4096], P('expert'), may hold values from -0.09375 to 0.09375
Outputs:
- hessian_probe: bfloat16 [6144, 4096], P('expert', 'dp')
Inputs may be any that keep to these rules, and one draw needn't show every extreme that they name: `expert_ids`: each row names 8 different experts. In each aligned block of 1024 rows (the rows of one index of dp) no expert is named by more than 128 rows, a bound that some block reaches.
All inputs are finite; a program needn't handle non-finite values.
Results may differ from a plain program's by a relative error of at most 0.0058.
Values may be sent and summed in bfloat16 or wider, within the bound.
No kernel may reach another device: no remote copies, remote signals or barrier semaphores. Data moves between devices by JAX's collectives and lax.ppermute only.
A program may use at most 32 MiB of HBM per device.

v0:
```python
import jax
import jax.numpy as jnp
from jax import lax
from jax.sharding import PartitionSpec as P

FF = 1536
EXPERTS = 128
TOPK = 8


def on_device(tokens, cotangent, expert_ids, gate_values, gate_proj, up_proj, down_proj, probe):
    groups = lax.axis_size("expert")
    hid_dev = gate_proj.shape[0]
    window = groups * hid_dev // FF
    per_expert = groups // window
    tok_rows = tokens.shape[0]
    capacity = tok_rows * TOPK * 2 // EXPERTS
    named = expert_ids[:, :, None] == jnp.arange(window, dtype=jnp.int32)[None, None, :]
    present = jnp.any(named, axis=1)
    gate_sum = jnp.sum(jnp.where(named, gate_values[:, :, None], 0.0), axis=1)
    slot_of = jnp.cumsum(present.astype(jnp.int32), axis=0) - 1
    slot_index = jnp.arange(capacity, dtype=jnp.int32)
    placer = present.T[:, None, :] & (slot_of.T[:, None, :] == slot_index[None, :, None])
    place_half = placer.astype(jnp.bfloat16)
    feature_slots = jnp.einsum(
        "ect,td->ecd", place_half, tokens, preferred_element_type=jnp.float32
    ).astype(jnp.bfloat16)
    cot_slots = jnp.einsum("ect,td->ecd", place_half, cotangent, preferred_element_type=jnp.float32)
    factor = jnp.sum(jnp.where(placer, gate_sum.T[:, None, :], 0.0), axis=2)
    weighted_slots = (factor[:, :, None] * cot_slots).astype(jnp.bfloat16)
    send_x = jnp.repeat(feature_slots, per_expert, axis=0)
    send_c = jnp.repeat(weighted_slots, per_expert, axis=0)
    owned_x, owned_c = (
        lax.all_to_all(send_x, "expert", split_axis=0, concat_axis=2, tiled=True),
        lax.all_to_all(send_c, "expert", split_axis=0, concat_axis=2, tiled=True),
    )
    rows_x = owned_x[0]
    rows_c = owned_c[0]
    contract = (((1,), (1,)), ((), ()))
    preact = lax.dot_general(gate_proj, rows_x, contract, preferred_element_type=jnp.float32)
    linear = lax.dot_general(up_proj, rows_x, contract, preferred_element_type=jnp.float32)
    probe_pre = lax.dot_general(probe, rows_x, contract, preferred_element_type=jnp.float32)
    backward = lax.dot_general(down_proj, rows_c, contract, preferred_element_type=jnp.float32)
    sigmoid_pre = jax.nn.sigmoid(preact)
    curvature = sigmoid_pre * (1.0 - sigmoid_pre) * (2.0 + preact * (1.0 - 2.0 * sigmoid_pre))
    tangent = (backward * linear * curvature * probe_pre).astype(jnp.bfloat16)
    result = lax.psum_scatter(
        lax.dot_general(
            rows_x, tangent, (((0,), (1,)), ((), ())), preferred_element_type=jnp.float32
        ),
        "dp",
        scatter_dimension=0,
        tiled=True,
    ).T
    return result.astype(jnp.bfloat16)


def solution(mesh):
    return jax.shard_map(
        on_device,
        mesh=mesh,
        in_specs=(
            P("dp", "expert"),
            P("dp", "expert"),
            P("dp", None),
            P("dp", None),
            P("expert", None),
            P("expert", None),
            P("expert", None),
            P("expert", None),
        ),
        out_specs=P("expert", "dp"),
        check_vma=False,
    )
```

profile of v0, /device:TPU:2, one launch (start us, length us, event | category | flops | bytes accessed | tf_op | source)
XLA Modules:
  0.0 217.5 jit_solution(12935966616227265904)
XLA Ops:
  6.5 0.0 copy-start
  6.5 0.9 fusion.25
  7.5 1.1 reduce-window.6
  8.6 0.2 slice_reduce_fusion
  8.9 0.2 reduce-window.9
  9.0 0.1 add_bitcast_fusion
  9.1 1.5 fusion.11
  10.6 0.1 copy.15
  10.8 0.0 copy-start.1
  10.8 0.0 copy-start.2
  10.8 0.0 copy-start.4
  10.8 1.2 broadcast_in_dim.38
  12.0 16.8 %all-to-all-start = ((bf16[32,128,128]{1,2,0:T(8,128)(2,1)}), bf16[32,128,128]{1,2,0:T(8,128)(2,1)S(1)}, u32[]{:S(2)}, u32[]{:S(2)}) async-start(bf16[32,128,128]{1,2,0:T(8,128)(2,1)} %bitcast.60), calls=%async_computation | async-start | bytes 2097152 | tf_op jit(solution)/shard_map/all_to_all | solution.py:34
  28.8 0.0 copy-done.1
  28.8 0.0 copy-done.2
  28.8 0.1 select_reduce_fusion.1
  28.9 0.5 select_reduce_fusion
  29.4 0.0 copy-done.4
  29.4 0.5 fusion.8
  30.0 0.1 copy.16
  30.1 14.9 %all-to-all-done = bf16[32,128,128]{1,2,0:T(8,128)(2,1)S(1)} async-done(((bf16[32,128,128]{1,2,0:T(8,128)(2,1)}), bf16[32,128,128]{1,2,0:T(8,128)(2,1)S(1)}, u32[]{:S(2)}, u32[]{:S(2)}) %all-to-all-start) | async-done | bytes 1048608 | tf_op jit(solution)/shard_map/all_to_all | solution.py:34
  45.0 1.3 broadcast_in_dim.43
  46.3 5.7 %all-to-all-start.1 = ((bf16[32,128,128]{1,2,0:T(8,128)(2,1)}), bf16[32,128,128]{1,2,0:T(8,128)(2,1)}, u32[]{:S(2)}, u32[]{:S(2)}) async-start(bf16[32,128,128]{1,2,0:T(8,128)(2,1)} %bitcast.61), calls=%async_computation.1 | async-start | bytes 2097152 | tf_op jit(solution)/shard_map/all_to_all | solution.py:35
  52.0 0.0 reduce-scatter.2.cloned.1.call-start
  52.1 2.0 convolution_bitcast_fusion.1
  54.0 14.2 %all-to-all-done.1 = bf16[32,128,128]{1,2,0:T(8,128)(2,1)} async-done(((bf16[32,128,128]{1,2,0:T(8,128)(2,1)}), bf16[32,128,128]{1,2,0:T(8,128)(2,1)}, u32[]{:S(2)}, u32[]{:S(2)}) %all-to-all-start.1) | async-done | bytes 1048608 | tf_op jit(solution)/shard_map/all_to_all | solution.py:35
  68.3 0.0 copy-start.3
  68.3 2.4 %fusion.27 = f32[128,192]{0,1:T(8,128)S(1)} fusion(bf16[192,4096]{1,0:T(8,128)(2,1)} %param.14, bf16[128,4096]{0,1:T(8,128)(2,1)} %bitcast.11), kind=kOutput, calls=%fused_computation.33 | convolution fusion | flops 201326592 | bytes 2719744 | tf_op jit(solution)/shard_map/dot_general | solution.py:43
  70.7 0.0 copy-done.3
  70.7 0.6 fusion.16
  71.2 0.0 copy-done
  71.2 2.7 %fusion.18 = f32[4096,192]{0,1:T(8,128)} fusion(bf16[128,4096]{0,1:T(8,128)(2,1)S(1)} %bitcast.59, f32[192,128]{1,0:T(8,128)S(1)} %fusion.16, bf16[192,4096]{1,0:T(8,128)(2,1)S(1)} %copy-done), kind=kOutput, calls=%fused_computation.15 | convolution fusion | flops 402702336 | bytes 5865472 | tf_op jit(solution)/shard_map/dot_general | solution.py:48
  74.0 0.0 reduce-scatter.2.cloned.1.call-update
  74.0 135.2 %reduce-scatter.2.cloned.1.call-done = f32[128,192]{0,1:T(8,128)} async-done(((f32[4096,192]{0,1:T(8,128)}), f32[128,192]{0,1:T(8,128)}) %reduce-scatter.2.cloned.1.call-update) | async-done | bytes 98320 | tf_op jit(solution)/shard_map/reduce_scatter | solution.py:47
  209.2 1.5 convert_bitcast_fusion
  (3 shorter events, 0.0 us)
Async XLA Ops:
  6.5 64.7 %copy-start = (bf16[192,4096]{1,0:T(8,128)(2,1)S(1)}, bf16[192,4096]{1,0:T(8,128)(2,1)}, u32[]{:S(2)}) copy-start(bf16[192,4096]{1,0:T(8,128)(2,1)} %param.15) | copy-start | bytes 4718596
  10.8 18.0 %copy-start.1 = (s32[1024,8]{0,1:T(8,128)S(1)}, s32[1024,8]{0,1:T(8,128)}, u32[]{:S(2)}) copy-start(s32[1024,8]{0,1:T(8,128)} %param.10) | copy-start | bytes 98308
  10.8 18.0 %copy-start.2 = (f32[1024,8]{0,1:T(8,128)S(1)}, f32[1024,8]{0,1:T(8,128)}, u32[]{:S(2)}) copy-start(f32[1024,8]{0,1:T(8,128)} %param.11) | copy-start | bytes 98308
  10.8 18.6 %copy-start.4 = (bf16[1024,128]{1,0:T(8,128)(2,1)S(1)}, bf16[1024,128]{1,0:T(8,128)(2,1)}, u32[]{:S(2)}) copy-start(bf16[1024,128]{1,0:T(8,128)(2,1)} %param.9) | copy-start | bytes 786436
  12.0 33.0 %all-to-all-start = ((bf16[32,128,128]{1,2,0:T(8,128)(2,1)}), bf16[32,128,128]{1,2,0:T(8,128)(2,1)S(1)}, u32[]{:S(2)}, u32[]{:S(2)}) async-start(bf16[32,128,128]{1,2,0:T(8,128)(2,1)} %bitcast.60), calls=%async_computation | async-start | bytes 2097152 | tf_op jit(solution)/shard_map/all_to_all | solution.py:34
  46.3 22.0 %all-to-all-start.1 = ((bf16[32,128,128]{1,2,0:T(8,128)(2,1)}), bf16[32,128,128]{1,2,0:T(8,128)(2,1)}, u32[]{:S(2)}, u32[]{:S(2)}) async-start(bf16[32,128,128]{1,2,0:T(8,128)(2,1)} %bitcast.61), calls=%async_computation.1 | async-start | bytes 2097152 | tf_op jit(solution)/shard_map/all_to_all | solution.py:35
  52.0 157.2 %reduce-scatter.2.cloned.1.call-start = ((), (), s32[]{:S(2)}) async-start(), calls=%async_computation.3 | async-start | bytes 3244032 | tf_op jit(solution)/shard_map/reduce_scatter | solution.py:47
  68.3 2.4 %copy-start.3 = (bf16[192,4096]{1,0:T(8,128)(2,1)S(1)}, bf16[192,4096]{1,0:T(8,128)(2,1)}, u32[]{:S(2)}) copy-start(bf16[192,4096]{1,0:T(8,128)(2,1)} %param.13) | copy-start | bytes 4718596
Sparse Core Ops, SparseCore 0:
  74.1 135.0 reduce-scatter.1
where the time goes:
time: 218 us
  waiting for transfers between devices  164 us (75%)
  starting transfers between devices  22.5 us (10%)
  between operations  13.5 us (6%)
  matrix products  9.68 us (4%)
  other arithmetic  4.44 us (2%)
  local copies, waits for them, and re-layouts  3.02 us (1%)
    reduce_scatter x1, waiting for transfers between devices, on_device(): lax.psum_scatter(lax.dot_general(rows_x, tangent, (((0,), (1,)), ((), ())...  135 us
    all_to_all x1, starting transfers between devices, on_device(): lax.all_to_all(send_x, 'expert', split_axis=0, concat_axis=2, tiled=True)  16.8 us
    all_to_all x1, waiting for transfers between devices, on_device(): lax.all_to_all(send_x, 'expert', split_axis=0, concat_axis=2, tiled=True)  14.9 us
    all_to_all x1, waiting for transfers between devices, on_device(): lax.all_to_all(send_c, 'expert', split_axis=0, concat_axis=2, tiled=True)  14.2 us
    all_to_all x1, starting transfers between devices, on_device(): lax.all_to_all(send_c, 'expert', split_axis=0, concat_axis=2, tiled=True)  5.7 us
  transfers between devices with their start and end apart: 3, of which 3 were waited for; matrix products, arithmetic and copies ran while one was open for 1% of the time, Pallas kernels for 0%

commit v1 on v0

v1 whole, which is shorter than its diff:
```python
import functools

import jax
import jax.numpy as jnp
from jax import lax
from jax.experimental import pallas as pl
from jax.experimental.pallas import tpu as pltpu
from jax.sharding import PartitionSpec as P

WIN = 4
CAP = 128
ZN, ZLO, ZHI = 32, 8, 4
F32, BF16 = jnp.float32, jnp.bfloat16
DPX = ("dp", "expert")
SMEM = pl.BlockSpec(memory_space=pltpu.SMEM)
VMEM = pl.BlockSpec(memory_space=pltpu.VMEM)


def dot(a, b):
    return jnp.dot(a, b, preferred_element_type=F32)


def prep_kernel(y_ref, ids_ref, gates_ref, tok_ref, cot_ref, send_ref, *rot_refs):
    y = y_ref[0]
    rows = tok_ref.shape[0]
    ids = ids_ref[...]
    gates = gates_ref[...]
    present, gate = [], []
    for j in range(WIN):
        named = ids == (y + j) % WIN
        present.append(jnp.max(jnp.where(named, 1.0, 0.0), axis=0, keepdims=True))
        gate.append(jnp.sum(jnp.where(named, gates, 0.0), axis=0, keepdims=True))
    marks = jnp.concatenate(present + present, axis=0)
    upper = (
        lax.broadcasted_iota(jnp.int32, (CAP, CAP), 0)
        <= lax.broadcasted_iota(jnp.int32, (CAP, CAP), 1)
    ).astype(BF16)
    base = jnp.full((2 * WIN, 1), -1.0, F32)
    slots = []
    for b in range(rows // CAP):
        part = dot(marks[:, b * CAP : (b + 1) * CAP].astype(BF16), upper)
        slots.append(part + base)
        base = base + part[:, CAP - 1 :]
    slot = jnp.concatenate(slots, axis=1)
    slot = jnp.where(marks > 0.0, slot, -1.0).astype(jnp.int32)
    both = jnp.concatenate([tok_ref[...], cot_ref[...]], axis=1)
    index = lax.broadcasted_iota(jnp.int32, (CAP, rows), 0)
    for j in range(WIN):
        placer = slot[j : j + 1, :] == index
        got = dot(jnp.where(placer, 1.0, 0.0).astype(BF16), both)
        factor = jnp.sum(jnp.where(placer, gate[j], 0.0), axis=1, keepdims=True)
        xs = got[:, :CAP]
        cs = got[:, CAP:] * factor
        rot_refs[j][...] = xs.astype(BF16)
        chunk = jnp.concatenate([xs.T, cs.T], axis=0).astype(BF16)
        for x in range(WIN):
            send_ref[((y + j) % WIN) * WIN + x] = chunk


def tangent_kernel(c_ref, own_ref, oth_ref, g_ref, u_ref, d_ref, p_ref, out_ref):
    c = c_ref[0]
    hid = g_ref.shape[0]
    accs = [jnp.zeros((hid, CAP), F32) for _ in range(4)]
    for s in range(0, 16, 2):
        for ref, side in ((own_ref, c), (oth_ref, 1 - c)):
            cols = [
                pl.ds(pl.multiple_of((2 * (s + t) + side) * CAP, CAP), CAP)
                for t in range(2)
            ]
            xs = jnp.concatenate([ref[s, :CAP], ref[s + 1, :CAP]], axis=0)
            cs = jnp.concatenate([ref[s, CAP:], ref[s + 1, CAP:]], axis=0)
            for n, (w_ref, rhs) in enumerate(
                ((g_ref, xs), (u_ref, xs), (p_ref, xs), (d_ref, cs))
            ):
                lhs = jnp.concatenate([w_ref[:, cols[0]], w_ref[:, cols[1]]], axis=1)
                accs[n] = accs[n] + dot(lhs, rhs)
    preact, linear, probe_pre, backward = accs
    sig = 1.0 / (1.0 + jnp.exp(-preact))
    curvature = sig * (1.0 - sig) * (2.0 + preact * (1.0 - 2.0 * sig))
    tangent = (backward * linear * curvature * probe_pre).astype(BF16)
    for i in range(ZLO):
        out_ref[i] = tangent


def outer_kernel(offsets, at_ref, tan_ref, own_ref, oth_ref, *out_refs):
    zhi, e, x, c = at_ref[0], at_ref[1], at_ref[2], at_ref[3]
    for m, out_ref in zip(offsets, out_refs, strict=True):
        j = (e - zhi - m + 2 * WIN) % WIN
        acc = None
        for dx in range(WIN):
            chip = (x - dx + WIN) % WIN
            lhs = jnp.concatenate(
                [tan_ref[2 * chip + c], tan_ref[2 * chip + 1 - c]], axis=1
            )
            rhs = jnp.concatenate([own_ref[dx, j], oth_ref[dx, j]], axis=0)
            part = dot(lhs, rhs)
            acc = part if acc is None else acc + part
        out_ref[...] = acc.astype(out_ref.dtype)


def call(kernel, out_shape, specs, flops, nbytes):
    return pl.pallas_call(
        kernel,
        out_shape=out_shape,
        in_specs=specs,
        out_specs=jax.tree.map(lambda _: VMEM, out_shape),
        compiler_params=pltpu.CompilerParams(vmem_limit_bytes=40 * 1024 * 1024),
        cost_estimate=pl.CostEstimate(
            flops=flops, bytes_accessed=nbytes, transcendentals=0
        ),
    )


def sds(shape, dtype):
    return jax.ShapeDtypeStruct(shape, dtype)


def on_device(tokens, cotangent, expert_ids, gate_values, gate_proj, up_proj, down_proj, probe):
    z, h = lax.axis_index("dp"), lax.axis_index("expert")
    zhi, e, x, c = z // ZLO, h // 8, (h // 2) % WIN, h % 2
    hid, feats = gate_proj.shape[0], tokens.shape[1]
    at = jnp.stack([zhi, e, x, c]).astype(jnp.int32)

    prepared = call(
        prep_kernel,
        [sds((16, 2 * feats, CAP), BF16)] + [sds((CAP, feats), BF16)] * WIN,
        [SMEM] + [VMEM] * 4,
        2 * 512 * 1024 * 256,
        2 << 20,
    )(at[1:2], expert_ids.T, gate_values.T, tokens, cotangent)
    send, rotated = prepared[0], prepared[1:]

    same_core = [[c0 + 2 * i for i in range(16)] for c0 in range(2)]
    own = lax.all_to_all(
        send, "expert", split_axis=0, concat_axis=0, tiled=True, axis_index_groups=same_core
    )
    swap = [(i, i ^ 1) for i in range(32)]
    oth = lax.ppermute(own, "expert", swap)

    moved = []
    for j in range(WIN):
        perm = [
            (i * 32 + k, (i // 8 * 8 + k % 8) * 32 + ((k // 8 + j) % 4) * 8 + i % 8)
            for i in range(ZN)
            for k in range(32)
        ]
        moved.append(lax.ppermute(rotated[j], DPX, perm))
    mine = jnp.stack(moved)
    ring = [mine]
    for dx in range(1, WIN):
        perm = [(k, k // 8 * 8 + (k // 2 % 4 + dx) % 4 * 2 + k % 2) for k in range(32)]
        ring.append(lax.ppermute(mine, "expert", perm))
    own_t = jnp.stack(ring)
    oth_t = lax.ppermute(own_t, "expert", swap)

    tangent = call(
        tangent_kernel,
        sds((ZLO, hid, CAP), BF16),
        [SMEM] + [VMEM] * 6,
        2 * 4 * hid * 4096 * CAP,
        9 << 20,
    )(at[3:4], own, oth, gate_proj, up_proj, down_proj, probe)
    near = [[8 * a + b for b in range(8)] for a in range(4)]
    tangents = lax.all_to_all(
        tangent, "dp", split_axis=0, concat_axis=0, tiled=True, axis_index_groups=near
    )

    def outer(offsets, dtype):
        return call(
            functools.partial(outer_kernel, offsets),
            [sds((hid, feats), dtype) for _ in offsets],
            [SMEM] + [VMEM] * 3,
            2 * len(offsets) * hid * 1024 * CAP,
            2 << 20,
        )(at, tangents, own_t, oth_t)

    def hop(value, by):
        return lax.ppermute(value, "dp", [(i, (i + by) % ZN) for i in range(ZN)])

    (far,) = outer((2,), BF16)
    half = hid // 2
    from_below, from_above = hop(far[:half], ZLO), hop(far[half:], -ZLO)
    here, up, down = outer((0, 1, 3), F32)
    up = jnp.concatenate([up[:half] + from_below.astype(F32), up[half:]]).astype(BF16)
    down = jnp.concatenate([down[:half], down[half:] + from_above.astype(F32)]).astype(BF16)
    total = here + hop(up, ZLO).astype(F32) + hop(down, -ZLO).astype(F32)
    return total.astype(BF16)


def solution(mesh):
    return jax.shard_map(
        on_device,
        mesh=mesh,
        in_specs=(
            P("dp", "expert"),
            P("dp", "expert"),
            P("dp", None),
            P("dp", None),
            P("expert", None),
            P("expert", None),
            P("expert", None),
            P("expert", None),
        ),
        out_specs=P("expert", "dp"),
        check_vma=False,
    )
```

time: 218 us -> 162 us (0.74)
  the two profiles are of different devices: /device:TPU:2 before, /device:TPU:8 now
where the time goes in v1:
time: 162 us; the launch traced here: 161 us
  starting transfers between devices  92.9 us (57%)
  blocking collectives  26.5 us (16%)
  waiting for transfers between devices  25.6 us (16%)
  local copies, waits for them, and re-layouts  7.78 us (5%)
  Pallas kernels  6.81 us (4%)
    ppermute x3, starting transfers between devices, on_device(): ring.append(lax.ppermute(mine, 'expert', perm))  36.9 us
    ppermute x4, starting transfers between devices, hop(): return lax.ppermute(value, 'dp', [(i, (i + by) % ZN) for i in range(ZN)])  32.9 us
    all_to_all x1, blocking collectives, on_device(): lax.all_to_all(send, 'expert', split_axis=0, concat_axis=0, tiled=True, a...  26.5 us
    ppermute x4, waiting for transfers between devices, hop(): return lax.ppermute(value, 'dp', [(i, (i + by) % ZN) for i in range(ZN)])  12.3 us
    ppermute x4, starting transfers between devices, on_device(): moved.append(lax.ppermute(rotated[j], DPX, perm))  11.4 us
    all_to_all x1, starting transfers between devices, on_device(): lax.all_to_all(tangent, 'dp', split_axis=0, concat_axis=0, tiled=True, ax...  7.82 us
    ppermute x3, waiting for transfers between devices, on_device(): ring.append(lax.ppermute(mine, 'expert', perm))  7.76 us
    unnamed x16, local copies, waits for them, and re-layouts  7.76 us
  transfers between devices with their start and end apart: 14, of which 7 were waited for; matrix products, arithmetic and copies ran while one was open for 0% of the time, Pallas kernels for 1%

profile of v1, /device:TPU:8, one launch (start us, length us, event | category | flops | bytes accessed | tf_op | source)
XLA Modules:
  0.0 160.7 jit_solution(9448162062134416568)
XLA Ops:
  0.0 0.0 copy-start
  0.0 0.0 copy-start.4
  0.0 1.1 copy-done.4
  1.1 0.0 copy-start.5
  1.1 0.9 copy-done.5
  2.0 0.0 copy-start.6
  2.0 0.8 copy-done.6
  2.8 0.0 copy-start.7
  2.8 0.8 copy-done.7
  3.5 0.9 shard_map.82
  4.5 26.5 %all_to_all.10.own_ref = bf16[16,256,128]{2,1,0:T(8,128)(2,1)S(1)} all-to-all(bf16[16,256,128]{2,1,0:T(8,128)(2,1)S(1)} %get-tuple-element.13), channel_id=1, replica_groups={{0,2,4,6,8,10,12,14,16,18,20,22,24,26,28,30},{1,3,5,7,9,11,13,15,17,19,..., dimensions={0} | all-to-all | bytes 2097152 | tf_op jit(solution)/shard_map/all_to_all | solution.py:134
  30.9 1.9 %collective-permute-start = (bf16[16,256,128]{2,1,0:T(8,128)(2,1)S(1)}, bf16[16,256,128]{2,1,0:T(8,128)(2,1)}, u32[]{:S(2)}, u32[]{:S(2)}) collective-permute-start(bf16[16,256,128]{2,1,0:T(8,128)(2,1)S(1)} %all_to_all.10.own_ref), channel_id=1, source_target_pairs={{0,1},{1,0},{2,3},{3,2},{4,5},{5,4},{6,7},{7,6},{8,9},{9,8},{10,11... | collective-permute-start | bytes 3145736 | tf_op jit(solution)/shard_map/ppermute | solution.py:138
  32.9 2.7 %collective-permute-done.oth_ref = bf16[16,256,128]{2,1,0:T(8,128)(2,1)} collective-permute-done((bf16[16,256,128]{2,1,0:T(8,128)(2,1)S(1)}, bf16[16,256,128]{2,1,0:T(8,128)(2,1)}, u32[]{:S(2)}, u32[]{:S(2)}) %collective-permute-start) | collective-permute-done | bytes 1048608 | tf_op jit(solution)/shard_map/ppermute | solution.py:138
  35.6 0.0 copy-done
  35.6 0.0 copy-start.1
  35.6 1.4 copy-done.1
  37.0 0.0 copy-start.2
  37.0 1.4 copy-done.2
  38.4 0.0 copy-start.3
  38.4 1.4 copy-done.3
  39.8 4.1 %shard_map.83 = bf16[8,192,128]{2,1,0:T(8,128)(2,1)} custom-call(s32[1]{0:T(128)} %bitcast.3.c_ref, bf16[16,256,128]{2,1,0:T(8,128)(2,1)S(1)} %all_to_all.10.own_ref, bf16[16,256,128]{2,1,0:T(8,128)(2,1)} %collective-permute-done.oth_ref, bf16[192,4096]{1,0:T(8,128)(2,1)S(1)} %copy-done, bf16[192,4096]{1,0:T(8,128)(2,1)S(1)} %copy-done.1, ...), custom_call_target="tpu_custom_call" | custom-call | flops 805306368 | bytes 9437184 | tf_op jit(solution)/shard_map/pallas_call | solution.py:156
  43.9 7.8 %all-to-all-start.1 = ((bf16[8,192,128]{2,1,0:T(8,128)(2,1)}), bf16[8,192,128]{2,1,0:T(8,128)(2,1)S(1)}, u32[]{:S(2)}, u32[]{:S(2)}) async-start(bf16[8,192,128]{2,1,0:T(8,128)(2,1)} %shard_map.83), calls=%async_computation.1 | async-start | bytes 786432 | tf_op jit(solution)/shard_map/all_to_all | solution.py:164
  51.7 4.6 %collective-permute-start.4 = (bf16[128,128]{1,0:T(8,128)(2,1)S(1)}, bf16[128,128]{1,0:T(8,128)(2,1)S(1)}, u32[]{:S(2)}, u32[]{:S(2)}) collective-permute-start(bf16[128,128]{1,0:T(8,128)(2,1)S(1)} %get-tuple-element.17), channel_id=1, source_target_pairs={{0,24},{1,56},{2,88},{3,120},{4,152},{5,184},{6,216},{7,248},{8,0}... | collective-permute-start | bytes 98312 | tf_op jit(solution)/shard_map/ppermute | solution.py:147
  56.3 2.2 %collective-permute-start.3 = (bf16[128,128]{1,0:T(8,128)(2,1)S(1)}, bf16[128,128]{1,0:T(8,128)(2,1)S(1)}, u32[]{:S(2)}, u32[]{:S(2)}) collective-permute-start(bf16[128,128]{1,0:T(8,128)(2,1)S(1)} %get-tuple-element.16), channel_id=1, source_target_pairs={{0,16},{1,48},{2,80},{3,112},{4,144},{5,176},{6,208},{7,240},{8,24... | collective-permute-start | bytes 98312 | tf_op jit(solution)/shard_map/ppermute | solution.py:147
  58.5 4.0 %collective-permute-start.2 = (bf16[128,128]{1,0:T(8,128)(2,1)S(1)}, bf16[128,128]{1,0:T(8,128)(2,1)S(1)}, u32[]{:S(2)}, u32[]{:S(2)}) collective-permute-start(bf16[128,128]{1,0:T(8,128)(2,1)S(1)} %get-tuple-element.15), channel_id=1, source_target_pairs={{0,8},{1,40},{2,72},{3,104},{4,136},{5,168},{6,200},{7,232},{8,16}... | collective-permute-start | bytes 98312 | tf_op jit(solution)/shard_map/ppermute | solution.py:147
  62.5 0.7 collective-permute-start.1
  63.1 0.0 collective-permute-done.4
  63.1 0.5 collective-permute-done.3
  63.6 0.7 collective-permute-done.2
  64.3 0.0 collective-permute-done.1
  64.3 32.3 %collective-permute-start.7 = (bf16[4,128,128]{2,1,0:T(8,128)(2,1)S(1)}, bf16[4,128,128]{2,1,0:T(8,128)(2,1)S(1)}, u32[]{:S(2)}, u32[]{:S(2)}) collective-permute-start(bf16[4,128,128]{2,1,0:T(8,128)(2,1)S(1)} %get-tuple-element.22), channel_id=1, source_target_pairs={{0,6},{1,7},{2,0},{3,1},{4,2},{5,3},{6,4},{7,5},{8,14},{9,15},{10,... | collective-permute-start | bytes 393224 | tf_op jit(solution)/shard_map/ppermute | solution.py:152
  96.6 1.9 %collective-permute-start.6 = (bf16[4,128,128]{2,1,0:T(8,128)(2,1)S(1)}, bf16[4,128,128]{2,1,0:T(8,128)(2,1)S(1)}, u32[]{:S(2)}, u32[]{:S(2)}) collective-permute-start(bf16[4,128,128]{2,1,0:T(8,128)(2,1)S(1)} %get-tuple-element.22), channel_id=1, source_target_pairs={{0,4},{1,5},{2,6},{3,7},{4,0},{5,1},{6,2},{7,3},{8,12},{9,13},{10,... | collective-permute-start | bytes 393224 | tf_op jit(solution)/shard_map/ppermute | solution.py:152
  98.5 2.8 %collective-permute-start.5 = (bf16[4,128,128]{2,1,0:T(8,128)(2,1)S(1)}, bf16[4,128,128]{2,1,0:T(8,128)(2,1)S(1)}, u32[]{:S(2)}, u32[]{:S(2)}) collective-permute-start(bf16[4,128,128]{2,1,0:T(8,128)(2,1)S(1)} %get-tuple-element.22), channel_id=1, source_target_pairs={{0,2},{1,3},{2,4},{3,5},{4,6},{5,7},{6,0},{7,1},{8,10},{9,11},{10,... | collective-permute-start | bytes 393224 | tf_op jit(solution)/shard_map/ppermute | solution.py:152
  101.3 0.0 collective-permute-done.7
  101.3 4.4 %collective-permute-done.6 = bf16[4,128,128]{2,1,0:T(8,128)(2,1)S(1)} collective-permute-done((bf16[4,128,128]{2,1,0:T(8,128)(2,1)S(1)}, bf16[4,128,128]{2,1,0:T(8,128)(2,1)S(1)}, u32[]{:S(2)}, u32[]{:S(2)}) %collective-permute-start.6) | collective-permute-done | bytes 131104 | tf_op jit(solution)/shard_map/ppermute | solution.py:152
  105.7 3.3 %collective-permute-done.5 = bf16[4,128,128]{2,1,0:T(8,128)(2,1)S(1)} collective-permute-done((bf16[4,128,128]{2,1,0:T(8,128)(2,1)S(1)}, bf16[4,128,128]{2,1,0:T(8,128)(2,1)S(1)}, u32[]{:S(2)}, u32[]{:S(2)}) %collective-permute-start.5) | collective-permute-done | bytes 131104 | tf_op jit(solution)/shard_map/ppermute | solution.py:152
  109.1 0.1 pad_maximum_fusion.own_ref
  109.1 2.0 %collective-permute-start.8 = (bf16[4,4,128,128]{3,2,1,0:T(8,128)(2,1)S(1)}, bf16[4,4,128,128]{3,2,1,0:T(8,128)(2,1)S(1)}, u32[]{:S(2)}, u32[]{:S(2)}) collective-permute-start(bf16[4,4,128,128]{3,2,1,0:T(8,128)(2,1)S(1)} %pad_maximum_fusion.own_ref), channel_id=1, source_target_pairs={{0,1},{1,0},{2,3},{3,2},{4,5},{5,4},{6,7},{7,6},{8,9},{9,8},{10,11... | collective-permute-start | bytes 1572872 | tf_op jit(solution)/shard_map/ppermute | solution.py:154
  111.2 0.1 pad_add_fusion.at_ref
  111.3 1.7 %collective-permute-done.8.oth_ref = bf16[4,4,128,128]{3,2,1,0:T(8,128)(2,1)S(1)} collective-permute-done((bf16[4,4,128,128]{3,2,1,0:T(8,128)(2,1)S(1)}, bf16[4,4,128,128]{3,2,1,0:T(8,128)(2,1)S(1)}, u32[]{:S(2)}, u32[]{:S(2)}) %collective-permute-start.8) | collective-permute-done | bytes 524320 | tf_op jit(solution)/shard_map/ppermute | solution.py:154
  112.9 0.0 all-to-all-done.1.tan_ref
  112.9 0.8 shard_map.85
  113.8 15.5 %collective-permute-start.11 = (bf16[96,128]{1,0:T(8,128)(2,1)S(1)}, bf16[96,128]{1,0:T(8,128)(2,1)S(1)}, u32[]{:S(2)}, u32[]{:S(2)}) collective-permute-start(bf16[96,128]{1,0:T(8,128)(2,1)S(1)} %get-tuple-element.24), channel_id=1, source_target_pairs={{0,768},{32,800},{64,832},{96,864},{128,896},{160,928},{192,960},{... | collective-permute-start | bytes 73736 | tf_op jit(solution)/shard_map/ppermute | solution.py:178
  129.3 1.0 shard_map.84
  130.3 2.1 %collective-permute-start.9 = (bf16[96,128]{1,0:T(8,128)(2,1)S(1)}, bf16[96,128]{1,0:T(8,128)(2,1)S(1)}, u32[]{:S(2)}, u32[]{:S(2)}) collective-permute-start(bf16[96,128]{1,0:T(8,128)(2,1)S(1)} %get-tuple-element.23), channel_id=1, source_target_pairs={{0,256},{32,288},{64,320},{96,352},{128,384},{160,416},{192,448},{... | collective-permute-start | bytes 73736 | tf_op jit(solution)/shard_map/ppermute | solution.py:178
  132.5 0.0 collective-permute-done.11
  132.5 12.4 %collective-permute-start.12 = (bf16[192,128]{1,0:T(8,128)(2,1)S(1)}, bf16[192,128]{1,0:T(8,128)(2,1)S(1)}, u32[]{:S(2)}, u32[]{:S(2)}) collective-permute-start(bf16[192,128]{1,0:T(8,128)(2,1)S(1)} %pad_maximum_fusion.3), channel_id=1, source_target_pairs={{0,768},{32,800},{64,832},{96,864},{128,896},{160,928},{192,960},{... | collective-permute-start | bytes 147464 | tf_op jit(solution)/shard_map/ppermute | solution.py:178
  144.9 0.0 collective-permute-done.9
  145.0 2.8 %collective-permute-start.10 = (bf16[192,128]{1,0:T(8,128)(2,1)S(1)}, bf16[192,128]{1,0:T(8,128)(2,1)S(1)}, u32[]{:S(2)}, u32[]{:S(2)}) collective-permute-start(bf16[192,128]{1,0:T(8,128)(2,1)S(1)} %pad_maximum_fusion.2), channel_id=1, source_target_pairs={{0,256},{32,288},{64,320},{96,352},{128,384},{160,416},{192,448},{... | collective-permute-start | bytes 147464 | tf_op jit(solution)/shard_map/ppermute | solution.py:178
  147.8 0.0 collective-permute-done.12
  147.8 12.3 %collective-permute-done.10 = bf16[192,128]{1,0:T(8,128)(2,1)S(1)} collective-permute-done((bf16[192,128]{1,0:T(8,128)(2,1)S(1)}, bf16[192,128]{1,0:T(8,128)(2,1)S(1)}, u32[]{:S(2)}, u32[]{:S(2)}) %collective-permute-start.10) | collective-permute-done | bytes 49184 | tf_op jit(solution)/shard_map/ppermute | solution.py:178
  160.1 0.6 add_convert_fusion
  (8 shorter events, 0.1 us)
Async XLA Ops:
  0.0 35.6 %copy-start = (bf16[192,4096]{1,0:T(8,128)(2,1)S(1)}, bf16[192,4096]{1,0:T(8,128)(2,1)}, u32[]{:S(2)}) copy-start(bf16[192,4096]{1,0:T(8,128)(2,1)} %g_ref.1) | copy-start | bytes 4718596
  0.0 1.1 copy-start.4
  1.1 0.9 copy-start.5
  2.0 0.8 copy-start.6
  2.8 0.8 copy-start.7
  30.9 4.7 %collective-permute-start = (bf16[16,256,128]{2,1,0:T(8,128)(2,1)S(1)}, bf16[16,256,128]{2,1,0:T(8,128)(2,1)}, u32[]{:S(2)}, u32[]{:S(2)}) collective-permute-start(bf16[16,256,128]{2,1,0:T(8,128)(2,1)S(1)} %all_to_all.10.own_ref), channel_id=1, source_target_pairs={{0,1},{1,0},{2,3},{3,2},{4,5},{5,4},{6,7},{7,6},{8,9},{9,8},{10,11... | collective-permute-start | bytes 3145736 | tf_op jit(solution)/shard_map/ppermute | solution.py:138
  35.6 1.4 copy-start.1
  37.0 1.4 copy-start.2
  38.4 1.4 copy-start.3
  43.9 69.0 %all-to-all-start.1 = ((bf16[8,192,128]{2,1,0:T(8,128)(2,1)}), bf16[8,192,128]{2,1,0:T(8,128)(2,1)S(1)}, u32[]{:S(2)}, u32[]{:S(2)}) async-start(bf16[8,192,128]{2,1,0:T(8,128)(2,1)} %shard_map.83), calls=%async_computation.1 | async-start | bytes 786432 | tf_op jit(solution)/shard_map/all_to_all | solution.py:164
  51.7 11.4 %collective-permute-start.4 = (bf16[128,128]{1,0:T(8,128)(2,1)S(1)}, bf16[128,128]{1,0:T(8,128)(2,1)S(1)}, u32[]{:S(2)}, u32[]{:S(2)}) collective-permute-start(bf16[128,128]{1,0:T(8,128)(2,1)S(1)} %get-tuple-element.17), channel_id=1, source_target_pairs={{0,24},{1,56},{2,88},{3,120},{4,152},{5,184},{6,216},{7,248},{8,0}... | collective-permute-start | bytes 98312 | tf_op jit(solution)/shard_map/ppermute | solution.py:147
  56.3 7.3 %collective-permute-start.3 = (bf16[128,128]{1,0:T(8,128)(2,1)S(1)}, bf16[128,128]{1,0:T(8,128)(2,1)S(1)}, u32[]{:S(2)}, u32[]{:S(2)}) collective-permute-start(bf16[128,128]{1,0:T(8,128)(2,1)S(1)} %get-tuple-element.16), channel_id=1, source_target_pairs={{0,16},{1,48},{2,80},{3,112},{4,144},{5,176},{6,208},{7,240},{8,24... | collective-permute-start | bytes 98312 | tf_op jit(solution)/shard_map/ppermute | solution.py:147
  58.5 5.8 %collective-permute-start.2 = (bf16[128,128]{1,0:T(8,128)(2,1)S(1)}, bf16[128,128]{1,0:T(8,128)(2,1)S(1)}, u32[]{:S(2)}, u32[]{:S(2)}) collective-permute-start(bf16[128,128]{1,0:T(8,128)(2,1)S(1)} %get-tuple-element.15), channel_id=1, source_target_pairs={{0,8},{1,40},{2,72},{3,104},{4,136},{5,168},{6,200},{7,232},{8,16}... | collective-permute-start | bytes 98312 | tf_op jit(solution)/shard_map/ppermute | solution.py:147
  62.5 1.8 %collective-permute-start.1 = (bf16[128,128]{1,0:T(8,128)(2,1)S(1)}, bf16[128,128]{1,0:T(8,128)(2,1)S(1)}, u32[]{:S(2)}, u32[]{:S(2)}) collective-permute-start(bf16[128,128]{1,0:T(8,128)(2,1)S(1)} %get-tuple-element.14), channel_id=1, source_target_pairs={{0,0},{1,32},{2,64},{3,96},{4,128},{5,160},{6,192},{7,224},{8,8},{... | collective-permute-start | bytes 98312 | tf_op jit(solution)/shard_map/ppermute | solution.py:147
  64.3 37.0 %collective-permute-start.7 = (bf16[4,128,128]{2,1,0:T(8,128)(2,1)S(1)}, bf16[4,128,128]{2,1,0:T(8,128)(2,1)S(1)}, u32[]{:S(2)}, u32[]{:S(2)}) collective-permute-start(bf16[4,128,128]{2,1,0:T(8,128)(2,1)S(1)} %get-tuple-element.22), channel_id=1, source_target_pairs={{0,6},{1,7},{2,0},{3,1},{4,2},{5,3},{6,4},{7,5},{8,14},{9,15},{10,... | collective-permute-start | bytes 393224 | tf_op jit(solution)/shard_map/ppermute | solution.py:152
  96.6 9.2 %collective-permute-start.6 = (bf16[4,128,128]{2,1,0:T(8,128)(2,1)S(1)}, bf16[4,128,128]{2,1,0:T(8,128)(2,1)S(1)}, u32[]{:S(2)}, u32[]{:S(2)}) collective-permute-start(bf16[4,128,128]{2,1,0:T(8,128)(2,1)S(1)} %get-tuple-element.22), channel_id=1, source_target_pairs={{0,4},{1,5},{2,6},{3,7},{4,0},{5,1},{6,2},{7,3},{8,12},{9,13},{10,... | collective-permute-start | bytes 393224 | tf_op jit(solution)/shard_map/ppermute | solution.py:152
  98.5 10.5 %collective-permute-start.5 = (bf16[4,128,128]{2,1,0:T(8,128)(2,1)S(1)}, bf16[4,128,128]{2,1,0:T(8,128)(2,1)S(1)}, u32[]{:S(2)}, u32[]{:S(2)}) collective-permute-start(bf16[4,128,128]{2,1,0:T(8,128)(2,1)S(1)} %get-tuple-element.22), channel_id=1, source_target_pairs={{0,2},{1,3},{2,4},{3,5},{4,6},{5,7},{6,0},{7,1},{8,10},{9,11},{10,... | collective-permute-start | bytes 393224 | tf_op jit(solution)/shard_map/ppermute | solution.py:152
  109.1 3.8 %collective-permute-start.8 = (bf16[4,4,128,128]{3,2,1,0:T(8,128)(2,1)S(1)}, bf16[4,4,128,128]{3,2,1,0:T(8,128)(2,1)S(1)}, u32[]{:S(2)}, u32[]{:S(2)}) collective-permute-start(bf16[4,4,128,128]{3,2,1,0:T(8,128)(2,1)S(1)} %pad_maximum_fusion.own_ref), channel_id=1, source_target_pairs={{0,1},{1,0},{2,3},{3,2},{4,5},{5,4},{6,7},{7,6},{8,9},{9,8},{10,11... | collective-permute-start | bytes 1572872 | tf_op jit(solution)/shard_map/ppermute | solution.py:154
  113.8 18.7 %collective-permute-start.11 = (bf16[96,128]{1,0:T(8,128)(2,1)S(1)}, bf16[96,128]{1,0:T(8,128)(2,1)S(1)}, u32[]{:S(2)}, u32[]{:S(2)}) collective-permute-start(bf16[96,128]{1,0:T(8,128)(2,1)S(1)} %get-tuple-element.24), channel_id=1, source_target_pairs={{0,768},{32,800},{64,832},{96,864},{128,896},{160,928},{192,960},{... | collective-permute-start | bytes 73736 | tf_op jit(solution)/shard_map/ppermute | solution.py:178
  130.3 14.6 %collective-permute-start.9 = (bf16[96,128]{1,0:T(8,128)(2,1)S(1)}, bf16[96,128]{1,0:T(8,128)(2,1)S(1)}, u32[]{:S(2)}, u32[]{:S(2)}) collective-permute-start(bf16[96,128]{1,0:T(8,128)(2,1)S(1)} %get-tuple-element.23), channel_id=1, source_target_pairs={{0,256},{32,288},{64,320},{96,352},{128,384},{160,416},{192,448},{... | collective-permute-start | bytes 73736 | tf_op jit(solution)/shard_map/ppermute | solution.py:178
  132.5 15.3 %collective-permute-start.12 = (bf16[192,128]{1,0:T(8,128)(2,1)S(1)}, bf16[192,128]{1,0:T(8,128)(2,1)S(1)}, u32[]{:S(2)}, u32[]{:S(2)}) collective-permute-start(bf16[192,128]{1,0:T(8,128)(2,1)S(1)} %pad_maximum_fusion.3), channel_id=1, source_target_pairs={{0,768},{32,800},{64,832},{96,864},{128,896},{160,928},{192,960},{... | collective-permute-start | bytes 147464 | tf_op jit(solution)/shard_map/ppermute | solution.py:178
  145.0 15.1 %collective-permute-start.10 = (bf16[192,128]{1,0:T(8,128)(2,1)S(1)}, bf16[192,128]{1,0:T(8,128)(2,1)S(1)}, u32[]{:S(2)}, u32[]{:S(2)}) collective-permute-start(bf16[192,128]{1,0:T(8,128)(2,1)S(1)} %pad_maximum_fusion.2), channel_id=1, source_target_pairs={{0,256},{32,288},{64,320},{96,352},{128,384},{160,416},{192,448},{... | collective-permute-start | bytes 147464 | tf_op jit(solution)/shard_map/ppermute | solution.py:178

commit v2 on v1

--- a/solution.py
+++ b/solution.py
@@ -14,15 +14,34 @@
 DPX = ("dp", "expert")
 SMEM = pl.BlockSpec(memory_space=pltpu.SMEM)
 VMEM = pl.BlockSpec(memory_space=pltpu.VMEM)
+ANY = pl.BlockSpec(memory_space=pl.ANY)
+HBM = pl.BlockSpec(memory_space=pltpu.HBM)
+DMA = pltpu.SemaphoreType.DMA
 
 
 def dot(a, b):
     return jnp.dot(a, b, preferred_element_type=F32)
 
 
-def prep_kernel(y_ref, ids_ref, gates_ref, tok_ref, cot_ref, send_ref, *rot_refs):
+def prep_kernel(y_ref, ids_hbm, gates_hbm, tok_hbm, cot_hbm, send_ref, *refs):
+    rot_refs, (ids_ref, gates_ref, both_ref, sems) = refs[:WIN], refs[WIN:]
+    feats = tok_hbm.shape[1]
+    copies = [
+        pltpu.make_async_copy(ids_hbm, ids_ref, sems.at[0]),
+        pltpu.make_async_copy(gates_hbm, gates_ref, sems.at[1]),
+        pltpu.make_async_copy(tok_hbm, both_ref.at[:, pl.ds(0, feats)], sems.at[2]),
+        pltpu.make_async_copy(cot_hbm, both_ref.at[:, pl.ds(feats, feats)], sems.at[3]),
+    ]
+    for copy in copies:
+        copy.start()
     y = y_ref[0]
-    rows = tok_ref.shape[0]
+    rows = tok_hbm.shape[0]
+    upper = (
+        lax.broadcasted_iota(jnp.int32, (CAP, CAP), 0)
+        <= lax.broadcasted_iota(jnp.int32, (CAP, CAP), 1)
+    ).astype(BF16)
+    copies[0].wait()
+    copies[1].wait()
     ids = ids_ref[...]
     gates = gates_ref[...]
     present, gate = [], []
@@ -31,10 +50,6 @@
         present.append(jnp.max(jnp.where(named, 1.0, 0.0), axis=0, keepdims=True))
         gate.append(jnp.sum(jnp.where(named, gates, 0.0), axis=0, keepdims=True))
     marks = jnp.concatenate(present + present, axis=0)
-    upper = (
-        lax.broadcasted_iota(jnp.int32, (CAP, CAP), 0)
-        <= lax.broadcasted_iota(jnp.int32, (CAP, CAP), 1)
-    ).astype(BF16)
     base = jnp.full((2 * WIN, 1), -1.0, F32)
     slots = []
     for b in range(rows // CAP):
@@ -43,38 +58,59 @@
         base = base + part[:, CAP - 1 :]
     slot = jnp.concatenate(slots, axis=1)
     slot = jnp.where(marks > 0.0, slot, -1.0).astype(jnp.int32)
-    both = jnp.concatenate([tok_ref[...], cot_ref[...]], axis=1)
     index = lax.broadcasted_iota(jnp.int32, (CAP, rows), 0)
+    copies[2].wait()
+    copies[3].wait()
+    both = both_ref[...]
     for j in range(WIN):
         placer = slot[j : j + 1, :] == index
         got = dot(jnp.where(placer, 1.0, 0.0).astype(BF16), both)
         factor = jnp.sum(jnp.where(placer, gate[j], 0.0), axis=1, keepdims=True)
-        xs = got[:, :CAP]
-        cs = got[:, CAP:] * factor
+        xs = got[:, :feats]
+        cs = got[:, feats:] * factor
         rot_refs[j][...] = xs.astype(BF16)
         chunk = jnp.concatenate([xs.T, cs.T], axis=0).astype(BF16)
         for x in range(WIN):
             send_ref[((y + j) % WIN) * WIN + x] = chunk
 
 
-def tangent_kernel(c_ref, own_ref, oth_ref, g_ref, u_ref, d_ref, p_ref, out_ref):
-    c = c_ref[0]
-    hid = g_ref.shape[0]
-    accs = [jnp.zeros((hid, CAP), F32) for _ in range(4)]
-    for s in range(0, 16, 2):
-        for ref, side in ((own_ref, c), (oth_ref, 1 - c)):
-            cols = [
-                pl.ds(pl.multiple_of((2 * (s + t) + side) * CAP, CAP), CAP)
-                for t in range(2)
-            ]
-            xs = jnp.concatenate([ref[s, :CAP], ref[s + 1, :CAP]], axis=0)
-            cs = jnp.concatenate([ref[s, CAP:], ref[s + 1, CAP:]], axis=0)
-            for n, (w_ref, rhs) in enumerate(
-                ((g_ref, xs), (u_ref, xs), (p_ref, xs), (d_ref, cs))
-            ):
-                lhs = jnp.concatenate([w_ref[:, cols[0]], w_ref[:, cols[1]]], axis=1)
-                accs[n] = accs[n] + dot(lhs, rhs)
-    preact, linear, probe_pre, backward = accs
+def gate_kernel(rows_in, *refs):
+    del rows_in
+    moved_refs, mine_ref = refs[:WIN], refs[WIN + 1]
+    for j in range(WIN):
+        mine_ref[j] = moved_refs[j][...]
+
+
+def load(side, w_hbms, w_ref, sem):
+    for n, w_hbm in enumerate(w_hbms):
+        for s in range(w_hbm.shape[1] // (2 * CAP)):
+            cols = pl.ds(pl.multiple_of((2 * s + side) * CAP, CAP), CAP)
+            dst = w_ref.at[n, :, pl.ds(s * CAP, CAP)]
+            pltpu.make_async_copy(w_hbm.at[:, cols], dst, sem.at[n]).start()
+
+
+def half(rows_ref, w_ref, sem):
+    chips, both, slots = rows_ref.shape
+    xs = rows_ref[:, : both // 2].reshape(chips * both // 2, slots)
+    cs = rows_ref[:, both // 2 :].reshape(chips * both // 2, slots)
+    parts = []
+    for n, rows in enumerate((xs, xs, xs, cs)):
+        pltpu.make_async_copy(w_ref.at[n], w_ref.at[n], sem.at[n]).wait()
+        parts.append(dot(w_ref[n], rows))
+    return parts
+
+
+def own_kernel(c_ref, rows_ref, g_hbm, u_hbm, p_hbm, d_hbm, acc_ref, w_ref, sem):
+    load(c_ref[0], (g_hbm, u_hbm, p_hbm, d_hbm), w_ref, sem)
+    for n, part in enumerate(half(rows_ref, w_ref, sem)):
+        acc_ref[n] = part
+
+
+def tangent_kernel(c_ref, rows_ref, g_hbm, u_hbm, p_hbm, d_hbm, acc_ref, out_ref, w_ref, sem):
+    load(1 - c_ref[0], (g_hbm, u_hbm, p_hbm, d_hbm), w_ref, sem)
+    preact, linear, probe_pre, backward = [
+        acc_ref[n] + part for n, part in enumerate(half(rows_ref, w_ref, sem))
+    ]
     sig = 1.0 / (1.0 + jnp.exp(-preact))
     curvature = sig * (1.0 - sig) * (2.0 + preact * (1.0 - 2.0 * sig))
     tangent = (backward * linear * curvature * probe_pre).astype(BF16)
@@ -98,17 +134,22 @@
         out_ref[...] = acc.astype(out_ref.dtype)
 
 
-def call(kernel, out_shape, specs, flops, nbytes):
+def call(kernel, out_shape, specs, flops, nbytes, scratch=(), **more):
     return pl.pallas_call(
         kernel,
         out_shape=out_shape,
         in_specs=specs,
-        out_specs=jax.tree.map(lambda _: VMEM, out_shape),
-        compiler_params=pltpu.CompilerParams(vmem_limit_bytes=40 * 1024 * 1024),
+        scratch_shapes=scratch,
+        compiler_params=pltpu.CompilerParams(vmem_limit_bytes=16 << 20),
         cost_estimate=pl.CostEstimate(
             flops=flops, bytes_accessed=nbytes, transcendentals=0
         ),
-    )
+        **({"out_specs": jax.tree.map(lambda _: VMEM, out_shape)} | more),
+    )
+
+
+def in_hbm(value):
+    return pltpu.with_memory_space_constraint(value, pltpu.HBM)
 
 
 def sds(shape, dtype):
@@ -121,22 +162,24 @@
     hid, feats = gate_proj.shape[0], tokens.shape[1]
     at = jnp.stack([zhi, e, x, c]).astype(jnp.int32)
 
-    prepared = call(
+    rows, cols = tokens.shape[0], gate_proj.shape[1]
+    send, *rotated = call(
         prep_kernel,
         [sds((16, 2 * feats, CAP), BF16)] + [sds((CAP, feats), BF16)] * WIN,
-        [SMEM] + [VMEM] * 4,
+        [SMEM] + [HBM] * 4,
         2 * 512 * 1024 * 256,
         2 << 20,
-    )(at[1:2], expert_ids.T, gate_values.T, tokens, cotangent)
-    send, rotated = prepared[0], prepared[1:]
-
+        [
+            pltpu.VMEM((8, rows), jnp.int32),
+            pltpu.VMEM((8, rows), F32),
+            pltpu.VMEM((rows, 2 * feats), BF16),
+            DMA((4,)),
+        ],
+    )(at[1:2], *map(in_hbm, (expert_ids.T, gate_values.T, tokens, cotangent)))
     same_core = [[c0 + 2 * i for i in range(16)] for c0 in range(2)]
     own = lax.all_to_all(
         send, "expert", split_axis=0, concat_axis=0, tiled=True, axis_index_groups=same_core
     )
-    swap = [(i, i ^ 1) for i in range(32)]
-    oth = lax.ppermute(own, "expert", swap)
-
     moved = []
     for j in range(WIN):
         perm = [
@@ -145,7 +188,37 @@
             for k in range(32)
         ]
         moved.append(lax.ppermute(rotated[j], DPX, perm))
-    mine = jnp.stack(moved)
+    own, mine = call(
+        gate_kernel,
+        [sds(own.shape, BF16), sds((WIN, CAP, feats), BF16)],
+        [ANY] + [VMEM] * WIN,
+        0,
+        1 << 18,
+        out_specs=[ANY, VMEM],
+        input_output_aliases={0: 0},
+    )(own, *moved)
+    swap = [(i, i ^ 1) for i in range(32)]
+    oth = lax.ppermute(own, "expert", swap)
+
+    weights = [in_hbm(w) for w in (gate_proj, up_proj, probe, down_proj)]
+    columns = [pltpu.VMEM((4, hid, cols // 2), BF16), DMA((4,))]
+    sums = call(
+        own_kernel,
+        sds((4, hid, CAP), F32),
+        [SMEM, VMEM] + [HBM] * 4,
+        4 * hid * cols * CAP,
+        4 << 20,
+        columns,
+    )(at[3:4], own, *weights)
+    tangent = call(
+        tangent_kernel,
+        sds((ZLO, hid, CAP), BF16),
+        [SMEM, VMEM] + [HBM] * 4 + [VMEM],
+        4 * hid * cols * CAP,
+        4 << 20,
+        columns,
+    )(at[3:4], oth, *weights, sums)
+
     ring = [mine]
     for dx in range(1, WIN):
         perm = [(k, k // 8 * 8 + (k // 2 % 4 + dx) % 4 * 2 + k % 2) for k in range(32)]
@@ -153,13 +226,6 @@
     own_t = jnp.stack(ring)
     oth_t = lax.ppermute(own_t, "expert", swap)
 
-    tangent = call(
-        tangent_kernel,
-        sds((ZLO, hid, CAP), BF16),
-        [SMEM] + [VMEM] * 6,
-        2 * 4 * hid * 4096 * CAP,
-        9 << 20,
-    )(at[3:4], own, oth, gate_proj, up_proj, down_proj, probe)
     near = [[8 * a + b for b in range(8)] for a in range(4)]
     tangents = lax.all_to_all(
         tangent, "dp", split_axis=0, concat_axis=0, tiled=True, axis_index_groups=near

time: 162 us -> 148 us (0.914)
  the two profiles are of different devices: /device:TPU:8 before, /device:TPU:32 now
where the time goes in v2:
time: 148 us; the launch traced here: 147 us
  starting transfers between devices  102 us (69%)
  waiting for transfers between devices  33.7 us (23%)
  Pallas kernels  10.7 us (7%)
    all_to_all x1, starting transfers between devices, on_device(): lax.all_to_all(tangent, 'dp', split_axis=0, concat_axis=0, tiled=True, ax...  36.4 us
    ppermute x4, starting transfers between devices, hop(): return lax.ppermute(value, 'dp', [(i, (i + by) % ZN) for i in range(ZN)])  31.1 us
    ppermute x4, waiting for transfers between devices, hop(): return lax.ppermute(value, 'dp', [(i, (i + by) % ZN) for i in range(ZN)])  19.3 us
    ppermute x4, starting transfers between devices, on_device(): moved.append(lax.ppermute(rotated[j], DPX, perm))  15.5 us
    ppermute x3, starting transfers between devices, on_device(): ring.append(lax.ppermute(mine, 'expert', perm))  7.75 us
    all_to_all x1, starting transfers between devices, on_device(): lax.all_to_all(send, 'expert', split_axis=0, concat_axis=0, tiled=True, a...  7.05 us
    ppermute x3, waiting for transfers between devices, on_device(): ring.append(lax.ppermute(mine, 'expert', perm))  5.7 us
    all_to_all x1, waiting for transfers between devices, on_device(): lax.all_to_all(tangent, 'dp', split_axis=0, concat_axis=0, tiled=True, ax...  4.82 us
  transfers between devices with their start and end apart: 15, of which 10 were waited for; matrix products, arithmetic and copies ran while one was open for 0% of the time, Pallas kernels for 2%

profile of v2, /device:TPU:32, one launch (start us, length us, event | category | flops | bytes accessed | tf_op | source)
XLA Modules:
  0.0 147.2 jit_solution(15486456403340347671)
XLA Ops:
  0.0 2.8 %shard_map.82 = (bf16[16,256,128]{2,1,0:T(8,128)(2,1)}, bf16[128,128]{1,0:T(8,128)(2,1)S(1)}, bf16[128,128]{1,0:T(8,128)(2,1)S(1)}, bf16[128,128]{1,0:T(8,128)(2,1)S(1)}, bf16[128,128]{1,0:T(8,128)(2,1)S(1)}) custom-call(s32[1]{0:T(128)} %bitcast.1.y_ref, s32[8,1024]{1,0:T(8,128)} %bitcast.14, f32[8,1024]{1,0:T(8,128)} %bitcast.15, ...), custom_call_target="tpu_custom_call" | custom-call | flops 268435456 | bytes 2097152 | tf_op jit(solution)/shard_map/pallas_call | solution.py:166
  2.8 7.0 %all-to-all-start = ((bf16[16,256,128]{2,1,0:T(8,128)(2,1)}), bf16[16,256,128]{2,1,0:T(8,128)(2,1)S(1)}, u32[]{:S(2)}, u32[]{:S(2)}) async-start(bf16[16,256,128]{2,1,0:T(8,128)(2,1)} %get-tuple-element.15), calls=%async_computation | async-start | bytes 2097152 | tf_op jit(solution)/shard_map/all_to_all | solution.py:180
  9.9 1.9 %collective-permute-start = (bf16[128,128]{1,0:T(8,128)(2,1)S(1)}, bf16[128,128]{1,0:T(8,128)(2,1)S(1)}, u32[]{:S(2)}, u32[]{:S(2)}) collective-permute-start(bf16[128,128]{1,0:T(8,128)(2,1)S(1)} %get-tuple-element.16), channel_id=1, source_target_pairs={{0,0},{1,32},{2,64},{3,96},{4,128},{5,160},{6,192},{7,224},{8,8},{... | collective-permute-start | bytes 98312 | tf_op jit(solution)/shard_map/ppermute | solution.py:190
  11.8 5.0 %collective-permute-start.1 = (bf16[128,128]{1,0:T(8,128)(2,1)S(1)}, bf16[128,128]{1,0:T(8,128)(2,1)S(1)}, u32[]{:S(2)}, u32[]{:S(2)}) collective-permute-start(bf16[128,128]{1,0:T(8,128)(2,1)S(1)} %get-tuple-element.17), channel_id=1, source_target_pairs={{0,8},{1,40},{2,72},{3,104},{4,136},{5,168},{6,200},{7,232},{8,16}... | collective-permute-start | bytes 98312 | tf_op jit(solution)/shard_map/ppermute | solution.py:190
  16.8 4.0 %collective-permute-start.2 = (bf16[128,128]{1,0:T(8,128)(2,1)S(1)}, bf16[128,128]{1,0:T(8,128)(2,1)S(1)}, u32[]{:S(2)}, u32[]{:S(2)}) collective-permute-start(bf16[128,128]{1,0:T(8,128)(2,1)S(1)} %get-tuple-element.18), channel_id=1, source_target_pairs={{0,16},{1,48},{2,80},{3,112},{4,144},{5,176},{6,208},{7,240},{8,24... | collective-permute-start | bytes 98312 | tf_op jit(solution)/shard_map/ppermute | solution.py:190
  20.9 4.5 %collective-permute-start.3 = (bf16[128,128]{1,0:T(8,128)(2,1)S(1)}, bf16[128,128]{1,0:T(8,128)(2,1)S(1)}, u32[]{:S(2)}, u32[]{:S(2)}) collective-permute-start(bf16[128,128]{1,0:T(8,128)(2,1)S(1)} %get-tuple-element.19), channel_id=1, source_target_pairs={{0,24},{1,56},{2,88},{3,120},{4,152},{5,184},{6,216},{7,248},{8,0}... | collective-permute-start | bytes 98312 | tf_op jit(solution)/shard_map/ppermute | solution.py:190
  25.4 0.0 collective-permute-done.refs_0_
  25.4 0.0 collective-permute-done.1.refs_1_
  25.4 0.0 collective-permute-done.2.refs_2_
  25.5 1.6 %collective-permute-done.3.refs_3_ = bf16[128,128]{1,0:T(8,128)(2,1)S(1)} collective-permute-done((bf16[128,128]{1,0:T(8,128)(2,1)S(1)}, bf16[128,128]{1,0:T(8,128)(2,1)S(1)}, u32[]{:S(2)}, u32[]{:S(2)}) %collective-permute-start.3) | collective-permute-done | bytes 32800 | tf_op jit(solution)/shard_map/ppermute | solution.py:190
  27.0 0.5 all-to-all-done.rows_in
  27.6 1.9 %collective-permute-start.4 = (bf16[16,256,128]{2,1,0:T(8,128)(2,1)S(1)}, bf16[16,256,128]{2,1,0:T(8,128)(2,1)S(1)}, u32[]{:S(2)}, u32[]{:S(2)}) collective-permute-start(bf16[16,256,128]{2,1,0:T(8,128)(2,1)S(1)} %get-tuple-element.20.rows_ref), channel_id=1, source_target_pairs={{0,1},{1,0},{2,3},{3,2},{4,5},{5,4},{6,7},{7,6},{8,9},{9,8},{10,11... | collective-permute-start | bytes 3145736 | tf_op jit(solution)/shard_map/ppermute | solution.py:201
  29.5 2.6 %shard_map.84.acc_ref = f32[4,192,128]{2,1,0:T(8,128)S(1)} custom-call(s32[1]{0:T(128)} %bitcast.3.c_ref, bf16[16,256,128]{2,1,0:T(8,128)(2,1)S(1)} %get-tuple-element.20.rows_ref, bf16[192,4096]{1,0:T(8,128)(2,1)} %g_hbm.3, bf16[192,4096]{1,0:T(8,128)(2,1)} %u_hbm.3, bf16[192,4096]{1,0:T(8,128)(2,1)} %p_hbm.3, bf16[192,4096]{1,0:T(8,128)(2,1)} %d_hbm.3), custom_call_target="tpu_custom_call" | custom-call | flops 402653184 | bytes 4194304 | tf_op jit(solution)/shard_map/pallas_call | solution.py:205
  32.1 0.0 collective-permute-done.4.rows_ref
  32.1 3.4 %shard_map.85 = bf16[8,192,128]{2,1,0:T(8,128)(2,1)} custom-call(s32[1]{0:T(128)} %bitcast.3.c_ref, bf16[16,256,128]{2,1,0:T(8,128)(2,1)S(1)} %collective-permute-done.4.rows_ref, bf16[192,4096]{1,0:T(8,128)(2,1)} %g_hbm.3, bf16[192,4096]{1,0:T(8,128)(2,1)} %u_hbm.3, bf16[192,4096]{1,0:T(8,128)(2,1)} %p_hbm.3, bf16[192,4096]{1,0:T(8,128)(2,1)} %d_hbm.3, ...), custom_call_target="tpu_custom_call" | custom-call | flops 402653184 | bytes 4194304 | tf_op jit(solution)/shard_map/pallas_call | solution.py:213
  35.5 36.4 %all-to-all-start.1 = ((bf16[8,192,128]{2,1,0:T(8,128)(2,1)}), bf16[8,192,128]{2,1,0:T(8,128)(2,1)S(1)}, u32[]{:S(2)}, u32[]{:S(2)}) async-start(bf16[8,192,128]{2,1,0:T(8,128)(2,1)} %shard_map.85), calls=%async_computation.1 | async-start | bytes 786432 | tf_op jit(solution)/shard_map/all_to_all | solution.py:230
  71.9 1.9 %collective-permute-start.7 = (bf16[4,128,128]{2,1,0:T(8,128)(2,1)S(1)}, bf16[4,128,128]{2,1,0:T(8,128)(2,1)S(1)}, u32[]{:S(2)}, u32[]{:S(2)}) collective-permute-start(bf16[4,128,128]{2,1,0:T(8,128)(2,1)S(1)} %get-tuple-element.21), channel_id=1, source_target_pairs={{0,6},{1,7},{2,0},{3,1},{4,2},{5,3},{6,4},{7,5},{8,14},{9,15},{10,... | collective-permute-start | bytes 393224 | tf_op jit(solution)/shard_map/ppermute | solution.py:225
  73.8 1.9 %collective-permute-start.6 = (bf16[4,128,128]{2,1,0:T(8,128)(2,1)S(1)}, bf16[4,128,128]{2,1,0:T(8,128)(2,1)S(1)}, u32[]{:S(2)}, u32[]{:S(2)}) collective-permute-start(bf16[4,128,128]{2,1,0:T(8,128)(2,1)S(1)} %get-tuple-element.21), channel_id=1, source_target_pairs={{0,4},{1,5},{2,6},{3,7},{4,0},{5,1},{6,2},{7,3},{8,12},{9,13},{10,... | collective-permute-start | bytes 393224 | tf_op jit(solution)/shard_map/ppermute | solution.py:225
  75.8 3.9 %collective-permute-start.5 = (bf16[4,128,128]{2,1,0:T(8,128)(2,1)S(1)}, bf16[4,128,128]{2,1,0:T(8,128)(2,1)S(1)}, u32[]{:S(2)}, u32[]{:S(2)}) collective-permute-start(bf16[4,128,128]{2,1,0:T(8,128)(2,1)S(1)} %get-tuple-element.21), channel_id=1, source_target_pairs={{0,2},{1,3},{2,4},{3,5},{4,6},{5,7},{6,0},{7,1},{8,10},{9,11},{10,... | collective-permute-start | bytes 393224 | tf_op jit(solution)/shard_map/ppermute | solution.py:225
  79.7 0.4 collective-permute-done.7
  80.1 2.5 %collective-permute-done.6 = bf16[4,128,128]{2,1,0:T(8,128)(2,1)S(1)} collective-permute-done((bf16[4,128,128]{2,1,0:T(8,128)(2,1)S(1)}, bf16[4,128,128]{2,1,0:T(8,128)(2,1)S(1)}, u32[]{:S(2)}, u32[]{:S(2)}) %collective-permute-start.6) | collective-permute-done | bytes 131104 | tf_op jit(solution)/shard_map/ppermute | solution.py:225
  82.6 2.8 %collective-permute-done.5 = bf16[4,128,128]{2,1,0:T(8,128)(2,1)S(1)} collective-permute-done((bf16[4,128,128]{2,1,0:T(8,128)(2,1)S(1)}, bf16[4,128,128]{2,1,0:T(8,128)(2,1)S(1)}, u32[]{:S(2)}, u32[]{:S(2)}) %collective-permute-start.5) | collective-permute-done | bytes 131104 | tf_op jit(solution)/shard_map/ppermute | solution.py:225
  85.4 0.1 pad_maximum_fusion.own_ref
  85.5 1.9 %collective-permute-start.8 = (bf16[4,4,128,128]{3,2,1,0:T(8,128)(2,1)S(1)}, bf16[4,4,128,128]{3,2,1,0:T(8,128)(2,1)S(1)}, u32[]{:S(2)}, u32[]{:S(2)}) collective-permute-start(bf16[4,4,128,128]{3,2,1,0:T(8,128)(2,1)S(1)} %pad_maximum_fusion.own_ref), channel_id=1, source_target_pairs={{0,1},{1,0},{2,3},{3,2},{4,5},{5,4},{6,7},{7,6},{8,9},{9,8},{10,11... | collective-permute-start | bytes 1572872 | tf_op jit(solution)/shard_map/ppermute | solution.py:227
  87.4 0.1 pad_add_fusion.at_ref
  87.5 1.8 %collective-permute-done.8.oth_ref = bf16[4,4,128,128]{3,2,1,0:T(8,128)(2,1)S(1)} collective-permute-done((bf16[4,4,128,128]{3,2,1,0:T(8,128)(2,1)S(1)}, bf16[4,4,128,128]{3,2,1,0:T(8,128)(2,1)S(1)}, u32[]{:S(2)}, u32[]{:S(2)}) %collective-permute-start.8) | collective-permute-done | bytes 524320 | tf_op jit(solution)/shard_map/ppermute | solution.py:227
  89.3 4.8 %all-to-all-done.1.tan_ref = bf16[8,192,128]{2,1,0:T(8,128)(2,1)S(1)} async-done(((bf16[8,192,128]{2,1,0:T(8,128)(2,1)}), bf16[8,192,128]{2,1,0:T(8,128)(2,1)S(1)}, u32[]{:S(2)}, u32[]{:S(2)}) %all-to-all-start.1) | async-done | bytes 393248 | tf_op jit(solution)/shard_map/all_to_all | solution.py:230
  94.1 0.8 shard_map.87
  94.9 14.6 %collective-permute-start.11 = (bf16[96,128]{1,0:T(8,128)(2,1)S(1)}, bf16[96,128]{1,0:T(8,128)(2,1)S(1)}, u32[]{:S(2)}, u32[]{:S(2)}) collective-permute-start(bf16[96,128]{1,0:T(8,128)(2,1)S(1)} %get-tuple-element.26), channel_id=1, source_target_pairs={{0,768},{32,800},{64,832},{96,864},{128,896},{160,928},{192,960},{... | collective-permute-start | bytes 73736 | tf_op jit(solution)/shard_map/ppermute | solution.py:244
  109.6 1.0 shard_map.86
  110.6 1.9 %collective-permute-start.9 = (bf16[96,128]{1,0:T(8,128)(2,1)S(1)}, bf16[96,128]{1,0:T(8,128)(2,1)S(1)}, u32[]{:S(2)}, u32[]{:S(2)}) collective-permute-start(bf16[96,128]{1,0:T(8,128)(2,1)S(1)} %get-tuple-element.25), channel_id=1, source_target_pairs={{0,256},{32,288},{64,320},{96,352},{128,384},{160,416},{192,448},{... | collective-permute-start | bytes 73736 | tf_op jit(solution)/shard_map/ppermute | solution.py:244
  112.5 0.0 collective-permute-done.11
  112.6 12.6 %collective-permute-start.12 = (bf16[192,128]{1,0:T(8,128)(2,1)S(1)}, bf16[192,128]{1,0:T(8,128)(2,1)S(1)}, u32[]{:S(2)}, u32[]{:S(2)}) collective-permute-start(bf16[192,128]{1,0:T(8,128)(2,1)S(1)} %pad_maximum_fusion.2), channel_id=1, source_target_pairs={{0,768},{32,800},{64,832},{96,864},{128,896},{160,928},{192,960},{... | collective-permute-start | bytes 147464 | tf_op jit(solution)/shard_map/ppermute | solution.py:244
  125.2 0.4 collective-permute-done.9
  125.6 1.9 %collective-permute-start.10 = (bf16[192,128]{1,0:T(8,128)(2,1)S(1)}, bf16[192,128]{1,0:T(8,128)(2,1)S(1)}, u32[]{:S(2)}, u32[]{:S(2)}) collective-permute-start(bf16[192,128]{1,0:T(8,128)(2,1)S(1)} %pad_maximum_fusion.1), channel_id=1, source_target_pairs={{0,256},{32,288},{64,320},{96,352},{128,384},{160,416},{192,448},{... | collective-permute-start | bytes 147464 | tf_op jit(solution)/shard_map/ppermute | solution.py:244
  127.6 4.0 %collective-permute-done.12 = bf16[192,128]{1,0:T(8,128)(2,1)S(1)} collective-permute-done((bf16[192,128]{1,0:T(8,128)(2,1)S(1)}, bf16[192,128]{1,0:T(8,128)(2,1)S(1)}, u32[]{:S(2)}, u32[]{:S(2)}) %collective-permute-start.12) | collective-permute-done | bytes 49184 | tf_op jit(solution)/shard_map/ppermute | solution.py:244
  131.6 14.9 %collective-permute-done.10 = bf16[192,128]{1,0:T(8,128)(2,1)S(1)} collective-permute-done((bf16[192,128]{1,0:T(8,128)(2,1)S(1)}, bf16[192,128]{1,0:T(8,128)(2,1)S(1)}, u32[]{:S(2)}, u32[]{:S(2)}) %collective-permute-start.10) | collective-permute-done | bytes 49184 | tf_op jit(solution)/shard_map/ppermute | solution.py:244
  146.5 0.6 add_convert_fusion
  (8 shorter events, 0.1 us)
Async XLA Ops:
  2.8 24.7 %all-to-all-start = ((bf16[16,256,128]{2,1,0:T(8,128)(2,1)}), bf16[16,256,128]{2,1,0:T(8,128)(2,1)S(1)}, u32[]{:S(2)}, u32[]{:S(2)}) async-start(bf16[16,256,128]{2,1,0:T(8,128)(2,1)} %get-tuple-element.15), calls=%async_computation | async-start | bytes 2097152 | tf_op jit(solution)/shard_map/all_to_all | solution.py:180
  9.9 15.5 %collective-permute-start = (bf16[128,128]{1,0:T(8,128)(2,1)S(1)}, bf16[128,128]{1,0:T(8,128)(2,1)S(1)}, u32[]{:S(2)}, u32[]{:S(2)}) collective-permute-start(bf16[128,128]{1,0:T(8,128)(2,1)S(1)} %get-tuple-element.16), channel_id=1, source_target_pairs={{0,0},{1,32},{2,64},{3,96},{4,128},{5,160},{6,192},{7,224},{8,8},{... | collective-permute-start | bytes 98312 | tf_op jit(solution)/shard_map/ppermute | solution.py:190
  11.8 13.6 %collective-permute-start.1 = (bf16[128,128]{1,0:T(8,128)(2,1)S(1)}, bf16[128,128]{1,0:T(8,128)(2,1)S(1)}, u32[]{:S(2)}, u32[]{:S(2)}) collective-permute-start(bf16[128,128]{1,0:T(8,128)(2,1)S(1)} %get-tuple-element.17), channel_id=1, source_target_pairs={{0,8},{1,40},{2,72},{3,104},{4,136},{5,168},{6,200},{7,232},{8,16}... | collective-permute-start | bytes 98312 | tf_op jit(solution)/shard_map/ppermute | solution.py:190
  16.8 8.6 %collective-permute-start.2 = (bf16[128,128]{1,0:T(8,128)(2,1)S(1)}, bf16[128,128]{1,0:T(8,128)(2,1)S(1)}, u32[]{:S(2)}, u32[]{:S(2)}) collective-permute-start(bf16[128,128]{1,0:T(8,128)(2,1)S(1)} %get-tuple-element.18), channel_id=1, source_target_pairs={{0,16},{1,48},{2,80},{3,112},{4,144},{5,176},{6,208},{7,240},{8,24... | collective-permute-start | bytes 98312 | tf_op jit(solution)/shard_map/ppermute | solution.py:190
  20.9 6.1 %collective-permute-start.3 = (bf16[128,128]{1,0:T(8,128)(2,1)S(1)}, bf16[128,128]{1,0:T(8,128)(2,1)S(1)}, u32[]{:S(2)}, u32[]{:S(2)}) collective-permute-start(bf16[128,128]{1,0:T(8,128)(2,1)S(1)} %get-tuple-element.19), channel_id=1, source_target_pairs={{0,24},{1,56},{2,88},{3,120},{4,152},{5,184},{6,216},{7,248},{8,0}... | collective-permute-start | bytes 98312 | tf_op jit(solution)/shard_map/ppermute | solution.py:190
  27.6 4.6 %collective-permute-start.4 = (bf16[16,256,128]{2,1,0:T(8,128)(2,1)S(1)}, bf16[16,256,128]{2,1,0:T(8,128)(2,1)S(1)}, u32[]{:S(2)}, u32[]{:S(2)}) collective-permute-start(bf16[16,256,128]{2,1,0:T(8,128)(2,1)S(1)} %get-tuple-element.20.rows_ref), channel_id=1, source_target_pairs={{0,1},{1,0},{2,3},{3,2},{4,5},{5,4},{6,7},{7,6},{8,9},{9,8},{10,11... | collective-permute-start | bytes 3145736 | tf_op jit(solution)/shard_map/ppermute | solution.py:201
  35.5 58.6 %all-to-all-start.1 = ((bf16[8,192,128]{2,1,0:T(8,128)(2,1)}), bf16[8,192,128]{2,1,0:T(8,128)(2,1)S(1)}, u32[]{:S(2)}, u32[]{:S(2)}) async-start(bf16[8,192,128]{2,1,0:T(8,128)(2,1)} %shard_map.85), calls=%async_computation.1 | async-start | bytes 786432 | tf_op jit(solution)/shard_map/all_to_all | solution.py:230
  71.9 8.1 %collective-permute-start.7 = (bf16[4,128,128]{2,1,0:T(8,128)(2,1)S(1)}, bf16[4,128,128]{2,1,0:T(8,128)(2,1)S(1)}, u32[]{:S(2)}, u32[]{:S(2)}) collective-permute-start(bf16[4,128,128]{2,1,0:T(8,128)(2,1)S(1)} %get-tuple-element.21), channel_id=1, source_target_pairs={{0,6},{1,7},{2,0},{3,1},{4,2},{5,3},{6,4},{7,5},{8,14},{9,15},{10,... | collective-permute-start | bytes 393224 | tf_op jit(solution)/shard_map/ppermute | solution.py:225
  73.8 8.7 %collective-permute-start.6 = (bf16[4,128,128]{2,1,0:T(8,128)(2,1)S(1)}, bf16[4,128,128]{2,1,0:T(8,128)(2,1)S(1)}, u32[]{:S(2)}, u32[]{:S(2)}) collective-permute-start(bf16[4,128,128]{2,1,0:T(8,128)(2,1)S(1)} %get-tuple-element.21), channel_id=1, source_target_pairs={{0,4},{1,5},{2,6},{3,7},{4,0},{5,1},{6,2},{7,3},{8,12},{9,13},{10,... | collective-permute-start | bytes 393224 | tf_op jit(solution)/shard_map/ppermute | solution.py:225
  75.8 9.6 %collective-permute-start.5 = (bf16[4,128,128]{2,1,0:T(8,128)(2,1)S(1)}, bf16[4,128,128]{2,1,0:T(8,128)(2,1)S(1)}, u32[]{:S(2)}, u32[]{:S(2)}) collective-permute-start(bf16[4,128,128]{2,1,0:T(8,128)(2,1)S(1)} %get-tuple-element.21), channel_id=1, source_target_pairs={{0,2},{1,3},{2,4},{3,5},{4,6},{5,7},{6,0},{7,1},{8,10},{9,11},{10,... | collective-permute-start | bytes 393224 | tf_op jit(solution)/shard_map/ppermute | solution.py:225
  85.5 3.8 %collective-permute-start.8 = (bf16[4,4,128,128]{3,2,1,0:T(8,128)(2,1)S(1)}, bf16[4,4,128,128]{3,2,1,0:T(8,128)(2,1)S(1)}, u32[]{:S(2)}, u32[]{:S(2)}) collective-permute-start(bf16[4,4,128,128]{3,2,1,0:T(8,128)(2,1)S(1)} %pad_maximum_fusion.own_ref), channel_id=1, source_target_pairs={{0,1},{1,0},{2,3},{3,2},{4,5},{5,4},{6,7},{7,6},{8,9},{9,8},{10,11... | collective-permute-start | bytes 1572872 | tf_op jit(solution)/shard_map/ppermute | solution.py:227
  94.9 17.6 %collective-permute-start.11 = (bf16[96,128]{1,0:T(8,128)(2,1)S(1)}, bf16[96,128]{1,0:T(8,128)(2,1)S(1)}, u32[]{:S(2)}, u32[]{:S(2)}) collective-permute-start(bf16[96,128]{1,0:T(8,128)(2,1)S(1)} %get-tuple-element.26), channel_id=1, source_target_pairs={{0,768},{32,800},{64,832},{96,864},{128,896},{160,928},{192,960},{... | collective-permute-start | bytes 73736 | tf_op jit(solution)/shard_map/ppermute | solution.py:244
  110.6 15.0 %collective-permute-start.9 = (bf16[96,128]{1,0:T(8,128)(2,1)S(1)}, bf16[96,128]{1,0:T(8,128)(2,1)S(1)}, u32[]{:S(2)}, u32[]{:S(2)}) collective-permute-start(bf16[96,128]{1,0:T(8,128)(2,1)S(1)} %get-tuple-element.25), channel_id=1, source_target_pairs={{0,256},{32,288},{64,320},{96,352},{128,384},{160,416},{192,448},{... | collective-permute-start | bytes 73736 | tf_op jit(solution)/shard_map/ppermute | solution.py:244
  112.6 19.0 %collective-permute-start.12 = (bf16[192,128]{1,0:T(8,128)(2,1)S(1)}, bf16[192,128]{1,0:T(8,128)(2,1)S(1)}, u32[]{:S(2)}, u32[]{:S(2)}) collective-permute-start(bf16[192,128]{1,0:T(8,128)(2,1)S(1)} %pad_maximum_fusion.2), channel_id=1, source_target_pairs={{0,768},{32,800},{64,832},{96,864},{128,896},{160,928},{192,960},{... | collective-permute-start | bytes 147464 | tf_op jit(solution)/shard_map/ppermute | solution.py:244
  125.6 20.9 %collective-permute-start.10 = (bf16[192,128]{1,0:T(8,128)(2,1)S(1)}, bf16[192,128]{1,0:T(8,128)(2,1)S(1)}, u32[]{:S(2)}, u32[]{:S(2)}) collective-permute-start(bf16[192,128]{1,0:T(8,128)(2,1)S(1)} %pad_maximum_fusion.1), channel_id=1, source_target_pairs={{0,256},{32,288},{64,320},{96,352},{128,384},{160,416},{192,448},{... | collective-permute-start | bytes 147464 | tf_op jit(solution)/shard_map/ppermute | solution.py:244

commit v3 on v2

--- a/solution.py
+++ b/solution.py
@@ -1,5 +1,3 @@
-import functools
-
 import jax
 import jax.numpy as jnp
 from jax import lax
@@ -118,10 +116,10 @@
         out_ref[i] = tangent
 
 
-def outer_kernel(offsets, at_ref, tan_ref, own_ref, oth_ref, *out_refs):
-    zhi, e, x, c = at_ref[0], at_ref[1], at_ref[2], at_ref[3]
-    for m, out_ref in zip(offsets, out_refs, strict=True):
-        j = (e - zhi - m + 2 * WIN) % WIN
+def outer_kernel(at_ref, tan_ref, own_ref, oth_ref, out_ref):
+    e, x, c = at_ref[0], at_ref[1], at_ref[2]
+    for dest in range(ZHI):
+        j = (e - dest + WIN) % WIN
         acc = None
         for dx in range(WIN):
             chip = (x - dx + WIN) % WIN
@@ -131,7 +129,7 @@
             rhs = jnp.concatenate([own_ref[dx, j], oth_ref[dx, j]], axis=0)
             part = dot(lhs, rhs)
             acc = part if acc is None else acc + part
-        out_ref[...] = acc.astype(out_ref.dtype)
+        out_ref[dest] = acc.astype(out_ref.dtype)
 
 
 def call(kernel, out_shape, specs, flops, nbytes, scratch=(), **more):
@@ -157,10 +155,10 @@
 
 
 def on_device(tokens, cotangent, expert_ids, gate_values, gate_proj, up_proj, down_proj, probe):
-    z, h = lax.axis_index("dp"), lax.axis_index("expert")
-    zhi, e, x, c = z // ZLO, h // 8, (h // 2) % WIN, h % 2
+    h = lax.axis_index("expert")
+    e, x, c = h // 8, (h // 2) % WIN, h % 2
     hid, feats = gate_proj.shape[0], tokens.shape[1]
-    at = jnp.stack([zhi, e, x, c]).astype(jnp.int32)
+    at = jnp.stack([e, x, c]).astype(jnp.int32)
 
     rows, cols = tokens.shape[0], gate_proj.shape[1]
     send, *rotated = call(
@@ -175,7 +173,7 @@
             pltpu.VMEM((rows, 2 * feats), BF16),
             DMA((4,)),
         ],
-    )(at[1:2], *map(in_hbm, (expert_ids.T, gate_values.T, tokens, cotangent)))
+    )(at[:1], *map(in_hbm, (expert_ids.T, gate_values.T, tokens, cotangent)))
     same_core = [[c0 + 2 * i for i in range(16)] for c0 in range(2)]
     own = lax.all_to_all(
         send, "expert", split_axis=0, concat_axis=0, tiled=True, axis_index_groups=same_core
@@ -209,7 +207,7 @@
         4 * hid * cols * CAP,
         4 << 20,
         columns,
-    )(at[3:4], own, *weights)
+    )(at[2:], own, *weights)
     tangent = call(
         tangent_kernel,
         sds((ZLO, hid, CAP), BF16),
@@ -217,7 +215,7 @@
         4 * hid * cols * CAP,
         4 << 20,
         columns,
-    )(at[3:4], oth, *weights, sums)
+    )(at[2:], oth, *weights, sums)
 
     ring = [mine]
     for dx in range(1, WIN):
@@ -231,26 +229,18 @@
         tangent, "dp", split_axis=0, concat_axis=0, tiled=True, axis_index_groups=near
     )
 
-    def outer(offsets, dtype):
-        return call(
-            functools.partial(outer_kernel, offsets),
-            [sds((hid, feats), dtype) for _ in offsets],
-            [SMEM] + [VMEM] * 3,
-            2 * len(offsets) * hid * 1024 * CAP,
-            2 << 20,
-        )(at, tangents, own_t, oth_t)
-
-    def hop(value, by):
-        return lax.ppermute(value, "dp", [(i, (i + by) % ZN) for i in range(ZN)])
-
-    (far,) = outer((2,), BF16)
-    half = hid // 2
-    from_below, from_above = hop(far[:half], ZLO), hop(far[half:], -ZLO)
-    here, up, down = outer((0, 1, 3), F32)
-    up = jnp.concatenate([up[:half] + from_below.astype(F32), up[half:]]).astype(BF16)
-    down = jnp.concatenate([down[:half], down[half:] + from_above.astype(F32)]).astype(BF16)
-    total = here + hop(up, ZLO).astype(F32) + hop(down, -ZLO).astype(F32)
-    return total.astype(BF16)
+    partial = call(
+        outer_kernel,
+        sds((ZHI, hid, feats), BF16),
+        [SMEM] + [VMEM] * 3,
+        2 * ZHI * hid * 1024 * CAP,
+        2 << 20,
+    )(at, tangents, own_t, oth_t)
+    far = [[8 * a + b for a in range(4)] for b in range(8)]
+    parts = lax.all_to_all(
+        partial, "dp", split_axis=0, concat_axis=0, tiled=True, axis_index_groups=far
+    )
+    return jnp.sum(parts.astype(F32), axis=0).astype(BF16)
 
 
 def solution(mesh):

time: 148 us -> 150 us (1.014)
  blocking collectives: 0 us -> 53.6 us
  starting transfers between devices: 102 us -> 70.5 us
  waiting for transfers between devices: 33.7 us -> 14.4 us
    all_to_all x0 -> x1, blocking collectives: none -> 53.6 us  [on_device(): lax.all_to_all(partial, 'dp', split_axis=0, concat_axis=0, tiled=True, ax...]
    ppermute x4 -> x0, starting transfers between devices: 31.1 us -> none  [hop(): return lax.ppermute(value, 'dp', [(i, (i + by) % ZN) for i in range(ZN)])]
    ppermute x4 -> x0, waiting for transfers between devices: 19.3 us -> none  [hop(): return lax.ppermute(value, 'dp', [(i, (i + by) % ZN) for i in range(ZN)])]
  transfers between devices with their start and end apart: 15 -> 11, of which waited for: 10 -> 7; matrix products, arithmetic and copies ran while one was open for 0% -> 0% of each run, Pallas kernels for 2% -> 2%
where the time goes in v3:
time: 150 us; the launch traced here: 149 us
  starting transfers between devices  70.5 us (47%)
  blocking collectives  53.6 us (36%)
  waiting for transfers between devices  14.4 us (10%)
  Pallas kernels  9.93 us (7%)
    all_to_all x1, blocking collectives, on_device(): lax.all_to_all(partial, 'dp', split_axis=0, concat_axis=0, tiled=True, ax...  53.6 us
    all_to_all x1, starting transfers between devices, on_device(): lax.all_to_all(tangent, 'dp', split_axis=0, concat_axis=0, tiled=True, ax...  36.4 us
    ppermute x4, starting transfers between devices, on_device(): moved.append(lax.ppermute(rotated[j], DPX, perm))  15.5 us
    ppermute x3, starting transfers between devices, on_device(): ring.append(lax.ppermute(mine, 'expert', perm))  7.75 us
    all_to_all x1, starting transfers between devices, on_device(): lax.all_to_all(send, 'expert', split_axis=0, concat_axis=0, tiled=True, a...  7.05 us
    ppermute x3, waiting for transfers between devices, on_device(): ring.append(lax.ppermute(mine, 'expert', perm))  5.68 us
    all_to_all x1, waiting for transfers between devices, on_device(): lax.all_to_all(tangent, 'dp', split_axis=0, concat_axis=0, tiled=True, ax...  4.82 us
    pallas_call x1, Pallas kernels, on_device(): call(tangent_kernel, sds((ZLO, hid, CAP), BF16), [SMEM, VMEM] + [HBM] * 4...  3.36 us
  transfers between devices with their start and end apart: 11, of which 7 were waited for; matrix products, arithmetic and copies ran while one was open for 0% of the time, Pallas kernels for 2%

profile of v3, /device:TPU:32, one launch (start us, length us, event | category | flops | bytes accessed | tf_op | source)
XLA Modules:
  0.0 149.4 jit_solution(11117805233087272987)
XLA Ops:
  0.0 2.8 %shard_map.82 = (bf16[16,256,128]{2,1,0:T(8,128)(2,1)}, bf16[128,128]{1,0:T(8,128)(2,1)S(1)}, bf16[128,128]{1,0:T(8,128)(2,1)S(1)}, bf16[128,128]{1,0:T(8,128)(2,1)S(1)}, bf16[128,128]{1,0:T(8,128)(2,1)S(1)}) custom-call(s32[1]{0:T(128)} %bitcast.y_ref, s32[8,1024]{1,0:T(8,128)} %bitcast.13, f32[8,1024]{1,0:T(8,128)} %bitcast.14, bf16[1024,128]{1,0:T(8,128)(2,1)} %tok_hbm.1, ...), custom_call_target="tpu_custom_call" | custom-call | flops 268435456 | bytes 2097152 | tf_op jit(solution)/shard_map/pallas_call | solution.py:164
  2.8 7.0 %all-to-all-start = ((bf16[16,256,128]{2,1,0:T(8,128)(2,1)}), bf16[16,256,128]{2,1,0:T(8,128)(2,1)S(1)}, u32[]{:S(2)}, u32[]{:S(2)}) async-start(bf16[16,256,128]{2,1,0:T(8,128)(2,1)} %get-tuple-element.12), calls=%async_computation | async-start | bytes 2097152 | tf_op jit(solution)/shard_map/all_to_all | solution.py:178
  9.9 1.9 %collective-permute-start = (bf16[128,128]{1,0:T(8,128)(2,1)S(1)}, bf16[128,128]{1,0:T(8,128)(2,1)S(1)}, u32[]{:S(2)}, u32[]{:S(2)}) collective-permute-start(bf16[128,128]{1,0:T(8,128)(2,1)S(1)} %get-tuple-element.13), channel_id=1, source_target_pairs={{0,0},{1,32},{2,64},{3,96},{4,128},{5,160},{6,192},{7,224},{8,8},{... | collective-permute-start | bytes 98312 | tf_op jit(solution)/shard_map/ppermute | solution.py:188
  11.8 5.0 %collective-permute-start.1 = (bf16[128,128]{1,0:T(8,128)(2,1)S(1)}, bf16[128,128]{1,0:T(8,128)(2,1)S(1)}, u32[]{:S(2)}, u32[]{:S(2)}) collective-permute-start(bf16[128,128]{1,0:T(8,128)(2,1)S(1)} %get-tuple-element.14), channel_id=1, source_target_pairs={{0,8},{1,40},{2,72},{3,104},{4,136},{5,168},{6,200},{7,232},{8,16}... | collective-permute-start | bytes 98312 | tf_op jit(solution)/shard_map/ppermute | solution.py:188
  16.8 4.0 %collective-permute-start.2 = (bf16[128,128]{1,0:T(8,128)(2,1)S(1)}, bf16[128,128]{1,0:T(8,128)(2,1)S(1)}, u32[]{:S(2)}, u32[]{:S(2)}) collective-permute-start(bf16[128,128]{1,0:T(8,128)(2,1)S(1)} %get-tuple-element.15), channel_id=1, source_target_pairs={{0,16},{1,48},{2,80},{3,112},{4,144},{5,176},{6,208},{7,240},{8,24... | collective-permute-start | bytes 98312 | tf_op jit(solution)/shard_map/ppermute | solution.py:188
  20.9 4.5 %collective-permute-start.3 = (bf16[128,128]{1,0:T(8,128)(2,1)S(1)}, bf16[128,128]{1,0:T(8,128)(2,1)S(1)}, u32[]{:S(2)}, u32[]{:S(2)}) collective-permute-start(bf16[128,128]{1,0:T(8,128)(2,1)S(1)} %get-tuple-element.16), channel_id=1, source_target_pairs={{0,24},{1,56},{2,88},{3,120},{4,152},{5,184},{6,216},{7,248},{8,0}... | collective-permute-start | bytes 98312 | tf_op jit(solution)/shard_map/ppermute | solution.py:188
  25.4 0.0 collective-permute-done.refs_0_
  25.4 0.0 collective-permute-done.1.refs_1_
  25.4 0.0 collective-permute-done.2.refs_2_
  25.4 1.6 %collective-permute-done.3.refs_3_ = bf16[128,128]{1,0:T(8,128)(2,1)S(1)} collective-permute-done((bf16[128,128]{1,0:T(8,128)(2,1)S(1)}, bf16[128,128]{1,0:T(8,128)(2,1)S(1)}, u32[]{:S(2)}, u32[]{:S(2)}) %collective-permute-start.3) | collective-permute-done | bytes 32800 | tf_op jit(solution)/shard_map/ppermute | solution.py:188
  27.0 0.5 all-to-all-done.rows_in
  27.5 1.9 %collective-permute-start.4 = (bf16[16,256,128]{2,1,0:T(8,128)(2,1)S(1)}, bf16[16,256,128]{2,1,0:T(8,128)(2,1)S(1)}, u32[]{:S(2)}, u32[]{:S(2)}) collective-permute-start(bf16[16,256,128]{2,1,0:T(8,128)(2,1)S(1)} %get-tuple-element.17.rows_ref), channel_id=1, source_target_pairs={{0,1},{1,0},{2,3},{3,2},{4,5},{5,4},{6,7},{7,6},{8,9},{9,8},{10,11... | collective-permute-start | bytes 3145736 | tf_op jit(solution)/shard_map/ppermute | solution.py:199
  29.5 2.6 %shard_map.84.acc_ref = f32[4,192,128]{2,1,0:T(8,128)S(1)} custom-call(s32[1]{0:T(128)} %bitcast.2.c_ref, bf16[16,256,128]{2,1,0:T(8,128)(2,1)S(1)} %get-tuple-element.17.rows_ref, bf16[192,4096]{1,0:T(8,128)(2,1)} %g_hbm.3, bf16[192,4096]{1,0:T(8,128)(2,1)} %u_hbm.3, bf16[192,4096]{1,0:T(8,128)(2,1)} %p_hbm.3, bf16[192,4096]{1,0:T(8,128)(2,1)} %d_hbm.3), custom_call_target="tpu_custom_call" | custom-call | flops 402653184 | bytes 4194304 | tf_op jit(solution)/shard_map/pallas_call | solution.py:203
  32.1 0.0 collective-permute-done.4.rows_ref
  32.1 3.4 %shard_map.85 = bf16[8,192,128]{2,1,0:T(8,128)(2,1)} custom-call(s32[1]{0:T(128)} %bitcast.2.c_ref, bf16[16,256,128]{2,1,0:T(8,128)(2,1)S(1)} %collective-permute-done.4.rows_ref, bf16[192,4096]{1,0:T(8,128)(2,1)} %g_hbm.3, bf16[192,4096]{1,0:T(8,128)(2,1)} %u_hbm.3, bf16[192,4096]{1,0:T(8,128)(2,1)} %p_hbm.3, bf16[192,4096]{1,0:T(8,128)(2,1)} %d_hbm.3, ...), custom_call_target="tpu_custom_call" | custom-call | flops 402653184 | bytes 4194304 | tf_op jit(solution)/shard_map/pallas_call | solution.py:211
  35.5 36.4 %all-to-all-start.1 = ((bf16[8,192,128]{2,1,0:T(8,128)(2,1)}), bf16[8,192,128]{2,1,0:T(8,128)(2,1)S(1)}, u32[]{:S(2)}, u32[]{:S(2)}) async-start(bf16[8,192,128]{2,1,0:T(8,128)(2,1)} %shard_map.85), calls=%async_computation.1 | async-start | bytes 786432 | tf_op jit(solution)/shard_map/all_to_all | solution.py:228
  71.9 1.9 %collective-permute-start.7 = (bf16[4,128,128]{2,1,0:T(8,128)(2,1)S(1)}, bf16[4,128,128]{2,1,0:T(8,128)(2,1)S(1)}, u32[]{:S(2)}, u32[]{:S(2)}) collective-permute-start(bf16[4,128,128]{2,1,0:T(8,128)(2,1)S(1)} %get-tuple-element.18), channel_id=1, source_target_pairs={{0,6},{1,7},{2,0},{3,1},{4,2},{5,3},{6,4},{7,5},{8,14},{9,15},{10,... | collective-permute-start | bytes 393224 | tf_op jit(solution)/shard_map/ppermute | solution.py:223
  73.8 1.9 %collective-permute-start.6 = (bf16[4,128,128]{2,1,0:T(8,128)(2,1)S(1)}, bf16[4,128,128]{2,1,0:T(8,128)(2,1)S(1)}, u32[]{:S(2)}, u32[]{:S(2)}) collective-permute-start(bf16[4,128,128]{2,1,0:T(8,128)(2,1)S(1)} %get-tuple-element.18), channel_id=1, source_target_pairs={{0,4},{1,5},{2,6},{3,7},{4,0},{5,1},{6,2},{7,3},{8,12},{9,13},{10,... | collective-permute-start | bytes 393224 | tf_op jit(solution)/shard_map/ppermute | solution.py:223
  75.8 3.9 %collective-permute-start.5 = (bf16[4,128,128]{2,1,0:T(8,128)(2,1)S(1)}, bf16[4,128,128]{2,1,0:T(8,128)(2,1)S(1)}, u32[]{:S(2)}, u32[]{:S(2)}) collective-permute-start(bf16[4,128,128]{2,1,0:T(8,128)(2,1)S(1)} %get-tuple-element.18), channel_id=1, source_target_pairs={{0,2},{1,3},{2,4},{3,5},{4,6},{5,7},{6,0},{7,1},{8,10},{9,11},{10,... | collective-permute-start | bytes 393224 | tf_op jit(solution)/shard_map/ppermute | solution.py:223
  79.7 0.3 collective-permute-done.7
  80.0 2.5 %collective-permute-done.6 = bf16[4,128,128]{2,1,0:T(8,128)(2,1)S(1)} collective-permute-done((bf16[4,128,128]{2,1,0:T(8,128)(2,1)S(1)}, bf16[4,128,128]{2,1,0:T(8,128)(2,1)S(1)}, u32[]{:S(2)}, u32[]{:S(2)}) %collective-permute-start.6) | collective-permute-done | bytes 131104 | tf_op jit(solution)/shard_map/ppermute | solution.py:223
  82.6 2.8 %collective-permute-done.5 = bf16[4,128,128]{2,1,0:T(8,128)(2,1)S(1)} collective-permute-done((bf16[4,128,128]{2,1,0:T(8,128)(2,1)S(1)}, bf16[4,128,128]{2,1,0:T(8,128)(2,1)S(1)}, u32[]{:S(2)}, u32[]{:S(2)}) %collective-permute-start.5) | collective-permute-done | bytes 131104 | tf_op jit(solution)/shard_map/ppermute | solution.py:223
  85.4 0.1 pad_maximum_fusion.own_ref
  85.4 1.9 %collective-permute-start.8 = (bf16[4,4,128,128]{3,2,1,0:T(8,128)(2,1)S(1)}, bf16[4,4,128,128]{3,2,1,0:T(8,128)(2,1)S(1)}, u32[]{:S(2)}, u32[]{:S(2)}) collective-permute-start(bf16[4,4,128,128]{3,2,1,0:T(8,128)(2,1)S(1)} %pad_maximum_fusion.own_ref), channel_id=1, source_target_pairs={{0,1},{1,0},{2,3},{3,2},{4,5},{5,4},{6,7},{7,6},{8,9},{9,8},{10,11... | collective-permute-start | bytes 1572872 | tf_op jit(solution)/shard_map/ppermute | solution.py:225
  87.4 0.1 pad_add_fusion.at_ref
  87.5 1.8 %collective-permute-done.8.oth_ref = bf16[4,4,128,128]{3,2,1,0:T(8,128)(2,1)S(1)} collective-permute-done((bf16[4,4,128,128]{3,2,1,0:T(8,128)(2,1)S(1)}, bf16[4,4,128,128]{3,2,1,0:T(8,128)(2,1)S(1)}, u32[]{:S(2)}, u32[]{:S(2)}) %collective-permute-start.8) | collective-permute-done | bytes 524320 | tf_op jit(solution)/shard_map/ppermute | solution.py:225
  89.2 4.8 %all-to-all-done.1.tan_ref = bf16[8,192,128]{2,1,0:T(8,128)(2,1)S(1)} async-done(((bf16[8,192,128]{2,1,0:T(8,128)(2,1)}), bf16[8,192,128]{2,1,0:T(8,128)(2,1)S(1)}, u32[]{:S(2)}, u32[]{:S(2)}) %all-to-all-start.1) | async-done | bytes 393248 | tf_op jit(solution)/shard_map/all_to_all | solution.py:228
  94.1 1.1 shard_map.86
  95.2 53.6 %all_to_all.15 = bf16[4,192,128]{2,1,0:T(8,128)(2,1)S(1)} all-to-all(bf16[4,192,128]{2,1,0:T(8,128)(2,1)S(1)} %shard_map.86), channel_id=1, replica_groups={{0,256,512,768},{32,288,544,800},{64,320,576,832},{96,352,608,864},{128..., dimensions={0} | all-to-all | bytes 393216 | tf_op jit(solution)/shard_map/all_to_all | solution.py:240
  148.8 0.7 reduce_sum.12
  (1 shorter events, 0.0 us)
Async XLA Ops:
  2.8 24.7 %all-to-all-start = ((bf16[16,256,128]{2,1,0:T(8,128)(2,1)}), bf16[16,256,128]{2,1,0:T(8,128)(2,1)S(1)}, u32[]{:S(2)}, u32[]{:S(2)}) async-start(bf16[16,256,128]{2,1,0:T(8,128)(2,1)} %get-tuple-element.12), calls=%async_computation | async-start | bytes 2097152 | tf_op jit(solution)/shard_map/all_to_all | solution.py:178
  9.9 15.5 %collective-permute-start = (bf16[128,128]{1,0:T(8,128)(2,1)S(1)}, bf16[128,128]{1,0:T(8,128)(2,1)S(1)}, u32[]{:S(2)}, u32[]{:S(2)}) collective-permute-start(bf16[128,128]{1,0:T(8,128)(2,1)S(1)} %get-tuple-element.13), channel_id=1, source_target_pairs={{0,0},{1,32},{2,64},{3,96},{4,128},{5,160},{6,192},{7,224},{8,8},{... | collective-permute-start | bytes 98312 | tf_op jit(solution)/shard_map/ppermute | solution.py:188
  11.8 13.6 %collective-permute-start.1 = (bf16[128,128]{1,0:T(8,128)(2,1)S(1)}, bf16[128,128]{1,0:T(8,128)(2,1)S(1)}, u32[]{:S(2)}, u32[]{:S(2)}) collective-permute-start(bf16[128,128]{1,0:T(8,128)(2,1)S(1)} %get-tuple-element.14), channel_id=1, source_target_pairs={{0,8},{1,40},{2,72},{3,104},{4,136},{5,168},{6,200},{7,232},{8,16}... | collective-permute-start | bytes 98312 | tf_op jit(solution)/shard_map/ppermute | solution.py:188
  16.8 8.6 %collective-permute-start.2 = (bf16[128,128]{1,0:T(8,128)(2,1)S(1)}, bf16[128,128]{1,0:T(8,128)(2,1)S(1)}, u32[]{:S(2)}, u32[]{:S(2)}) collective-permute-start(bf16[128,128]{1,0:T(8,128)(2,1)S(1)} %get-tuple-element.15), channel_id=1, source_target_pairs={{0,16},{1,48},{2,80},{3,112},{4,144},{5,176},{6,208},{7,240},{8,24... | collective-permute-start | bytes 98312 | tf_op jit(solution)/shard_map/ppermute | solution.py:188
  20.9 6.1 %collective-permute-start.3 = (bf16[128,128]{1,0:T(8,128)(2,1)S(1)}, bf16[128,128]{1,0:T(8,128)(2,1)S(1)}, u32[]{:S(2)}, u32[]{:S(2)}) collective-permute-start(bf16[128,128]{1,0:T(8,128)(2,1)S(1)} %get-tuple-element.16), channel_id=1, source_target_pairs={{0,24},{1,56},{2,88},{3,120},{4,152},{5,184},{6,216},{7,248},{8,0}... | collective-permute-start | bytes 98312 | tf_op jit(solution)/shard_map/ppermute | solution.py:188
  27.5 4.6 %collective-permute-start.4 = (bf16[16,256,128]{2,1,0:T(8,128)(2,1)S(1)}, bf16[16,256,128]{2,1,0:T(8,128)(2,1)S(1)}, u32[]{:S(2)}, u32[]{:S(2)}) collective-permute-start(bf16[16,256,128]{2,1,0:T(8,128)(2,1)S(1)} %get-tuple-element.17.rows_ref), channel_id=1, source_target_pairs={{0,1},{1,0},{2,3},{3,2},{4,5},{5,4},{6,7},{7,6},{8,9},{9,8},{10,11... | collective-permute-start | bytes 3145736 | tf_op jit(solution)/shard_map/ppermute | solution.py:199
  35.5 58.6 %all-to-all-start.1 = ((bf16[8,192,128]{2,1,0:T(8,128)(2,1)}), bf16[8,192,128]{2,1,0:T(8,128)(2,1)S(1)}, u32[]{:S(2)}, u32[]{:S(2)}) async-start(bf16[8,192,128]{2,1,0:T(8,128)(2,1)} %shard_map.85), calls=%async_computation.1 | async-start | bytes 786432 | tf_op jit(solution)/shard_map/all_to_all | solution.py:228
  71.9 8.1 %collective-permute-start.7 = (bf16[4,128,128]{2,1,0:T(8,128)(2,1)S(1)}, bf16[4,128,128]{2,1,0:T(8,128)(2,1)S(1)}, u32[]{:S(2)}, u32[]{:S(2)}) collective-permute-start(bf16[4,128,128]{2,1,0:T(8,128)(2,1)S(1)} %get-tuple-element.18), channel_id=1, source_target_pairs={{0,6},{1,7},{2,0},{3,1},{4,2},{5,3},{6,4},{7,5},{8,14},{9,15},{10,... | collective-permute-start | bytes 393224 | tf_op jit(solution)/shard_map/ppermute | solution.py:223
  73.8 8.7 %collective-permute-start.6 = (bf16[4,128,128]{2,1,0:T(8,128)(2,1)S(1)}, bf16[4,128,128]{2,1,0:T(8,128)(2,1)S(1)}, u32[]{:S(2)}, u32[]{:S(2)}) collective-permute-start(bf16[4,128,128]{2,1,0:T(8,128)(2,1)S(1)} %get-tuple-element.18), channel_id=1, source_target_pairs={{0,4},{1,5},{2,6},{3,7},{4,0},{5,1},{6,2},{7,3},{8,12},{9,13},{10,... | collective-permute-start | bytes 393224 | tf_op jit(solution)/shard_map/ppermute | solution.py:223
  75.8 9.6 %collective-permute-start.5 = (bf16[4,128,128]{2,1,0:T(8,128)(2,1)S(1)}, bf16[4,128,128]{2,1,0:T(8,128)(2,1)S(1)}, u32[]{:S(2)}, u32[]{:S(2)}) collective-permute-start(bf16[4,128,128]{2,1,0:T(8,128)(2,1)S(1)} %get-tuple-element.18), channel_id=1, source_target_pairs={{0,2},{1,3},{2,4},{3,5},{4,6},{5,7},{6,0},{7,1},{8,10},{9,11},{10,... | collective-permute-start | bytes 393224 | tf_op jit(solution)/shard_map/ppermute | solution.py:223
  85.4 3.8 %collective-permute-start.8 = (bf16[4,4,128,128]{3,2,1,0:T(8,128)(2,1)S(1)}, bf16[4,4,128,128]{3,2,1,0:T(8,128)(2,1)S(1)}, u32[]{:S(2)}, u32[]{:S(2)}) collective-permute-start(bf16[4,4,128,128]{3,2,1,0:T(8,128)(2,1)S(1)} %pad_maximum_fusion.own_ref), channel_id=1, source_target_pairs={{0,1},{1,0},{2,3},{3,2},{4,5},{5,4},{6,7},{7,6},{8,9},{9,8},{10,11... | collective-permute-start | bytes 1572872 | tf_op jit(solution)/shard_map/ppermute | solution.py:225

commit v4 on v3

v4 whole, which is shorter than its diff:
```python
import jax
import jax.numpy as jnp
from jax import lax
from jax.experimental import pallas as pl
from jax.experimental.pallas import tpu as pltpu
from jax.sharding import PartitionSpec as P

WIN = 4
CAP = 128
ZN, ZLO, ZHI = 32, 8, 4
F32, BF16 = jnp.float32, jnp.bfloat16
DPX = ("dp", "expert")
SMEM = pl.BlockSpec(memory_space=pltpu.SMEM)
VMEM = pl.BlockSpec(memory_space=pltpu.VMEM)
ANY = pl.BlockSpec(memory_space=pl.ANY)
HBM = pl.BlockSpec(memory_space=pltpu.HBM)
DMA = pltpu.SemaphoreType.DMA


def dot(a, b):
    return jnp.dot(a, b, preferred_element_type=F32)


def prep_kernel(ids_hbm, gates_hbm, tok_hbm, cot_hbm, sx_ref, sc_ref, ids_ref, gates_ref, both_ref, sems):
    feats = tok_hbm.shape[1]
    copies = [
        pltpu.make_async_copy(ids_hbm, ids_ref, sems.at[0]),
        pltpu.make_async_copy(gates_hbm, gates_ref, sems.at[1]),
        pltpu.make_async_copy(tok_hbm, both_ref.at[:, pl.ds(0, feats)], sems.at[2]),
        pltpu.make_async_copy(cot_hbm, both_ref.at[:, pl.ds(feats, feats)], sems.at[3]),
    ]
    for copy in copies:
        copy.start()
    rows = tok_hbm.shape[0]
    upper = (
        lax.broadcasted_iota(jnp.int32, (CAP, CAP), 0)
        <= lax.broadcasted_iota(jnp.int32, (CAP, CAP), 1)
    ).astype(BF16)
    copies[0].wait()
    copies[1].wait()
    ids = ids_ref[...]
    gates = gates_ref[...]
    present, gate = [], []
    for j in range(WIN):
        named = ids == j
        present.append(jnp.max(jnp.where(named, 1.0, 0.0), axis=0, keepdims=True))
        gate.append(jnp.sum(jnp.where(named, gates, 0.0), axis=0, keepdims=True))
    marks = jnp.concatenate(present + present, axis=0)
    base = jnp.full((2 * WIN, 1), -1.0, F32)
    slots = []
    for b in range(rows // CAP):
        part = dot(marks[:, b * CAP : (b + 1) * CAP].astype(BF16), upper)
        slots.append(part + base)
        base = base + part[:, CAP - 1 :]
    slot = jnp.concatenate(slots, axis=1)
    slot = jnp.where(marks > 0.0, slot, -1.0).astype(jnp.int32)
    index = lax.broadcasted_iota(jnp.int32, (CAP, rows), 0)
    copies[2].wait()
    copies[3].wait()
    both = both_ref[...]
    for j in range(WIN):
        placer = slot[j : j + 1, :] == index
        got = dot(jnp.where(placer, 1.0, 0.0).astype(BF16), both)
        factor = jnp.sum(jnp.where(placer, gate[j], 0.0), axis=1, keepdims=True)
        xs = got[:, :feats]
        cs = got[:, feats:] * factor
        xs = xs.T.astype(BF16)
        cs = cs.T.astype(BF16)
        for x in range(WIN):
            sx_ref[j * WIN + x] = xs
            sc_ref[j * WIN + x] = cs


def pick_kernel(at_ref, rows_ref, out_ref):
    for y in range(WIN):
        out_ref[y] = rows_ref[y * WIN + at_ref[0]]


def gate_kernel(rows_in, sums_in, moved_ref, rows_out, mine_ref):
    del rows_in, sums_in, rows_out
    mine_ref[...] = moved_ref[...]


def load(side, w_hbm, w_ref, sem):
    for s in range(w_hbm.shape[1] // (2 * CAP)):
        cols = pl.ds(pl.multiple_of((2 * s + side) * CAP, CAP), CAP)
        dst = w_ref.at[:, pl.ds(s * CAP, CAP)]
        pltpu.make_async_copy(w_hbm.at[:, cols], dst, sem).start()


def times(w_ref, sem, rows_ref):
    pltpu.make_async_copy(w_ref, w_ref, sem).wait()
    chips, feats, slots = rows_ref.shape
    return dot(w_ref[...], rows_ref[...].reshape(chips * feats, slots))


def project_kernel(c_ref, own_ref, oth_ref, g_hbm, u_hbm, p_hbm, out_ref, w_ref, sem):
    weights = (g_hbm, u_hbm, p_hbm)
    for n, w_hbm in enumerate(weights):
        for side, which in ((0, c_ref[0]), (1, 1 - c_ref[0])):
            load(which, w_hbm, w_ref.at[n, side], sem.at[n, side])
    for n in range(len(weights)):
        out_ref[n] = times(w_ref.at[n, 0], sem.at[n, 0], own_ref) + times(
            w_ref.at[n, 1], sem.at[n, 1], oth_ref
        )


def own_kernel(c_ref, rows_ref, d_hbm, acc_ref, rest_ref, w_ref, sem):
    load(c_ref[0], d_hbm, w_ref, sem.at[0])
    load(1 - c_ref[0], d_hbm, rest_ref, sem.at[1])
    acc_ref[...] = times(w_ref, sem.at[0], rows_ref)
    pltpu.make_async_copy(rest_ref, rest_ref, sem.at[1]).wait()


def tangent_kernel(rows_ref, w_ref, acc_ref, sums_ref, out_ref):
    chips, feats, slots = rows_ref.shape
    backward = acc_ref[...] + dot(w_ref[...], rows_ref[...].reshape(chips * feats, slots))
    preact, linear, probe_pre = sums_ref[0], sums_ref[1], sums_ref[2]
    sig = 1.0 / (1.0 + jnp.exp(-preact))
    curvature = sig * (1.0 - sig) * (2.0 + preact * (1.0 - 2.0 * sig))
    tangent = (backward * linear * curvature * probe_pre).astype(BF16)
    for i in range(ZLO):
        out_ref[i] = tangent


def outer_kernel(at_ref, tan_ref, own_ref, oth_ref, out_ref):
    x, c = at_ref[0], at_ref[1]
    for dest in range(ZHI):
        acc = None
        for dx in range(WIN):
            chip = (x - dx + WIN) % WIN
            lhs = jnp.concatenate(
                [tan_ref[2 * chip + c], tan_ref[2 * chip + 1 - c]], axis=1
            )
            rhs = jnp.concatenate([own_ref[dx, dest], oth_ref[dx, dest]], axis=1)
            part = lax.dot_general(
                lhs, rhs, (((1,), (1,)), ((), ())), preferred_element_type=F32
            )
            acc = part if acc is None else acc + part
        out_ref[dest] = acc.astype(out_ref.dtype)


def call(kernel, out_shape, specs, flops, nbytes, scratch=(), **more):
    return pl.pallas_call(
        kernel,
        out_shape=out_shape,
        in_specs=specs,
        scratch_shapes=scratch,
        compiler_params=pltpu.CompilerParams(vmem_limit_bytes=16 << 20),
        cost_estimate=pl.CostEstimate(
            flops=flops, bytes_accessed=nbytes, transcendentals=0
        ),
        **({"out_specs": jax.tree.map(lambda _: VMEM, out_shape)} | more),
    )


def in_hbm(value):
    return pltpu.with_memory_space_constraint(value, pltpu.HBM)


def sds(shape, dtype):
    return jax.ShapeDtypeStruct(shape, dtype)


def on_device(tokens, cotangent, expert_ids, gate_values, gate_proj, up_proj, down_proj, probe):
    z, h = lax.axis_index("dp"), lax.axis_index("expert")
    x, c = (h // 2) % WIN, h % 2
    hid, feats = gate_proj.shape[0], tokens.shape[1]
    at = jnp.stack([x, c, (x + z % ZLO // 2) % WIN]).astype(jnp.int32)
    rows, cols = tokens.shape[0], gate_proj.shape[1]
    sent = sds((16, feats, CAP), BF16)

    send_x, send_c = call(
        prep_kernel,
        [sent, sent],
        [HBM] * 4,
        2 * 512 * 1024 * 256,
        2 << 20,
        [
            pltpu.VMEM((8, rows), jnp.int32),
            pltpu.VMEM((8, rows), F32),
            pltpu.VMEM((rows, 2 * feats), BF16),
            DMA((4,)),
        ],
    )(*map(in_hbm, (expert_ids.T, gate_values.T, tokens, cotangent)))

    same_core = [[c0 + 2 * i for i in range(16)] for c0 in range(2)]
    swap = [(i, i ^ 1) for i in range(32)]

    def spread(send):
        return lax.all_to_all(
            send, "expert", split_axis=0, concat_axis=0, tiled=True, axis_index_groups=same_core
        )

    own_x, own_c = spread(send_x), spread(send_c)

    picked = call(
        pick_kernel, sds((WIN, feats, CAP), BF16), [SMEM, VMEM], 0, 1 << 18
    )(at[2:], own_x)
    perm = [
        (
            i * 32 + k,
            (i // 8 * 8 + (k // 2 % 4 + i % 8 // 2) % 4 * 2 + k % 2) * 32 + k // 8 * 8 + i % 8,
        )
        for i in range(ZN)
        for k in range(32)
    ]
    moved = lax.ppermute(picked, DPX, perm)

    oth_x = lax.ppermute(own_x, "expert", swap)
    weights = [in_hbm(w) for w in (gate_proj, up_proj, probe)]
    sums = call(
        project_kernel,
        sds((3, hid, CAP), F32),
        [SMEM, VMEM, VMEM] + [HBM] * 3,
        6 * hid * cols * CAP,
        6 << 20,
        [pltpu.VMEM((3, 2, hid, cols // 2), BF16), DMA((3, 2))],
    )(at[1:2], own_x, oth_x, *weights)
    own_c, mine = call(
        gate_kernel,
        [sent, sds((WIN, feats, CAP), BF16)],
        [ANY, ANY, VMEM],
        0,
        1 << 18,
        out_specs=[ANY, VMEM],
        input_output_aliases={0: 0},
    )(own_c, sums, moved)
    oth_c = lax.ppermute(own_c, "expert", swap)
    acc, rest = call(
        own_kernel,
        [sds((hid, CAP), F32), sds((hid, cols // 2), BF16)],
        [SMEM, VMEM, HBM],
        hid * cols * CAP,
        2 << 20,
        [pltpu.VMEM((hid, cols // 2), BF16), DMA((2,))],
    )(at[1:2], own_c, in_hbm(down_proj))
    tangent = call(
        tangent_kernel,
        sds((ZLO, hid, CAP), BF16),
        [VMEM] * 4,
        hid * cols * CAP,
        2 << 20,
    )(oth_c, rest, acc, sums)

    ring = [mine]
    for dx in range(1, WIN):
        perm = [(k, k // 8 * 8 + (k // 2 % 4 + dx) % 4 * 2 + k % 2) for k in range(32)]
        ring.append(lax.ppermute(mine, "expert", perm))
    own_t = jnp.stack(ring)
    oth_t = lax.ppermute(own_t, "expert", swap)

    near = [[8 * a + b for b in range(8)] for a in range(4)]
    tangents = lax.all_to_all(
        tangent, "dp", split_axis=0, concat_axis=0, tiled=True, axis_index_groups=near
    )

    partial = call(
        outer_kernel,
        sds((ZHI, hid, feats), BF16),
        [SMEM] + [VMEM] * 3,
        2 * ZHI * hid * 1024 * CAP,
        2 << 20,
    )(at[:2], tangents, own_t, oth_t)
    far = [[8 * a + b for a in range(4)] for b in range(8)]
    parts = lax.all_to_all(
        partial, "dp", split_axis=0, concat_axis=0, tiled=True, axis_index_groups=far
    )
    return jnp.sum(parts.astype(F32), axis=0).astype(BF16)


def solution(mesh):
    return jax.shard_map(
        on_device,
        mesh=mesh,
        in_specs=(
            P("dp", "expert"),
            P("dp", "expert"),
            P("dp", None),
            P("dp", None),
            P("expert", None),
            P("expert", None),
            P("expert", None),
            P("expert", None),
        ),
        out_specs=P("expert", "dp"),
        check_vma=False,
    )
```

time: 150 us -> 144 us (0.960)
  starting transfers between devices: 70.5 us -> 46.6 us
  blocking collectives: 53.6 us -> 76.6 us
  waiting for transfers between devices: 14.4 us -> 9.3 us
    all_to_all x1, starting transfers between devices: 36.4 us -> 17.1 us  [on_device(): lax.all_to_all(tangent, 'dp', split_axis=0, concat_axis=0, tiled=True, ax...]
    all_to_all x0 -> x1, blocking collectives: none -> 18.4 us  [spread(): lax.all_to_all(send, 'expert', split_axis=0, concat_axis=0, tiled=True, a...]
    all_to_all x1, blocking collectives: 53.6 us -> 58.3 us  [on_device(): lax.all_to_all(partial, 'dp', split_axis=0, concat_axis=0, tiled=True, ax...]
    ppermute x5 -> x3, starting transfers between devices: 17.4 us -> 13 us  [the longest x1 9.16 us: on_device(): moved = lax.ppermute(picked, DPX, perm)]
    all_to_all x1, waiting for transfers between devices: 4.82 us -> 1.01 us  [on_device(): lax.all_to_all(tangent, 'dp', split_axis=0, concat_axis=0, tiled=True, ax...]
    all_to_all x1, starting transfers between devices: 7.05 us -> 3.58 us  [spread(): lax.all_to_all(send, 'expert', split_axis=0, concat_axis=0, tiled=True, a...]
    ppermute x3, starting transfers between devices: 7.75 us -> 11 us  [on_device(): ring.append(lax.ppermute(mine, 'expert', perm))]
    pallas_call x4 -> x6, Pallas kernels: 8.83 us -> 8.7 us  [the longest x1 3.4 us: on_device(): call(project_kernel, sds((3, hid, CAP), F32), [SMEM, VMEM, VMEM] + [HBM]...]
  transfers between devices with their start and end apart: 11 -> 9, of which waited for: 7 -> 5; matrix products, arithmetic and copies ran while one was open for 0% -> 0% of each run, Pallas kernels for 2% -> 3%
where the time goes in v4:
time: 144 us; the launch traced here: 143 us
  blocking collectives  76.6 us (53%)
  starting transfers between devices  46.6 us (32%)
  Pallas kernels  9.8 us (7%)
  waiting for transfers between devices  9.3 us (6%)
    all_to_all x1, blocking collectives, on_device(): lax.all_to_all(partial, 'dp', split_axis=0, concat_axis=0, tiled=True, ax...  58.3 us
    all_to_all x1, blocking collectives, spread(): lax.all_to_all(send, 'expert', split_axis=0, concat_axis=0, tiled=True, a...  18.4 us
    all_to_all x1, starting transfers between devices, on_device(): lax.all_to_all(tangent, 'dp', split_axis=0, concat_axis=0, tiled=True, ax...  17.1 us
    ppermute x3, starting transfers between devices, on_device(): ring.append(lax.ppermute(mine, 'expert', perm))  11 us
    ppermute x1, starting transfers between devices, on_device(): moved = lax.ppermute(picked, DPX, perm)  9.16 us
    ppermute x3, waiting for transfers between devices, on_device(): ring.append(lax.ppermute(mine, 'expert', perm))  6.14 us
    all_to_all x1, starting transfers between devices, spread(): lax.all_to_all(send, 'expert', split_axis=0, concat_axis=0, tiled=True, a...  3.58 us
    pallas_call x1, Pallas kernels, on_device(): call(project_kernel, sds((3, hid, CAP), F32), [SMEM, VMEM, VMEM] + [HBM]...  3.4 us
  transfers between devices with their start and end apart: 9, of which 5 were waited for; matrix products, arithmetic and copies ran while one was open for 0% of the time, Pallas kernels for 3%

profile of v4, /device:TPU:32, one launch (start us, length us, event | category | flops | bytes accessed | tf_op | source)
XLA Modules:
  0.0 143.3 jit_solution(7474627431637286288)
XLA Ops:
  0.0 2.6 %shard_map.82 = (bf16[16,128,128]{2,1,0:T(8,128)(2,1)S(1)}, bf16[16,128,128]{2,1,0:T(8,128)(2,1)}) custom-call(s32[8,1024]{1,0:T(8,128)} %bitcast.13, f32[8,1024]{1,0:T(8,128)} %bitcast.14, bf16[1024,128]{1,0:T(8,128)(2,1)} %tok_hbm.1, bf16[1024,128]{1,0:T(8,128)(2,1)} %cot_hbm.1), custom_call_target="tpu_custom_call" | custom-call | flops 268435456 | bytes 2097152 | tf_op jit(solution)/shard_map/pallas_call | solution.py:173
  2.6 18.4 %all_to_all.20.own_ref.rows_ref = bf16[16,128,128]{2,1,0:T(8,128)(2,1)S(1)} all-to-all(bf16[16,128,128]{2,1,0:T(8,128)(2,1)S(1)} %get-tuple-element.12), channel_id=1, replica_groups={{0,2,4,6,8,10,12,14,16,18,20,22,24,26,28,30},{1,3,5,7,9,11,13,15,17,19,..., dimensions={0} | all-to-all | bytes 1048576 | tf_op jit(solution)/shard_map/all_to_all | solution.py:191
  21.0 1.9 %collective-permute-start = (bf16[16,128,128]{2,1,0:T(8,128)(2,1)S(1)}, bf16[16,128,128]{2,1,0:T(8,128)(2,1)S(1)}, u32[]{:S(2)}, u32[]{:S(2)}) collective-permute-start(bf16[16,128,128]{2,1,0:T(8,128)(2,1)S(1)} %all_to_all.20.own_ref.rows_ref), channel_id=1, source_target_pairs={{0,1},{1,0},{2,3},{3,2},{4,5},{5,4},{6,7},{7,6},{8,9},{9,8},{10,11... | collective-permute-start | bytes 1572872 | tf_op jit(solution)/shard_map/ppermute | solution.py:210
  22.9 3.6 %all-to-all-start = ((bf16[16,128,128]{2,1,0:T(8,128)(2,1)}), bf16[16,128,128]{2,1,0:T(8,128)(2,1)S(1)}, u32[]{:S(2)}, u32[]{:S(2)}) async-start(bf16[16,128,128]{2,1,0:T(8,128)(2,1)} %get-tuple-element.11), calls=%async_computation | async-start | bytes 1048576 | tf_op jit(solution)/shard_map/all_to_all | solution.py:191
  26.6 9.2 %collective-permute-start.1 = (bf16[4,128,128]{2,1,0:T(8,128)(2,1)S(1)}, bf16[4,128,128]{2,1,0:T(8,128)(2,1)S(1)}, u32[]{:S(2)}, u32[]{:S(2)}) collective-permute-start(bf16[4,128,128]{2,1,0:T(8,128)(2,1)S(1)} %shard_map.84), channel_id=1, source_target_pairs={{0,0},{1,32},{2,64},{3,96},{4,128},{5,160},{6,192},{7,224},{8,8},{... | collective-permute-start | bytes 393224 | tf_op jit(solution)/shard_map/ppermute | solution.py:208
  35.8 0.0 collective-permute-done.oth_ref
  35.8 3.4 %shard_map.83.sums_in.sums_ref = f32[3,192,128]{2,1,0:T(8,128)S(1)} custom-call(s32[1]{0:T(128)} %bitcast.1.c_ref, bf16[16,128,128]{2,1,0:T(8,128)(2,1)S(1)} %all_to_all.20.own_ref.rows_ref, bf16[16,128,128]{2,1,0:T(8,128)(2,1)S(1)} %collective-permute-done.oth_ref, bf16[192,4096]{1,0:T(8,128)(2,1)} %g_hbm.1, bf16[192,4096]{1,0:T(8,128)(2,1)} %u_hbm.1, ...), custom_call_target="tpu_custom_call" | custom-call | flops 603979776 | bytes 6291456 | tf_op jit(solution)/shard_map/pallas_call | solution.py:212
  39.2 0.0 all-to-all-done.rows_in
  39.2 0.0 collective-permute-done.1.moved_ref
  39.3 1.9 %collective-permute-start.2 = (bf16[16,128,128]{2,1,0:T(8,128)(2,1)S(1)}, bf16[16,128,128]{2,1,0:T(8,128)(2,1)S(1)}, u32[]{:S(2)}, u32[]{:S(2)}) collective-permute-start(bf16[16,128,128]{2,1,0:T(8,128)(2,1)S(1)} %get-tuple-element.13.rows_ref), channel_id=1, source_target_pairs={{0,1},{1,0},{2,3},{3,2},{4,5},{5,4},{6,7},{7,6},{8,9},{9,8},{10,11... | collective-permute-start | bytes 1572872 | tf_op jit(solution)/shard_map/ppermute | solution.py:229
  41.2 1.5 %shard_map.86 = (f32[192,128]{1,0:T(8,128)S(1)}, bf16[192,2048]{1,0:T(8,128)(2,1)S(1)}) custom-call(s32[1]{0:T(128)} %bitcast.1.c_ref, bf16[16,128,128]{2,1,0:T(8,128)(2,1)S(1)} %get-tuple-element.13.rows_ref, bf16[192,4096]{1,0:T(8,128)(2,1)} %d_hbm.1), custom_call_target="tpu_custom_call" | custom-call | flops 100663296 | bytes 2097152 | tf_op jit(solution)/shard_map/pallas_call | solution.py:230
  42.7 0.3 collective-permute-done.2.rows_ref
  43.1 1.1 shard_map.87
  44.2 17.1 %all-to-all-start.2 = ((bf16[8,192,128]{2,1,0:T(8,128)(2,1)}), bf16[8,192,128]{2,1,0:T(8,128)(2,1)S(1)}, u32[]{:S(2)}, u32[]{:S(2)}) async-start(bf16[8,192,128]{2,1,0:T(8,128)(2,1)} %shard_map.87), calls=%async_computation.2 | async-start | bytes 786432 | tf_op jit(solution)/shard_map/all_to_all | solution.py:254
  61.3 2.0 %collective-permute-start.5 = (bf16[4,128,128]{2,1,0:T(8,128)(2,1)S(1)}, bf16[4,128,128]{2,1,0:T(8,128)(2,1)S(1)}, u32[]{:S(2)}, u32[]{:S(2)}) collective-permute-start(bf16[4,128,128]{2,1,0:T(8,128)(2,1)S(1)} %get-tuple-element.16), channel_id=1, source_target_pairs={{0,6},{1,7},{2,0},{3,1},{4,2},{5,3},{6,4},{7,5},{8,14},{9,15},{10,... | collective-permute-start | bytes 393224 | tf_op jit(solution)/shard_map/ppermute | solution.py:249
  63.3 7.1 %collective-permute-start.4 = (bf16[4,128,128]{2,1,0:T(8,128)(2,1)S(1)}, bf16[4,128,128]{2,1,0:T(8,128)(2,1)S(1)}, u32[]{:S(2)}, u32[]{:S(2)}) collective-permute-start(bf16[4,128,128]{2,1,0:T(8,128)(2,1)S(1)} %get-tuple-element.16), channel_id=1, source_target_pairs={{0,4},{1,5},{2,6},{3,7},{4,0},{5,1},{6,2},{7,3},{8,12},{9,13},{10,... | collective-permute-start | bytes 393224 | tf_op jit(solution)/shard_map/ppermute | solution.py:249
  70.3 1.9 %collective-permute-start.3 = (bf16[4,128,128]{2,1,0:T(8,128)(2,1)S(1)}, bf16[4,128,128]{2,1,0:T(8,128)(2,1)S(1)}, u32[]{:S(2)}, u32[]{:S(2)}) collective-permute-start(bf16[4,128,128]{2,1,0:T(8,128)(2,1)S(1)} %get-tuple-element.16), channel_id=1, source_target_pairs={{0,2},{1,3},{2,4},{3,5},{4,6},{5,7},{6,0},{7,1},{8,10},{9,11},{10,... | collective-permute-start | bytes 393224 | tf_op jit(solution)/shard_map/ppermute | solution.py:249
  72.3 0.0 collective-permute-done.5
  72.3 1.5 %collective-permute-done.4 = bf16[4,128,128]{2,1,0:T(8,128)(2,1)S(1)} collective-permute-done((bf16[4,128,128]{2,1,0:T(8,128)(2,1)S(1)}, bf16[4,128,128]{2,1,0:T(8,128)(2,1)S(1)}, u32[]{:S(2)}, u32[]{:S(2)}) %collective-permute-start.4) | collective-permute-done | bytes 131104 | tf_op jit(solution)/shard_map/ppermute | solution.py:249
  73.8 4.6 %collective-permute-done.3 = bf16[4,128,128]{2,1,0:T(8,128)(2,1)S(1)} collective-permute-done((bf16[4,128,128]{2,1,0:T(8,128)(2,1)S(1)}, bf16[4,128,128]{2,1,0:T(8,128)(2,1)S(1)}, u32[]{:S(2)}, u32[]{:S(2)}) %collective-permute-start.3) | collective-permute-done | bytes 131104 | tf_op jit(solution)/shard_map/ppermute | solution.py:249
  78.4 0.1 pad_maximum_fusion.own_ref
  78.5 1.9 %collective-permute-start.6 = (bf16[4,4,128,128]{3,2,1,0:T(8,128)(2,1)S(1)}, bf16[4,4,128,128]{3,2,1,0:T(8,128)(2,1)S(1)}, u32[]{:S(2)}, u32[]{:S(2)}) collective-permute-start(bf16[4,4,128,128]{3,2,1,0:T(8,128)(2,1)S(1)} %pad_maximum_fusion.own_ref), channel_id=1, source_target_pairs={{0,1},{1,0},{2,3},{3,2},{4,5},{5,4},{6,7},{7,6},{8,9},{9,8},{10,11... | collective-permute-start | bytes 1572872 | tf_op jit(solution)/shard_map/ppermute | solution.py:251
  80.4 0.1 pad_add_fusion.at_ref
  80.5 1.8 %collective-permute-done.6.oth_ref = bf16[4,4,128,128]{3,2,1,0:T(8,128)(2,1)S(1)} collective-permute-done((bf16[4,4,128,128]{3,2,1,0:T(8,128)(2,1)S(1)}, bf16[4,4,128,128]{3,2,1,0:T(8,128)(2,1)S(1)}, u32[]{:S(2)}, u32[]{:S(2)}) %collective-permute-start.6) | collective-permute-done | bytes 524320 | tf_op jit(solution)/shard_map/ppermute | solution.py:251
  82.3 1.0 all-to-all-done.2.tan_ref
  83.3 1.1 shard_map.88
  84.4 58.3 %all_to_all.21 = bf16[4,192,128]{2,1,0:T(8,128)(2,1)S(1)} all-to-all(bf16[4,192,128]{2,1,0:T(8,128)(2,1)S(1)} %shard_map.88), channel_id=1, replica_groups={{0,256,512,768},{32,288,544,800},{64,320,576,832},{96,352,608,864},{128..., dimensions={0} | all-to-all | bytes 393216 | tf_op jit(solution)/shard_map/all_to_all | solution.py:266
  142.7 0.7 reduce_sum.12
  (2 shorter events, 0.0 us)
Async XLA Ops:
  21.0 14.8 %collective-permute-start = (bf16[16,128,128]{2,1,0:T(8,128)(2,1)S(1)}, bf16[16,128,128]{2,1,0:T(8,128)(2,1)S(1)}, u32[]{:S(2)}, u32[]{:S(2)}) collective-permute-start(bf16[16,128,128]{2,1,0:T(8,128)(2,1)S(1)} %all_to_all.20.own_ref.rows_ref), channel_id=1, source_target_pairs={{0,1},{1,0},{2,3},{3,2},{4,5},{5,4},{6,7},{7,6},{8,9},{9,8},{10,11... | collective-permute-start | bytes 1572872 | tf_op jit(solution)/shard_map/ppermute | solution.py:210
  22.9 16.3 %all-to-all-start = ((bf16[16,128,128]{2,1,0:T(8,128)(2,1)}), bf16[16,128,128]{2,1,0:T(8,128)(2,1)S(1)}, u32[]{:S(2)}, u32[]{:S(2)}) async-start(bf16[16,128,128]{2,1,0:T(8,128)(2,1)} %get-tuple-element.11), calls=%async_computation | async-start | bytes 1048576 | tf_op jit(solution)/shard_map/all_to_all | solution.py:191
  26.6 12.6 %collective-permute-start.1 = (bf16[4,128,128]{2,1,0:T(8,128)(2,1)S(1)}, bf16[4,128,128]{2,1,0:T(8,128)(2,1)S(1)}, u32[]{:S(2)}, u32[]{:S(2)}) collective-permute-start(bf16[4,128,128]{2,1,0:T(8,128)(2,1)S(1)} %shard_map.84), channel_id=1, source_target_pairs={{0,0},{1,32},{2,64},{3,96},{4,128},{5,160},{6,192},{7,224},{8,8},{... | collective-permute-start | bytes 393224 | tf_op jit(solution)/shard_map/ppermute | solution.py:208
  39.3 3.8 %collective-permute-start.2 = (bf16[16,128,128]{2,1,0:T(8,128)(2,1)S(1)}, bf16[16,128,128]{2,1,0:T(8,128)(2,1)S(1)}, u32[]{:S(2)}, u32[]{:S(2)}) collective-permute-start(bf16[16,128,128]{2,1,0:T(8,128)(2,1)S(1)} %get-tuple-element.13.rows_ref), channel_id=1, source_target_pairs={{0,1},{1,0},{2,3},{3,2},{4,5},{5,4},{6,7},{7,6},{8,9},{9,8},{10,11... | collective-permute-start | bytes 1572872 | tf_op jit(solution)/shard_map/ppermute | solution.py:229
  44.2 39.1 %all-to-all-start.2 = ((bf16[8,192,128]{2,1,0:T(8,128)(2,1)}), bf16[8,192,128]{2,1,0:T(8,128)(2,1)S(1)}, u32[]{:S(2)}, u32[]{:S(2)}) async-start(bf16[8,192,128]{2,1,0:T(8,128)(2,1)} %shard_map.87), calls=%async_computation.2 | async-start | bytes 786432 | tf_op jit(solution)/shard_map/all_to_all | solution.py:254
  61.3 11.0 %collective-permute-start.5 = (bf16[4,128,128]{2,1,0:T(8,128)(2,1)S(1)}, bf16[4,128,128]{2,1,0:T(8,128)(2,1)S(1)}, u32[]{:S(2)}, u32[]{:S(2)}) collective-permute-start(bf16[4,128,128]{2,1,0:T(8,128)(2,1)S(1)} %get-tuple-element.16), channel_id=1, source_target_pairs={{0,6},{1,7},{2,0},{3,1},{4,2},{5,3},{6,4},{7,5},{8,14},{9,15},{10,... | collective-permute-start | bytes 393224 | tf_op jit(solution)/shard_map/ppermute | solution.py:249
  63.3 10.5 %collective-permute-start.4 = (bf16[4,128,128]{2,1,0:T(8,128)(2,1)S(1)}, bf16[4,128,128]{2,1,0:T(8,128)(2,1)S(1)}, u32[]{:S(2)}, u32[]{:S(2)}) collective-permute-start(bf16[4,128,128]{2,1,0:T(8,128)(2,1)S(1)} %get-tuple-element.16), channel_id=1, source_target_pairs={{0,4},{1,5},{2,6},{3,7},{4,0},{5,1},{6,2},{7,3},{8,12},{9,13},{10,... | collective-permute-start | bytes 393224 | tf_op jit(solution)/shard_map/ppermute | solution.py:249
  70.3 8.1 %collective-permute-start.3 = (bf16[4,128,128]{2,1,0:T(8,128)(2,1)S(1)}, bf16[4,128,128]{2,1,0:T(8,128)(2,1)S(1)}, u32[]{:S(2)}, u32[]{:S(2)}) collective-permute-start(bf16[4,128,128]{2,1,0:T(8,128)(2,1)S(1)} %get-tuple-element.16), channel_id=1, source_target_pairs={{0,2},{1,3},{2,4},{3,5},{4,6},{5,7},{6,0},{7,1},{8,10},{9,11},{10,... | collective-permute-start | bytes 393224 | tf_op jit(solution)/shard_map/ppermute | solution.py:249
  78.5 3.8 %collective-permute-start.6 = (bf16[4,4,128,128]{3,2,1,0:T(8,128)(2,1)S(1)}, bf16[4,4,128,128]{3,2,1,0:T(8,128)(2,1)S(1)}, u32[]{:S(2)}, u32[]{:S(2)}) collective-permute-start(bf16[4,4,128,128]{3,2,1,0:T(8,128)(2,1)S(1)} %pad_maximum_fusion.own_ref), channel_id=1, source_target_pairs={{0,1},{1,0},{2,3},{3,2},{4,5},{5,4},{6,7},{7,6},{8,9},{9,8},{10,11... | collective-permute-start | bytes 1572872 | tf_op jit(solution)/shard_map/ppermute | solution.py:251

commit v5 on v3

--- a/solution.py
+++ b/solution.py
@@ -12,7 +12,6 @@
 DPX = ("dp", "expert")
 SMEM = pl.BlockSpec(memory_space=pltpu.SMEM)
 VMEM = pl.BlockSpec(memory_space=pltpu.VMEM)
-ANY = pl.BlockSpec(memory_space=pl.ANY)
 HBM = pl.BlockSpec(memory_space=pltpu.HBM)
 DMA = pltpu.SemaphoreType.DMA
 
@@ -21,8 +20,7 @@
     return jnp.dot(a, b, preferred_element_type=F32)
 
 
-def prep_kernel(y_ref, ids_hbm, gates_hbm, tok_hbm, cot_hbm, send_ref, *refs):
-    rot_refs, (ids_ref, gates_ref, both_ref, sems) = refs[:WIN], refs[WIN:]
+def prep_kernel(ids_hbm, gates_hbm, tok_hbm, cot_hbm, send_ref, ids_ref, gates_ref, both_ref, sems):
     feats = tok_hbm.shape[1]
     copies = [
         pltpu.make_async_copy(ids_hbm, ids_ref, sems.at[0]),
@@ -32,7 +30,6 @@
     ]
     for copy in copies:
         copy.start()
-    y = y_ref[0]
     rows = tok_hbm.shape[0]
     upper = (
         lax.broadcasted_iota(jnp.int32, (CAP, CAP), 0)
@@ -44,7 +41,7 @@
     gates = gates_ref[...]
     present, gate = [], []
     for j in range(WIN):
-        named = ids == (y + j) % WIN
+        named = ids == j
         present.append(jnp.max(jnp.where(named, 1.0, 0.0), axis=0, keepdims=True))
         gate.append(jnp.sum(jnp.where(named, gates, 0.0), axis=0, keepdims=True))
     marks = jnp.concatenate(present + present, axis=0)
@@ -66,17 +63,14 @@
         factor = jnp.sum(jnp.where(placer, gate[j], 0.0), axis=1, keepdims=True)
         xs = got[:, :feats]
         cs = got[:, feats:] * factor
-        rot_refs[j][...] = xs.astype(BF16)
         chunk = jnp.concatenate([xs.T, cs.T], axis=0).astype(BF16)
         for x in range(WIN):
-            send_ref[((y + j) % WIN) * WIN + x] = chunk
-
-
-def gate_kernel(rows_in, *refs):
-    del rows_in
-    moved_refs, mine_ref = refs[:WIN], refs[WIN + 1]
-    for j in range(WIN):
-        mine_ref[j] = moved_refs[j][...]
+            send_ref[j * WIN + x] = chunk
+
+
+def pick_kernel(at_ref, rows_ref, out_ref):
+    for y in range(WIN):
+        out_ref[y] = rows_ref[y * WIN + at_ref[0], : out_ref.shape[1]]
 
 
 def load(side, w_hbms, w_ref, sem):
@@ -111,23 +105,28 @@
     ]
     sig = 1.0 / (1.0 + jnp.exp(-preact))
     curvature = sig * (1.0 - sig) * (2.0 + preact * (1.0 - 2.0 * sig))
-    tangent = (backward * linear * curvature * probe_pre).astype(BF16)
+    out_ref[...] = (backward * linear * curvature * probe_pre).astype(BF16)
+
+
+def fan_kernel(tan_ref, moved_ref, out_ref, mine_ref):
     for i in range(ZLO):
-        out_ref[i] = tangent
+        out_ref[i] = tan_ref[...]
+    mine_ref[...] = moved_ref[...]
 
 
 def outer_kernel(at_ref, tan_ref, own_ref, oth_ref, out_ref):
-    e, x, c = at_ref[0], at_ref[1], at_ref[2]
+    x, c = at_ref[0], at_ref[1]
     for dest in range(ZHI):
-        j = (e - dest + WIN) % WIN
         acc = None
         for dx in range(WIN):
             chip = (x - dx + WIN) % WIN
             lhs = jnp.concatenate(
                 [tan_ref[2 * chip + c], tan_ref[2 * chip + 1 - c]], axis=1
             )
-            rhs = jnp.concatenate([own_ref[dx, j], oth_ref[dx, j]], axis=0)
-            part = dot(lhs, rhs)
+            rhs = jnp.concatenate([own_ref[dx, dest], oth_ref[dx, dest]], axis=1)
+            part = lax.dot_general(
+                lhs, rhs, (((1,), (1,)), ((), ())), preferred_element_type=F32
+            )
             acc = part if acc is None else acc + part
         out_ref[dest] = acc.astype(out_ref.dtype)
 
@@ -155,16 +154,16 @@
 
 
 def on_device(tokens, cotangent, expert_ids, gate_values, gate_proj, up_proj, down_proj, probe):
-    h = lax.axis_index("expert")
-    e, x, c = h // 8, (h // 2) % WIN, h % 2
+    z, h = lax.axis_index("dp"), lax.axis_index("expert")
+    x, c = (h // 2) % WIN, h % 2
     hid, feats = gate_proj.shape[0], tokens.shape[1]
-    at = jnp.stack([e, x, c]).astype(jnp.int32)
-
+    at = jnp.stack([x, c, (x + z % ZLO // 2 + z % 2 + 2 * c) % WIN]).astype(jnp.int32)
     rows, cols = tokens.shape[0], gate_proj.shape[1]
-    send, *rotated = call(
+
+    send = call(
         prep_kernel,
-        [sds((16, 2 * feats, CAP), BF16)] + [sds((CAP, feats), BF16)] * WIN,
-        [SMEM] + [HBM] * 4,
+        sds((16, 2 * feats, CAP), BF16),
+        [HBM] * 4,
         2 * 512 * 1024 * 256,
         2 << 20,
         [
@@ -173,30 +172,27 @@
             pltpu.VMEM((rows, 2 * feats), BF16),
             DMA((4,)),
         ],
-    )(at[:1], *map(in_hbm, (expert_ids.T, gate_values.T, tokens, cotangent)))
+    )(*map(in_hbm, (expert_ids.T, gate_values.T, tokens, cotangent)))
+
     same_core = [[c0 + 2 * i for i in range(16)] for c0 in range(2)]
     own = lax.all_to_all(
         send, "expert", split_axis=0, concat_axis=0, tiled=True, axis_index_groups=same_core
     )
-    moved = []
-    for j in range(WIN):
-        perm = [
-            (i * 32 + k, (i // 8 * 8 + k % 8) * 32 + ((k // 8 + j) % 4) * 8 + i % 8)
-            for i in range(ZN)
-            for k in range(32)
-        ]
-        moved.append(lax.ppermute(rotated[j], DPX, perm))
-    own, mine = call(
-        gate_kernel,
-        [sds(own.shape, BF16), sds((WIN, CAP, feats), BF16)],
-        [ANY] + [VMEM] * WIN,
-        0,
-        1 << 18,
-        out_specs=[ANY, VMEM],
-        input_output_aliases={0: 0},
-    )(own, *moved)
     swap = [(i, i ^ 1) for i in range(32)]
     oth = lax.ppermute(own, "expert", swap)
+
+    picked = call(
+        pick_kernel, sds((WIN, feats, CAP), BF16), [SMEM, VMEM], 0, 1 << 18
+    )(at[2:], own)
+    perm = [
+        (
+            i * 32 + k,
+            (i // 8 * 8 + (k // 2 + i % 8 // 2 + i % 2 + 2 * (k % 2)) % 4 * 2 + k % 2) * 32 + k // 8 * 8 + i % 8,
+        )
+        for i in range(ZN)
+        for k in range(32)
+    ]
+    moved = lax.ppermute(picked, DPX, perm)
 
     weights = [in_hbm(w) for w in (gate_proj, up_proj, probe, down_proj)]
     columns = [pltpu.VMEM((4, hid, cols // 2), BF16), DMA((4,))]
@@ -207,15 +203,23 @@
         4 * hid * cols * CAP,
         4 << 20,
         columns,
-    )(at[2:], own, *weights)
+    )(at[1:2], own, *weights)
     tangent = call(
         tangent_kernel,
-        sds((ZLO, hid, CAP), BF16),
+        sds((hid, CAP), BF16),
         [SMEM, VMEM] + [HBM] * 4 + [VMEM],
         4 * hid * cols * CAP,
         4 << 20,
         columns,
-    )(at[2:], oth, *weights, sums)
+    )(at[1:2], oth, *weights, sums)
+
+    tangent, mine = call(
+        fan_kernel,
+        [sds((ZLO, hid, CAP), BF16), sds((WIN, feats, CAP), BF16)],
+        [VMEM, VMEM],
+        0,
+        1 << 19,
+    )(tangent, moved)
 
     ring = [mine]
     for dx in range(1, WIN):
@@ -235,7 +239,7 @@
         [SMEM] + [VMEM] * 3,
         2 * ZHI * hid * 1024 * CAP,
         2 << 20,
-    )(at, tangents, own_t, oth_t)
+    )(at[:2], tangents, own_t, oth_t)
     far = [[8 * a + b for a in range(4)] for b in range(8)]
     parts = lax.all_to_all(
         partial, "dp", split_axis=0, concat_axis=0, tiled=True, axis_index_groups=far

time: 150 us -> 136 us (0.907)
  starting transfers between devices: 70.5 us -> 33.4 us
  blocking collectives: 53.6 us -> 81.4 us
  waiting for transfers between devices: 14.4 us -> 10.9 us
    all_to_all x0 -> x1, blocking collectives: none -> 24 us  [on_device(): lax.all_to_all(send, 'expert', split_axis=0, concat_axis=0, tiled=True, a...]
    all_to_all x1, starting transfers between devices: 36.4 us -> 17.6 us  [on_device(): lax.all_to_all(tangent, 'dp', split_axis=0, concat_axis=0, tiled=True, ax...]
    ppermute x4 -> x1, starting transfers between devices: 15.5 us -> 3.93 us  [on_device(): moved = lax.ppermute(picked, DPX, perm)]
    all_to_all x1 -> x0, starting transfers between devices: 7.05 us -> none  [on_device(): lax.all_to_all(send, 'expert', split_axis=0, concat_axis=0, tiled=True, a...]
    all_to_all x1, blocking collectives: 53.6 us -> 57.5 us  [on_device(): lax.all_to_all(partial, 'dp', split_axis=0, concat_axis=0, tiled=True, ax...]
    all_to_all x1, waiting for transfers between devices: 4.82 us -> 2.33 us  [on_device(): lax.all_to_all(tangent, 'dp', split_axis=0, concat_axis=0, tiled=True, ax...]
    ppermute x4 -> x1, waiting for transfers between devices: 1.56 us -> 0.01 us  [on_device(): moved = lax.ppermute(picked, DPX, perm)]
    pallas_call x3 -> x4, Pallas kernels: 6.19 us -> 5.31 us  [the longest x1 2.63 us: on_device(): call(tangent_kernel, sds((hid, CAP), BF16), [SMEM, VMEM] + [HBM] * 4 + [V...]
  transfers between devices with their start and end apart: 11 -> 7, of which waited for: 7 -> 4; matrix products, arithmetic and copies ran while one was open for 0% -> 0% of each run, Pallas kernels for 2% -> 4%
where the time goes in v5:
time: 136 us
  blocking collectives  81.4 us (60%)
  starting transfers between devices  33.4 us (25%)
  waiting for transfers between devices  10.9 us (8%)
  Pallas kernels  9.04 us (7%)
    all_to_all x1, blocking collectives, on_device(): lax.all_to_all(partial, 'dp', split_axis=0, concat_axis=0, tiled=True, ax...  57.5 us
    all_to_all x1, blocking collectives, on_device(): lax.all_to_all(send, 'expert', split_axis=0, concat_axis=0, tiled=True, a...  24 us
    all_to_all x1, starting transfers between devices, on_device(): lax.all_to_all(tangent, 'dp', split_axis=0, concat_axis=0, tiled=True, ax...  17.6 us
    ppermute x3, starting transfers between devices, on_device(): ring.append(lax.ppermute(mine, 'expert', perm))  8.02 us
    ppermute x3, waiting for transfers between devices, on_device(): ring.append(lax.ppermute(mine, 'expert', perm))  6.77 us
    ppermute x1, starting transfers between devices, on_device(): moved = lax.ppermute(picked, DPX, perm)  3.93 us
  transfers between devices with their start and end apart: 7, of which 4 were waited for; matrix products, arithmetic and copies ran while one was open for 0% of the time, Pallas kernels for 4%

profile of v5, /device:TPU:32, one launch (start us, length us, event | category | flops | bytes accessed | tf_op | source)
XLA Modules:
  0.0 135.8 jit_solution(15164282159641056372)
XLA Ops:
  0.0 1.9 %shard_map.82 = bf16[16,256,128]{2,1,0:T(8,128)(2,1)S(1)} custom-call(s32[8,1024]{1,0:T(8,128)} %bitcast.13, f32[8,1024]{1,0:T(8,128)} %bitcast.14, bf16[1024,128]{1,0:T(8,128)(2,1)} %tok_hbm.1, bf16[1024,128]{1,0:T(8,128)(2,1)} %cot_hbm.1), custom_call_target="tpu_custom_call" | custom-call | flops 268435456 | bytes 2097152 | tf_op jit(solution)/shard_map/pallas_call | solution.py:163
  1.9 24.0 %all_to_all.15.rows_ref = bf16[16,256,128]{2,1,0:T(8,128)(2,1)S(1)} all-to-all(bf16[16,256,128]{2,1,0:T(8,128)(2,1)S(1)} %shard_map.82), channel_id=1, replica_groups={{0,2,4,6,8,10,12,14,16,18,20,22,24,26,28,30},{1,3,5,7,9,11,13,15,17,19,..., dimensions={0} | all-to-all | bytes 2097152 | tf_op jit(solution)/shard_map/all_to_all | solution.py:178
  25.8 1.9 %collective-permute-start = (bf16[16,256,128]{2,1,0:T(8,128)(2,1)S(1)}, bf16[16,256,128]{2,1,0:T(8,128)(2,1)S(1)}, u32[]{:S(2)}, u32[]{:S(2)}) collective-permute-start(bf16[16,256,128]{2,1,0:T(8,128)(2,1)S(1)} %all_to_all.15.rows_ref), channel_id=1, source_target_pairs={{0,1},{1,0},{2,3},{3,2},{4,5},{5,4},{6,7},{7,6},{8,9},{9,8},{10,11... | collective-permute-start | bytes 3145736 | tf_op jit(solution)/shard_map/ppermute | solution.py:182
  27.9 3.9 %collective-permute-start.1 = (bf16[4,128,128]{2,1,0:T(8,128)(2,1)S(1)}, bf16[4,128,128]{2,1,0:T(8,128)(2,1)S(1)}, u32[]{:S(2)}, u32[]{:S(2)}) collective-permute-start(bf16[4,128,128]{2,1,0:T(8,128)(2,1)S(1)} %shard_map.85), channel_id=1, source_target_pairs={{0,0},{1,160},{2,64},{3,224},{4,128},{5,32},{6,192},{7,96},{8,8},{... | collective-permute-start | bytes 393224 | tf_op jit(solution)/shard_map/ppermute | solution.py:195
  31.8 2.6 %shard_map.83.acc_ref = f32[4,192,128]{2,1,0:T(8,128)S(1)} custom-call(s32[1]{0:T(128)} %bitcast.1.c_ref, bf16[16,256,128]{2,1,0:T(8,128)(2,1)S(1)} %all_to_all.15.rows_ref, bf16[192,4096]{1,0:T(8,128)(2,1)} %g_hbm.3, bf16[192,4096]{1,0:T(8,128)(2,1)} %u_hbm.3, bf16[192,4096]{1,0:T(8,128)(2,1)} %p_hbm.3, bf16[192,4096]{1,0:T(8,128)(2,1)} %d_hbm.3), custom_call_target="tpu_custom_call" | custom-call | flops 402653184 | bytes 4194304 | tf_op jit(solution)/shard_map/pallas_call | solution.py:199
  34.4 0.0 collective-permute-done.rows_ref
  34.5 2.6 %shard_map.84.tan_ref = bf16[192,128]{1,0:T(8,128)(2,1)S(1)} custom-call(s32[1]{0:T(128)} %bitcast.1.c_ref, bf16[16,256,128]{2,1,0:T(8,128)(2,1)S(1)} %collective-permute-done.rows_ref, bf16[192,4096]{1,0:T(8,128)(2,1)} %g_hbm.3, bf16[192,4096]{1,0:T(8,128)(2,1)} %u_hbm.3, bf16[192,4096]{1,0:T(8,128)(2,1)} %p_hbm.3, bf16[192,4096]{1,0:T(8,128)(2,1)} %d_hbm.3, ...), custom_call_target="tpu_custom_call" | custom-call | flops 402653184 | bytes 4194304 | tf_op jit(solution)/shard_map/pallas_call | solution.py:207
  37.1 0.0 collective-permute-done.1.moved_ref
  37.1 0.8 shard_map.86
  37.9 17.6 %all-to-all-start.1 = ((bf16[8,192,128]{2,1,0:T(8,128)(2,1)}), bf16[8,192,128]{2,1,0:T(8,128)(2,1)S(1)}, u32[]{:S(2)}, u32[]{:S(2)}) async-start(bf16[8,192,128]{2,1,0:T(8,128)(2,1)} %get-tuple-element.7), calls=%async_computation.1 | async-start | bytes 786432 | tf_op jit(solution)/shard_map/all_to_all | solution.py:232
  55.5 1.9 %collective-permute-start.4 = (bf16[4,128,128]{2,1,0:T(8,128)(2,1)S(1)}, bf16[4,128,128]{2,1,0:T(8,128)(2,1)S(1)}, u32[]{:S(2)}, u32[]{:S(2)}) collective-permute-start(bf16[4,128,128]{2,1,0:T(8,128)(2,1)S(1)} %get-tuple-element.8), channel_id=1, source_target_pairs={{0,6},{1,7},{2,0},{3,1},{4,2},{5,3},{6,4},{7,5},{8,14},{9,15},{10,... | collective-permute-start | bytes 393224 | tf_op jit(solution)/shard_map/ppermute | solution.py:227
  57.5 4.2 %collective-permute-start.3 = (bf16[4,128,128]{2,1,0:T(8,128)(2,1)S(1)}, bf16[4,128,128]{2,1,0:T(8,128)(2,1)S(1)}, u32[]{:S(2)}, u32[]{:S(2)}) collective-permute-start(bf16[4,128,128]{2,1,0:T(8,128)(2,1)S(1)} %get-tuple-element.8), channel_id=1, source_target_pairs={{0,4},{1,5},{2,6},{3,7},{4,0},{5,1},{6,2},{7,3},{8,12},{9,13},{10,... | collective-permute-start | bytes 393224 | tf_op jit(solution)/shard_map/ppermute | solution.py:227
  61.7 1.9 %collective-permute-start.2 = (bf16[4,128,128]{2,1,0:T(8,128)(2,1)S(1)}, bf16[4,128,128]{2,1,0:T(8,128)(2,1)S(1)}, u32[]{:S(2)}, u32[]{:S(2)}) collective-permute-start(bf16[4,128,128]{2,1,0:T(8,128)(2,1)S(1)} %get-tuple-element.8), channel_id=1, source_target_pairs={{0,2},{1,3},{2,4},{3,5},{4,6},{5,7},{6,0},{7,1},{8,10},{9,11},{10,... | collective-permute-start | bytes 393224 | tf_op jit(solution)/shard_map/ppermute | solution.py:227
  63.6 0.0 collective-permute-done.4
  63.6 2.2 %collective-permute-done.3 = bf16[4,128,128]{2,1,0:T(8,128)(2,1)S(1)} collective-permute-done((bf16[4,128,128]{2,1,0:T(8,128)(2,1)S(1)}, bf16[4,128,128]{2,1,0:T(8,128)(2,1)S(1)}, u32[]{:S(2)}, u32[]{:S(2)}) %collective-permute-start.3) | collective-permute-done | bytes 131104 | tf_op jit(solution)/shard_map/ppermute | solution.py:227
  65.8 4.5 %collective-permute-done.2 = bf16[4,128,128]{2,1,0:T(8,128)(2,1)S(1)} collective-permute-done((bf16[4,128,128]{2,1,0:T(8,128)(2,1)S(1)}, bf16[4,128,128]{2,1,0:T(8,128)(2,1)S(1)}, u32[]{:S(2)}, u32[]{:S(2)}) %collective-permute-start.2) | collective-permute-done | bytes 131104 | tf_op jit(solution)/shard_map/ppermute | solution.py:227
  70.4 0.1 pad_maximum_fusion.own_ref
  70.4 1.9 %collective-permute-start.5 = (bf16[4,4,128,128]{3,2,1,0:T(8,128)(2,1)S(1)}, bf16[4,4,128,128]{3,2,1,0:T(8,128)(2,1)S(1)}, u32[]{:S(2)}, u32[]{:S(2)}) collective-permute-start(bf16[4,4,128,128]{3,2,1,0:T(8,128)(2,1)S(1)} %pad_maximum_fusion.own_ref), channel_id=1, source_target_pairs={{0,1},{1,0},{2,3},{3,2},{4,5},{5,4},{6,7},{7,6},{8,9},{9,8},{10,11... | collective-permute-start | bytes 1572872 | tf_op jit(solution)/shard_map/ppermute | solution.py:229
  72.4 0.1 pad_add_fusion.at_ref
  72.5 1.8 %collective-permute-done.5.oth_ref = bf16[4,4,128,128]{3,2,1,0:T(8,128)(2,1)S(1)} collective-permute-done((bf16[4,4,128,128]{3,2,1,0:T(8,128)(2,1)S(1)}, bf16[4,4,128,128]{3,2,1,0:T(8,128)(2,1)S(1)}, u32[]{:S(2)}, u32[]{:S(2)}) %collective-permute-start.5) | collective-permute-done | bytes 524320 | tf_op jit(solution)/shard_map/ppermute | solution.py:229
  74.2 2.3 %all-to-all-done.1.tan_ref = bf16[8,192,128]{2,1,0:T(8,128)(2,1)S(1)} async-done(((bf16[8,192,128]{2,1,0:T(8,128)(2,1)}), bf16[8,192,128]{2,1,0:T(8,128)(2,1)S(1)}, u32[]{:S(2)}, u32[]{:S(2)}) %all-to-all-start.1) | async-done | bytes 393248 | tf_op jit(solution)/shard_map/all_to_all | solution.py:232
  76.6 1.1 shard_map.87
  77.7 57.5 %all_to_all.16 = bf16[4,192,128]{2,1,0:T(8,128)(2,1)S(1)} all-to-all(bf16[4,192,128]{2,1,0:T(8,128)(2,1)S(1)} %shard_map.87), channel_id=1, replica_groups={{0,256,512,768},{32,288,544,800},{64,320,576,832},{96,352,608,864},{128..., dimensions={0} | all-to-all | bytes 393216 | tf_op jit(solution)/shard_map/all_to_all | solution.py:244
  135.1 0.7 reduce_sum.12
  (1 shorter events, 0.0 us)
Async XLA Ops:
  25.8 8.6 %collective-permute-start = (bf16[16,256,128]{2,1,0:T(8,128)(2,1)S(1)}, bf16[16,256,128]{2,1,0:T(8,128)(2,1)S(1)}, u32[]{:S(2)}, u32[]{:S(2)}) collective-permute-start(bf16[16,256,128]{2,1,0:T(8,128)(2,1)S(1)} %all_to_all.15.rows_ref), channel_id=1, source_target_pairs={{0,1},{1,0},{2,3},{3,2},{4,5},{5,4},{6,7},{7,6},{8,9},{9,8},{10,11... | collective-permute-start | bytes 3145736 | tf_op jit(solution)/shard_map/ppermute | solution.py:182
  27.9 9.2 %collective-permute-start.1 = (bf16[4,128,128]{2,1,0:T(8,128)(2,1)S(1)}, bf16[4,128,128]{2,1,0:T(8,128)(2,1)S(1)}, u32[]{:S(2)}, u32[]{:S(2)}) collective-permute-start(bf16[4,128,128]{2,1,0:T(8,128)(2,1)S(1)} %shard_map.85), channel_id=1, source_target_pairs={{0,0},{1,160},{2,64},{3,224},{4,128},{5,32},{6,192},{7,96},{8,8},{... | collective-permute-start | bytes 393224 | tf_op jit(solution)/shard_map/ppermute | solution.py:195
  37.9 38.7 %all-to-all-start.1 = ((bf16[8,192,128]{2,1,0:T(8,128)(2,1)}), bf16[8,192,128]{2,1,0:T(8,128)(2,1)S(1)}, u32[]{:S(2)}, u32[]{:S(2)}) async-start(bf16[8,192,128]{2,1,0:T(8,128)(2,1)} %get-tuple-element.7), calls=%async_computation.1 | async-start | bytes 786432 | tf_op jit(solution)/shard_map/all_to_all | solution.py:232
  55.5 8.0 %collective-permute-start.4 = (bf16[4,128,128]{2,1,0:T(8,128)(2,1)S(1)}, bf16[4,128,128]{2,1,0:T(8,128)(2,1)S(1)}, u32[]{:S(2)}, u32[]{:S(2)}) collective-permute-start(bf16[4,128,128]{2,1,0:T(8,128)(2,1)S(1)} %get-tuple-element.8), channel_id=1, source_target_pairs={{0,6},{1,7},{2,0},{3,1},{4,2},{5,3},{6,4},{7,5},{8,14},{9,15},{10,... | collective-permute-start | bytes 393224 | tf_op jit(solution)/shard_map/ppermute | solution.py:227
  57.5 8.4 %collective-permute-start.3 = (bf16[4,128,128]{2,1,0:T(8,128)(2,1)S(1)}, bf16[4,128,128]{2,1,0:T(8,128)(2,1)S(1)}, u32[]{:S(2)}, u32[]{:S(2)}) collective-permute-start(bf16[4,128,128]{2,1,0:T(8,128)(2,1)S(1)} %get-tuple-element.8), channel_id=1, source_target_pairs={{0,4},{1,5},{2,6},{3,7},{4,0},{5,1},{6,2},{7,3},{8,12},{9,13},{10,... | collective-permute-start | bytes 393224 | tf_op jit(solution)/shard_map/ppermute | solution.py:227
  61.7 8.7 %collective-permute-start.2 = (bf16[4,128,128]{2,1,0:T(8,128)(2,1)S(1)}, bf16[4,128,128]{2,1,0:T(8,128)(2,1)S(1)}, u32[]{:S(2)}, u32[]{:S(2)}) collective-permute-start(bf16[4,128,128]{2,1,0:T(8,128)(2,1)S(1)} %get-tuple-element.8), channel_id=1, source_target_pairs={{0,2},{1,3},{2,4},{3,5},{4,6},{5,7},{6,0},{7,1},{8,10},{9,11},{10,... | collective-permute-start | bytes 393224 | tf_op jit(solution)/shard_map/ppermute | solution.py:227
  70.4 3.8 %collective-permute-start.5 = (bf16[4,4,128,128]{3,2,1,0:T(8,128)(2,1)S(1)}, bf16[4,4,128,128]{3,2,1,0:T(8,128)(2,1)S(1)}, u32[]{:S(2)}, u32[]{:S(2)}) collective-permute-start(bf16[4,4,128,128]{3,2,1,0:T(8,128)(2,1)S(1)} %pad_maximum_fusion.own_ref), channel_id=1, source_target_pairs={{0,1},{1,0},{2,3},{3,2},{4,5},{5,4},{6,7},{7,6},{8,9},{9,8},{10,11... | collective-permute-start | bytes 1572872 | tf_op jit(solution)/shard_map/ppermute | solution.py:229

commit v6 on v5

--- a/solution.py
+++ b/solution.py
@@ -10,6 +10,7 @@
 ZN, ZLO, ZHI = 32, 8, 4
 F32, BF16 = jnp.float32, jnp.bfloat16
 DPX = ("dp", "expert")
+PAIRS = ((0, 2), (2, 3), (0, 3), (1, 2), (1, 3), (0, 1))
 SMEM = pl.BlockSpec(memory_space=pltpu.SMEM)
 VMEM = pl.BlockSpec(memory_space=pltpu.VMEM)
 HBM = pl.BlockSpec(memory_space=pltpu.HBM)
@@ -114,9 +115,9 @@
     mine_ref[...] = moved_ref[...]
 
 
-def outer_kernel(at_ref, tan_ref, own_ref, oth_ref, out_ref):
-    x, c = at_ref[0], at_ref[1]
-    for dest in range(ZHI):
+def outer_kernel(at_ref, tan_ref, own_ref, oth_ref, *out_refs):
+    x, c, zhi = at_ref[0], at_ref[1], at_ref[2]
+    for dest, out_ref in zip((zhi, *others(zhi)), out_refs, strict=True):
         acc = None
         for dx in range(WIN):
             chip = (x - dx + WIN) % WIN
@@ -128,7 +129,12 @@
                 lhs, rhs, (((1,), (1,)), ((), ())), preferred_element_type=F32
             )
             acc = part if acc is None else acc + part
-        out_ref[dest] = acc.astype(out_ref.dtype)
+        out_ref[...] = acc.astype(out_ref.dtype)
+
+
+def others(zhi):
+    low = zhi % 2
+    return zhi + 1 - 2 * low, (zhi + 2) % ZHI, 3 - zhi
 
 
 def call(kernel, out_shape, specs, flops, nbytes, scratch=(), **more):
@@ -157,7 +163,7 @@
     z, h = lax.axis_index("dp"), lax.axis_index("expert")
     x, c = (h // 2) % WIN, h % 2
     hid, feats = gate_proj.shape[0], tokens.shape[1]
-    at = jnp.stack([x, c, (x + z % ZLO // 2 + z % 2 + 2 * c) % WIN]).astype(jnp.int32)
+    at = jnp.stack([x, c, z // ZLO, (x + z % ZLO // 2 + z % 2 + 2 * c) % WIN]).astype(jnp.int32)
     rows, cols = tokens.shape[0], gate_proj.shape[1]
 
     send = call(
@@ -183,7 +189,7 @@
 
     picked = call(
         pick_kernel, sds((WIN, feats, CAP), BF16), [SMEM, VMEM], 0, 1 << 18
-    )(at[2:], own)
+    )(at[3:], own)
     perm = [
         (
             i * 32 + k,
@@ -233,18 +239,18 @@
         tangent, "dp", split_axis=0, concat_axis=0, tiled=True, axis_index_groups=near
     )
 
-    partial = call(
+    here, *away = call(
         outer_kernel,
-        sds((ZHI, hid, feats), BF16),
+        [sds((hid, feats), F32)] + [sds((hid, feats), BF16)] * 3,
         [SMEM] + [VMEM] * 3,
         2 * ZHI * hid * 1024 * CAP,
         2 << 20,
-    )(at[:2], tangents, own_t, oth_t)
-    far = [[8 * a + b for a in range(4)] for b in range(8)]
-    parts = lax.all_to_all(
-        partial, "dp", split_axis=0, concat_axis=0, tiled=True, axis_index_groups=far
-    )
-    return jnp.sum(parts.astype(F32), axis=0).astype(BF16)
+    )(at[:3], tangents, own_t, oth_t)
+    total = here
+    for a, b in PAIRS:
+        perm = [(8 * s + i, 8 * d + i) for s, d in ((a, b), (b, a)) for i in range(ZLO)]
+        total = total + lax.ppermute(away[(a ^ b) - 1], "dp", perm).astype(F32)
+    return total.astype(BF16)
 
 
 def solution(mesh):

time: 136 us -> 136 us (level)
  the two profiles are of different devices: /device:TPU:32 before, /device:TPU:2 now
where the time goes in v6:
time: 136 us
  starting transfers between devices  70 us (51%)
  waiting for transfers between devices  28.4 us (21%)
  blocking collectives  27.3 us (20%)
  Pallas kernels  9.03 us (7%)
    ppermute x6, starting transfers between devices, on_device(): total = total + lax.ppermute(away[(a ^ b) - 1], 'dp', perm).astype(F32)  44.4 us
    all_to_all x1, blocking collectives, on_device(): lax.all_to_all(send, 'expert', split_axis=0, concat_axis=0, tiled=True, a...  27.3 us
    ppermute x6, waiting for transfers between devices, on_device(): total = total + lax.ppermute(away[(a ^ b) - 1], 'dp', perm).astype(F32)  10.9 us
    all_to_all x1, starting transfers between devices, on_device(): lax.all_to_all(tangent, 'dp', split_axis=0, concat_axis=0, tiled=True, ax...  10.8 us
    ppermute x3, starting transfers between devices, on_device(): ring.append(lax.ppermute(mine, 'expert', perm))  8.99 us
    ppermute x3, waiting for transfers between devices, on_device(): ring.append(lax.ppermute(mine, 'expert', perm))  5.86 us
    all_to_all x1, waiting for transfers between devices, on_device(): lax.all_to_all(tangent, 'dp', split_axis=0, concat_axis=0, tiled=True, ax...  5.69 us
    ppermute x1, waiting for transfers between devices, on_device(): moved = lax.ppermute(picked, DPX, perm)  4.12 us
  transfers between devices with their start and end apart: 13, of which 6 were waited for; matrix products, arithmetic and copies ran while one was open for 0% of the time, Pallas kernels for 4%

profile of v6, /device:TPU:2, one launch (start us, length us, event | category | flops | bytes accessed | tf_op | source)
XLA Modules:
  0.0 135.8 jit_solution(11218288526238180624)
XLA Ops:
  0.0 1.9 %shard_map.82 = bf16[16,256,128]{2,1,0:T(8,128)(2,1)S(1)} custom-call(s32[8,1024]{1,0:T(8,128)} %bitcast.14, f32[8,1024]{1,0:T(8,128)} %bitcast.15, bf16[1024,128]{1,0:T(8,128)(2,1)} %tok_hbm.1, bf16[1024,128]{1,0:T(8,128)(2,1)} %cot_hbm.1), custom_call_target="tpu_custom_call" | custom-call | flops 268435456 | bytes 2097152 | tf_op jit(solution)/shard_map/pallas_call | solution.py:169
  1.9 27.3 %all_to_all.10.rows_ref = bf16[16,256,128]{2,1,0:T(8,128)(2,1)S(1)} all-to-all(bf16[16,256,128]{2,1,0:T(8,128)(2,1)S(1)} %shard_map.82), channel_id=1, replica_groups={{0,2,4,6,8,10,12,14,16,18,20,22,24,26,28,30},{1,3,5,7,9,11,13,15,17,19,..., dimensions={0} | all-to-all | bytes 2097152 | tf_op jit(solution)/shard_map/all_to_all | solution.py:184
  29.2 1.9 %collective-permute-start = (bf16[16,256,128]{2,1,0:T(8,128)(2,1)S(1)}, bf16[16,256,128]{2,1,0:T(8,128)(2,1)S(1)}, u32[]{:S(2)}, u32[]{:S(2)}) collective-permute-start(bf16[16,256,128]{2,1,0:T(8,128)(2,1)S(1)} %all_to_all.10.rows_ref), channel_id=1, source_target_pairs={{0,1},{1,0},{2,3},{3,2},{4,5},{5,4},{6,7},{7,6},{8,9},{9,8},{10,11... | collective-permute-start | bytes 3145736 | tf_op jit(solution)/shard_map/ppermute | solution.py:188
  31.2 1.9 %collective-permute-start.1 = (bf16[4,128,128]{2,1,0:T(8,128)(2,1)S(1)}, bf16[4,128,128]{2,1,0:T(8,128)(2,1)S(1)}, u32[]{:S(2)}, u32[]{:S(2)}) collective-permute-start(bf16[4,128,128]{2,1,0:T(8,128)(2,1)S(1)} %shard_map.85), channel_id=1, source_target_pairs={{0,0},{1,160},{2,64},{3,224},{4,128},{5,32},{6,192},{7,96},{8,8},{... | collective-permute-start | bytes 393224 | tf_op jit(solution)/shard_map/ppermute | solution.py:201
  33.2 2.6 %shard_map.83.acc_ref = f32[4,192,128]{2,1,0:T(8,128)S(1)} custom-call(s32[1]{0:T(128)} %bitcast.1.c_ref, bf16[16,256,128]{2,1,0:T(8,128)(2,1)S(1)} %all_to_all.10.rows_ref, bf16[192,4096]{1,0:T(8,128)(2,1)} %g_hbm.3, bf16[192,4096]{1,0:T(8,128)(2,1)} %u_hbm.3, bf16[192,4096]{1,0:T(8,128)(2,1)} %p_hbm.3, bf16[192,4096]{1,0:T(8,128)(2,1)} %d_hbm.3), custom_call_target="tpu_custom_call" | custom-call | flops 402653184 | bytes 4194304 | tf_op jit(solution)/shard_map/pallas_call | solution.py:205
  35.8 0.0 collective-permute-done.rows_ref
  35.8 2.6 %shard_map.84.tan_ref = bf16[192,128]{1,0:T(8,128)(2,1)S(1)} custom-call(s32[1]{0:T(128)} %bitcast.1.c_ref, bf16[16,256,128]{2,1,0:T(8,128)(2,1)S(1)} %collective-permute-done.rows_ref, bf16[192,4096]{1,0:T(8,128)(2,1)} %g_hbm.3, bf16[192,4096]{1,0:T(8,128)(2,1)} %u_hbm.3, bf16[192,4096]{1,0:T(8,128)(2,1)} %p_hbm.3, bf16[192,4096]{1,0:T(8,128)(2,1)} %d_hbm.3, ...), custom_call_target="tpu_custom_call" | custom-call | flops 402653184 | bytes 4194304 | tf_op jit(solution)/shard_map/pallas_call | solution.py:213
  38.4 4.1 %collective-permute-done.1.moved_ref = bf16[4,128,128]{2,1,0:T(8,128)(2,1)S(1)} collective-permute-done((bf16[4,128,128]{2,1,0:T(8,128)(2,1)S(1)}, bf16[4,128,128]{2,1,0:T(8,128)(2,1)S(1)}, u32[]{:S(2)}, u32[]{:S(2)}) %collective-permute-start.1) | collective-permute-done | bytes 131104 | tf_op jit(solution)/shard_map/ppermute | solution.py:201
  42.5 0.8 shard_map.86
  43.4 10.8 %all-to-all-start.1 = ((bf16[8,192,128]{2,1,0:T(8,128)(2,1)}), bf16[8,192,128]{2,1,0:T(8,128)(2,1)S(1)}, u32[]{:S(2)}, u32[]{:S(2)}) async-start(bf16[8,192,128]{2,1,0:T(8,128)(2,1)} %get-tuple-element.11), calls=%async_computation.1 | async-start | bytes 786432 | tf_op jit(solution)/shard_map/all_to_all | solution.py:238
  54.2 3.7 %collective-permute-start.4 = (bf16[4,128,128]{2,1,0:T(8,128)(2,1)S(1)}, bf16[4,128,128]{2,1,0:T(8,128)(2,1)S(1)}, u32[]{:S(2)}, u32[]{:S(2)}) collective-permute-start(bf16[4,128,128]{2,1,0:T(8,128)(2,1)S(1)} %get-tuple-element.12), channel_id=1, source_target_pairs={{0,6},{1,7},{2,0},{3,1},{4,2},{5,3},{6,4},{7,5},{8,14},{9,15},{10,... | collective-permute-start | bytes 393224 | tf_op jit(solution)/shard_map/ppermute | solution.py:233
  57.9 1.9 %collective-permute-start.3 = (bf16[4,128,128]{2,1,0:T(8,128)(2,1)S(1)}, bf16[4,128,128]{2,1,0:T(8,128)(2,1)S(1)}, u32[]{:S(2)}, u32[]{:S(2)}) collective-permute-start(bf16[4,128,128]{2,1,0:T(8,128)(2,1)S(1)} %get-tuple-element.12), channel_id=1, source_target_pairs={{0,4},{1,5},{2,6},{3,7},{4,0},{5,1},{6,2},{7,3},{8,12},{9,13},{10,... | collective-permute-start | bytes 393224 | tf_op jit(solution)/shard_map/ppermute | solution.py:233
  59.8 3.4 %collective-permute-start.2 = (bf16[4,128,128]{2,1,0:T(8,128)(2,1)S(1)}, bf16[4,128,128]{2,1,0:T(8,128)(2,1)S(1)}, u32[]{:S(2)}, u32[]{:S(2)}) collective-permute-start(bf16[4,128,128]{2,1,0:T(8,128)(2,1)S(1)} %get-tuple-element.12), channel_id=1, source_target_pairs={{0,2},{1,3},{2,4},{3,5},{4,6},{5,7},{6,0},{7,1},{8,10},{9,11},{10,... | collective-permute-start | bytes 393224 | tf_op jit(solution)/shard_map/ppermute | solution.py:233
  63.2 0.0 collective-permute-done.4
  63.2 3.0 %collective-permute-done.3 = bf16[4,128,128]{2,1,0:T(8,128)(2,1)S(1)} collective-permute-done((bf16[4,128,128]{2,1,0:T(8,128)(2,1)S(1)}, bf16[4,128,128]{2,1,0:T(8,128)(2,1)S(1)}, u32[]{:S(2)}, u32[]{:S(2)}) %collective-permute-start.3) | collective-permute-done | bytes 131104 | tf_op jit(solution)/shard_map/ppermute | solution.py:233
  66.2 2.8 %collective-permute-done.2 = bf16[4,128,128]{2,1,0:T(8,128)(2,1)S(1)} collective-permute-done((bf16[4,128,128]{2,1,0:T(8,128)(2,1)S(1)}, bf16[4,128,128]{2,1,0:T(8,128)(2,1)S(1)}, u32[]{:S(2)}, u32[]{:S(2)}) %collective-permute-start.2) | collective-permute-done | bytes 131104 | tf_op jit(solution)/shard_map/ppermute | solution.py:233
  69.1 0.1 pad_maximum_fusion.own_ref
  69.1 1.9 %collective-permute-start.5 = (bf16[4,4,128,128]{3,2,1,0:T(8,128)(2,1)S(1)}, bf16[4,4,128,128]{3,2,1,0:T(8,128)(2,1)S(1)}, u32[]{:S(2)}, u32[]{:S(2)}) collective-permute-start(bf16[4,4,128,128]{3,2,1,0:T(8,128)(2,1)S(1)} %pad_maximum_fusion.own_ref), channel_id=1, source_target_pairs={{0,1},{1,0},{2,3},{3,2},{4,5},{5,4},{6,7},{7,6},{8,9},{9,8},{10,11... | collective-permute-start | bytes 1572872 | tf_op jit(solution)/shard_map/ppermute | solution.py:235
  71.1 0.1 pad_add_fusion.at_ref
  71.1 1.8 %collective-permute-done.5.oth_ref = bf16[4,4,128,128]{3,2,1,0:T(8,128)(2,1)S(1)} collective-permute-done((bf16[4,4,128,128]{3,2,1,0:T(8,128)(2,1)S(1)}, bf16[4,4,128,128]{3,2,1,0:T(8,128)(2,1)S(1)}, u32[]{:S(2)}, u32[]{:S(2)}) %collective-permute-start.5) | collective-permute-done | bytes 524320 | tf_op jit(solution)/shard_map/ppermute | solution.py:235
  72.9 5.7 %all-to-all-done.1.tan_ref = bf16[8,192,128]{2,1,0:T(8,128)(2,1)S(1)} async-done(((bf16[8,192,128]{2,1,0:T(8,128)(2,1)}), bf16[8,192,128]{2,1,0:T(8,128)(2,1)S(1)}, u32[]{:S(2)}, u32[]{:S(2)}) %all-to-all-start.1) | async-done | bytes 393248 | tf_op jit(solution)/shard_map/all_to_all | solution.py:238
  78.6 1.1 shard_map.87
  79.7 15.7 %collective-permute-start.11 = (bf16[192,128]{1,0:T(8,128)(2,1)S(1)}, bf16[192,128]{1,0:T(8,128)(2,1)S(1)}, u32[]{:S(2)}, u32[]{:S(2)}) collective-permute-start(bf16[192,128]{1,0:T(8,128)(2,1)S(1)} %get-tuple-element.15), channel_id=1, source_target_pairs={{0,256},{32,288},{64,320},{96,352},{128,384},{160,416},{192,448},{... | collective-permute-start | bytes 147464 | tf_op jit(solution)/shard_map/ppermute | solution.py:252
  95.5 0.7 collective-permute-start.10
  96.1 0.7 collective-permute-start.9
  96.8 13.3 %collective-permute-start.8 = (bf16[192,128]{1,0:T(8,128)(2,1)S(1)}, bf16[192,128]{1,0:T(8,128)(2,1)S(1)}, u32[]{:S(2)}, u32[]{:S(2)}) collective-permute-start(bf16[192,128]{1,0:T(8,128)(2,1)S(1)} %get-tuple-element.16), channel_id=1, source_target_pairs={{0,768},{32,800},{64,832},{96,864},{128,896},{160,928},{192,960},{... | collective-permute-start | bytes 147464 | tf_op jit(solution)/shard_map/ppermute | solution.py:252
  110.2 0.7 collective-permute-start.7
  110.8 0.0 collective-permute-done.11
  110.9 13.3 %collective-permute-start.6 = (bf16[192,128]{1,0:T(8,128)(2,1)S(1)}, bf16[192,128]{1,0:T(8,128)(2,1)S(1)}, u32[]{:S(2)}, u32[]{:S(2)}) collective-permute-start(bf16[192,128]{1,0:T(8,128)(2,1)S(1)} %get-tuple-element.14), channel_id=1, source_target_pairs={{0,512},{32,544},{64,576},{96,608},{128,640},{160,672},{192,704},{... | collective-permute-start | bytes 147464 | tf_op jit(solution)/shard_map/ppermute | solution.py:252
  124.2 0.0 collective-permute-done.10
  124.2 0.0 collective-permute-done.9
  124.2 0.0 collective-permute-done.8
  124.2 0.0 collective-permute-done.7
  124.2 10.9 %collective-permute-done.6 = bf16[192,128]{1,0:T(8,128)(2,1)S(1)} collective-permute-done((bf16[192,128]{1,0:T(8,128)(2,1)S(1)}, bf16[192,128]{1,0:T(8,128)(2,1)S(1)}, u32[]{:S(2)}, u32[]{:S(2)}) %collective-permute-start.6) | collective-permute-done | bytes 49184 | tf_op jit(solution)/shard_map/ppermute | solution.py:252
  135.2 0.7 add_convert_fusion
  (1 shorter events, 0.0 us)
Async XLA Ops:
  29.2 6.6 %collective-permute-start = (bf16[16,256,128]{2,1,0:T(8,128)(2,1)S(1)}, bf16[16,256,128]{2,1,0:T(8,128)(2,1)S(1)}, u32[]{:S(2)}, u32[]{:S(2)}) collective-permute-start(bf16[16,256,128]{2,1,0:T(8,128)(2,1)S(1)} %all_to_all.10.rows_ref), channel_id=1, source_target_pairs={{0,1},{1,0},{2,3},{3,2},{4,5},{5,4},{6,7},{7,6},{8,9},{9,8},{10,11... | collective-permute-start | bytes 3145736 | tf_op jit(solution)/shard_map/ppermute | solution.py:188
  31.2 11.3 %collective-permute-start.1 = (bf16[4,128,128]{2,1,0:T(8,128)(2,1)S(1)}, bf16[4,128,128]{2,1,0:T(8,128)(2,1)S(1)}, u32[]{:S(2)}, u32[]{:S(2)}) collective-permute-start(bf16[4,128,128]{2,1,0:T(8,128)(2,1)S(1)} %shard_map.85), channel_id=1, source_target_pairs={{0,0},{1,160},{2,64},{3,224},{4,128},{5,32},{6,192},{7,96},{8,8},{... | collective-permute-start | bytes 393224 | tf_op jit(solution)/shard_map/ppermute | solution.py:201
  43.4 35.3 %all-to-all-start.1 = ((bf16[8,192,128]{2,1,0:T(8,128)(2,1)}), bf16[8,192,128]{2,1,0:T(8,128)(2,1)S(1)}, u32[]{:S(2)}, u32[]{:S(2)}) async-start(bf16[8,192,128]{2,1,0:T(8,128)(2,1)} %get-tuple-element.11), calls=%async_computation.1 | async-start | bytes 786432 | tf_op jit(solution)/shard_map/all_to_all | solution.py:238
  54.2 9.0 %collective-permute-start.4 = (bf16[4,128,128]{2,1,0:T(8,128)(2,1)S(1)}, bf16[4,128,128]{2,1,0:T(8,128)(2,1)S(1)}, u32[]{:S(2)}, u32[]{:S(2)}) collective-permute-start(bf16[4,128,128]{2,1,0:T(8,128)(2,1)S(1)} %get-tuple-element.12), channel_id=1, source_target_pairs={{0,6},{1,7},{2,0},{3,1},{4,2},{5,3},{6,4},{7,5},{8,14},{9,15},{10,... | collective-permute-start | bytes 393224 | tf_op jit(solution)/shard_map/ppermute | solution.py:233
  57.9 8.4 %collective-permute-start.3 = (bf16[4,128,128]{2,1,0:T(8,128)(2,1)S(1)}, bf16[4,128,128]{2,1,0:T(8,128)(2,1)S(1)}, u32[]{:S(2)}, u32[]{:S(2)}) collective-permute-start(bf16[4,128,128]{2,1,0:T(8,128)(2,1)S(1)} %get-tuple-element.12), channel_id=1, source_target_pairs={{0,4},{1,5},{2,6},{3,7},{4,0},{5,1},{6,2},{7,3},{8,12},{9,13},{10,... | collective-permute-start | bytes 393224 | tf_op jit(solution)/shard_map/ppermute | solution.py:233
  59.8 9.2 %collective-permute-start.2 = (bf16[4,128,128]{2,1,0:T(8,128)(2,1)S(1)}, bf16[4,128,128]{2,1,0:T(8,128)(2,1)S(1)}, u32[]{:S(2)}, u32[]{:S(2)}) collective-permute-start(bf16[4,128,128]{2,1,0:T(8,128)(2,1)S(1)} %get-tuple-element.12), channel_id=1, source_target_pairs={{0,2},{1,3},{2,4},{3,5},{4,6},{5,7},{6,0},{7,1},{8,10},{9,11},{10,... | collective-permute-start | bytes 393224 | tf_op jit(solution)/shard_map/ppermute | solution.py:233
  69.1 3.8 %collective-permute-start.5 = (bf16[4,4,128,128]{3,2,1,0:T(8,128)(2,1)S(1)}, bf16[4,4,128,128]{3,2,1,0:T(8,128)(2,1)S(1)}, u32[]{:S(2)}, u32[]{:S(2)}) collective-permute-start(bf16[4,4,128,128]{3,2,1,0:T(8,128)(2,1)S(1)} %pad_maximum_fusion.own_ref), channel_id=1, source_target_pairs={{0,1},{1,0},{2,3},{3,2},{4,5},{5,4},{6,7},{7,6},{8,9},{9,8},{10,11... | collective-permute-start | bytes 1572872 | tf_op jit(solution)/shard_map/ppermute | solution.py:235
  79.7 31.1 %collective-permute-start.11 = (bf16[192,128]{1,0:T(8,128)(2,1)S(1)}, bf16[192,128]{1,0:T(8,128)(2,1)S(1)}, u32[]{:S(2)}, u32[]{:S(2)}) collective-permute-start(bf16[192,128]{1,0:T(8,128)(2,1)S(1)} %get-tuple-element.15), channel_id=1, source_target_pairs={{0,256},{32,288},{64,320},{96,352},{128,384},{160,416},{192,448},{... | collective-permute-start | bytes 147464 | tf_op jit(solution)/shard_map/ppermute | solution.py:252
  95.5 28.7 %collective-permute-start.10 = (bf16[192,128]{1,0:T(8,128)(2,1)S(1)}, bf16[192,128]{1,0:T(8,128)(2,1)S(1)}, u32[]{:S(2)}, u32[]{:S(2)}) collective-permute-start(bf16[192,128]{1,0:T(8,128)(2,1)S(1)} %get-tuple-element.14), channel_id=1, source_target_pairs={{256,768},{288,800},{320,832},{352,864},{384,896},{416,928},{448,9... | collective-permute-start | bytes 147464 | tf_op jit(solution)/shard_map/ppermute | solution.py:252
  96.1 28.1 %collective-permute-start.9 = (bf16[192,128]{1,0:T(8,128)(2,1)S(1)}, bf16[192,128]{1,0:T(8,128)(2,1)S(1)}, u32[]{:S(2)}, u32[]{:S(2)}) collective-permute-start(bf16[192,128]{1,0:T(8,128)(2,1)S(1)} %get-tuple-element.16), channel_id=1, source_target_pairs={{256,512},{288,544},{320,576},{352,608},{384,640},{416,672},{448,7... | collective-permute-start | bytes 147464 | tf_op jit(solution)/shard_map/ppermute | solution.py:252
  96.8 27.4 %collective-permute-start.8 = (bf16[192,128]{1,0:T(8,128)(2,1)S(1)}, bf16[192,128]{1,0:T(8,128)(2,1)S(1)}, u32[]{:S(2)}, u32[]{:S(2)}) collective-permute-start(bf16[192,128]{1,0:T(8,128)(2,1)S(1)} %get-tuple-element.16), channel_id=1, source_target_pairs={{0,768},{32,800},{64,832},{96,864},{128,896},{160,928},{192,960},{... | collective-permute-start | bytes 147464 | tf_op jit(solution)/shard_map/ppermute | solution.py:252
  110.2 14.1 %collective-permute-start.7 = (bf16[192,128]{1,0:T(8,128)(2,1)S(1)}, bf16[192,128]{1,0:T(8,128)(2,1)S(1)}, u32[]{:S(2)}, u32[]{:S(2)}) collective-permute-start(bf16[192,128]{1,0:T(8,128)(2,1)S(1)} %get-tuple-element.15), channel_id=1, source_target_pairs={{512,768},{544,800},{576,832},{608,864},{640,896},{672,928},{704,9... | collective-permute-start | bytes 147464 | tf_op jit(solution)/shard_map/ppermute | solution.py:252
  110.9 24.3 %collective-permute-start.6 = (bf16[192,128]{1,0:T(8,128)(2,1)S(1)}, bf16[192,128]{1,0:T(8,128)(2,1)S(1)}, u32[]{:S(2)}, u32[]{:S(2)}) collective-permute-start(bf16[192,128]{1,0:T(8,128)(2,1)S(1)} %get-tuple-element.14), channel_id=1, source_target_pairs={{0,512},{32,544},{64,576},{96,608},{128,640},{160,672},{192,704},{... | collective-permute-start | bytes 147464 | tf_op jit(solution)/shard_map/ppermute | solution.py:252

commit v7 on v6

--- a/solution.py
+++ b/solution.py
@@ -1,3 +1,5 @@
+import functools
+
 import jax
 import jax.numpy as jnp
 from jax import lax
@@ -10,7 +12,6 @@
 ZN, ZLO, ZHI = 32, 8, 4
 F32, BF16 = jnp.float32, jnp.bfloat16
 DPX = ("dp", "expert")
-PAIRS = ((0, 2), (2, 3), (0, 3), (1, 2), (1, 3), (0, 1))
 SMEM = pl.BlockSpec(memory_space=pltpu.SMEM)
 VMEM = pl.BlockSpec(memory_space=pltpu.VMEM)
 HBM = pl.BlockSpec(memory_space=pltpu.HBM)
@@ -115,9 +116,10 @@
     mine_ref[...] = moved_ref[...]
 
 
-def outer_kernel(at_ref, tan_ref, own_ref, oth_ref, *out_refs):
+def outer_kernel(flips, at_ref, tan_ref, own_ref, oth_ref, out_ref):
     x, c, zhi = at_ref[0], at_ref[1], at_ref[2]
-    for dest, out_ref in zip((zhi, *others(zhi)), out_refs, strict=True):
+    for n, flip in enumerate(flips):
+        dest = flipped(zhi, flip, c)
         acc = None
         for dx in range(WIN):
             chip = (x - dx + WIN) % WIN
@@ -129,12 +131,13 @@
                 lhs, rhs, (((1,), (1,)), ((), ())), preferred_element_type=F32
             )
             acc = part if acc is None else acc + part
-        out_ref[...] = acc.astype(out_ref.dtype)
-
-
-def others(zhi):
-    low = zhi % 2
-    return zhi + 1 - 2 * low, (zhi + 2) % ZHI, 3 - zhi
+        out_ref[n] = acc.astype(out_ref.dtype)
+
+
+def flipped(zhi, flip, core):
+    near, mirror = zhi + 1 - 2 * (zhi % 2), 3 - zhi
+    first = near + core * (mirror - near)
+    return (zhi, first, near + mirror - first, (zhi + 2) % ZHI)[flip]
 
 
 def call(kernel, out_shape, specs, flops, nbytes, scratch=(), **more):
@@ -239,18 +242,27 @@
         tangent, "dp", split_axis=0, concat_axis=0, tiled=True, axis_index_groups=near
     )
 
-    here, *away = call(
-        outer_kernel,
-        [sds((hid, feats), F32)] + [sds((hid, feats), BF16)] * 3,
-        [SMEM] + [VMEM] * 3,
-        2 * ZHI * hid * 1024 * CAP,
-        2 << 20,
-    )(at[:3], tangents, own_t, oth_t)
-    total = here
-    for a, b in PAIRS:
-        perm = [(8 * s + i, 8 * d + i) for s, d in ((a, b), (b, a)) for i in range(ZLO)]
-        total = total + lax.ppermute(away[(a ^ b) - 1], "dp", perm).astype(F32)
-    return total.astype(BF16)
+    def outer(flips, dtype):
+        return call(
+            functools.partial(outer_kernel, flips),
+            sds((len(flips), hid, feats), dtype),
+            [SMEM] + [VMEM] * 3,
+            2 * len(flips) * hid * 1024 * CAP,
+            2 << 20,
+        )(at[:3], tangents, own_t, oth_t)
+
+    def exchange(value, flip):
+        perm = [
+            (i * 32 + k, (flipped(i // ZLO, flip, k % 2) * ZLO + i % ZLO) * 32 + k)
+            for i in range(ZN)
+            for k in range(32)
+        ]
+        return lax.ppermute(value, DPX, perm)
+
+    got = exchange(outer((1, 3), BF16), 1).astype(F32)
+    here, there = outer((0, 2), F32)
+    last = exchange((there + got[1]).astype(BF16), 2).astype(F32)
+    return (here + got[0] + last).astype(BF16)
 
 
 def solution(mesh):

time: 136 us -> 121 us (0.89)
  starting transfers between devices: 70 us -> 47.8 us
  waiting for transfers between devices: 28.4 us -> 35 us
    ppermute x6 -> x2, starting transfers between devices: 44.4 us -> 22.2 us  [exchange(): return lax.ppermute(value, DPX, perm)]
    ppermute x6 -> x2, waiting for transfers between devices: 10.9 us -> 17.6 us  [exchange(): return lax.ppermute(value, DPX, perm)]
  transfers between devices with their start and end apart: 13 -> 9, of which waited for: 6 -> 7; matrix products, arithmetic and copies ran while one was open for 0% -> 0% of each run, Pallas kernels for 4% -> 5%
where the time goes in v7:
time: 121 us
  starting transfers between devices  47.8 us (40%)
  waiting for transfers between devices  35 us (29%)
  blocking collectives  27.3 us (23%)
  Pallas kernels  9.74 us (8%)
    all_to_all x1, blocking collectives, on_device(): lax.all_to_all(send, 'expert', split_axis=0, concat_axis=0, tiled=True, a...  27.3 us
    ppermute x2, starting transfers between devices, exchange(): return lax.ppermute(value, DPX, perm)  22.2 us
    ppermute x2, waiting for transfers between devices, exchange(): return lax.ppermute(value, DPX, perm)  17.6 us
    all_to_all x1, starting transfers between devices, on_device(): lax.all_to_all(tangent, 'dp', split_axis=0, concat_axis=0, tiled=True, ax...  10.8 us
    ppermute x3, starting transfers between devices, on_device(): ring.append(lax.ppermute(mine, 'expert', perm))  8.99 us
    ppermute x3, waiting for transfers between devices, on_device(): ring.append(lax.ppermute(mine, 'expert', perm))  5.86 us
    all_to_all x1, waiting for transfers between devices, on_device(): lax.all_to_all(tangent, 'dp', split_axis=0, concat_axis=0, tiled=True, ax...  5.69 us
    ppermute x1, waiting for transfers between devices, on_device(): moved = lax.ppermute(picked, DPX, perm)  4.12 us
  transfers between devices with their start and end apart: 9, of which 7 were waited for; matrix products, arithmetic and copies ran while one was open for 0% of the time, Pallas kernels for 5%

profile of v7, /device:TPU:2, one launch (start us, length us, event | category | flops | bytes accessed | tf_op | source)
XLA Modules:
  0.0 120.9 jit_solution(4109443207980004985)
XLA Ops:
  0.0 1.9 %shard_map.82 = bf16[16,256,128]{2,1,0:T(8,128)(2,1)S(1)} custom-call(s32[8,1024]{1,0:T(8,128)} %bitcast.22, f32[8,1024]{1,0:T(8,128)} %bitcast.23, bf16[1024,128]{1,0:T(8,128)(2,1)} %tok_hbm.1, bf16[1024,128]{1,0:T(8,128)(2,1)} %cot_hbm.1), custom_call_target="tpu_custom_call" | custom-call | flops 268435456 | bytes 2097152 | tf_op jit(solution)/shard_map/pallas_call | solution.py:172
  1.9 27.3 %all_to_all.10.rows_ref = bf16[16,256,128]{2,1,0:T(8,128)(2,1)S(1)} all-to-all(bf16[16,256,128]{2,1,0:T(8,128)(2,1)S(1)} %shard_map.82), channel_id=1, replica_groups={{0,2,4,6,8,10,12,14,16,18,20,22,24,26,28,30},{1,3,5,7,9,11,13,15,17,19,..., dimensions={0} | all-to-all | bytes 2097152 | tf_op jit(solution)/shard_map/all_to_all | solution.py:187
  29.2 1.9 %collective-permute-start = (bf16[16,256,128]{2,1,0:T(8,128)(2,1)S(1)}, bf16[16,256,128]{2,1,0:T(8,128)(2,1)S(1)}, u32[]{:S(2)}, u32[]{:S(2)}) collective-permute-start(bf16[16,256,128]{2,1,0:T(8,128)(2,1)S(1)} %all_to_all.10.rows_ref), channel_id=1, source_target_pairs={{0,1},{1,0},{2,3},{3,2},{4,5},{5,4},{6,7},{7,6},{8,9},{9,8},{10,11... | collective-permute-start | bytes 3145736 | tf_op jit(solution)/shard_map/ppermute | solution.py:191
  31.2 1.9 %collective-permute-start.1 = (bf16[4,128,128]{2,1,0:T(8,128)(2,1)S(1)}, bf16[4,128,128]{2,1,0:T(8,128)(2,1)S(1)}, u32[]{:S(2)}, u32[]{:S(2)}) collective-permute-start(bf16[4,128,128]{2,1,0:T(8,128)(2,1)S(1)} %shard_map.85), channel_id=1, source_target_pairs={{0,0},{1,160},{2,64},{3,224},{4,128},{5,32},{6,192},{7,96},{8,8},{... | collective-permute-start | bytes 393224 | tf_op jit(solution)/shard_map/ppermute | solution.py:204
  33.2 2.6 %shard_map.83.acc_ref = f32[4,192,128]{2,1,0:T(8,128)S(1)} custom-call(s32[1]{0:T(128)} %bitcast.1.c_ref, bf16[16,256,128]{2,1,0:T(8,128)(2,1)S(1)} %all_to_all.10.rows_ref, bf16[192,4096]{1,0:T(8,128)(2,1)} %g_hbm.3, bf16[192,4096]{1,0:T(8,128)(2,1)} %u_hbm.3, bf16[192,4096]{1,0:T(8,128)(2,1)} %p_hbm.3, bf16[192,4096]{1,0:T(8,128)(2,1)} %d_hbm.3), custom_call_target="tpu_custom_call" | custom-call | flops 402653184 | bytes 4194304 | tf_op jit(solution)/shard_map/pallas_call | solution.py:208
  35.8 0.0 collective-permute-done.rows_ref
  35.8 2.6 %shard_map.84.tan_ref = bf16[192,128]{1,0:T(8,128)(2,1)S(1)} custom-call(s32[1]{0:T(128)} %bitcast.1.c_ref, bf16[16,256,128]{2,1,0:T(8,128)(2,1)S(1)} %collective-permute-done.rows_ref, bf16[192,4096]{1,0:T(8,128)(2,1)} %g_hbm.3, bf16[192,4096]{1,0:T(8,128)(2,1)} %u_hbm.3, bf16[192,4096]{1,0:T(8,128)(2,1)} %p_hbm.3, bf16[192,4096]{1,0:T(8,128)(2,1)} %d_hbm.3, ...), custom_call_target="tpu_custom_call" | custom-call | flops 402653184 | bytes 4194304 | tf_op jit(solution)/shard_map/pallas_call | solution.py:216
  38.4 4.1 %collective-permute-done.1.moved_ref = bf16[4,128,128]{2,1,0:T(8,128)(2,1)S(1)} collective-permute-done((bf16[4,128,128]{2,1,0:T(8,128)(2,1)S(1)}, bf16[4,128,128]{2,1,0:T(8,128)(2,1)S(1)}, u32[]{:S(2)}, u32[]{:S(2)}) %collective-permute-start.1) | collective-permute-done | bytes 131104 | tf_op jit(solution)/shard_map/ppermute | solution.py:204
  42.5 0.8 shard_map.86
  43.4 10.8 %all-to-all-start.1 = ((bf16[8,192,128]{2,1,0:T(8,128)(2,1)}), bf16[8,192,128]{2,1,0:T(8,128)(2,1)S(1)}, u32[]{:S(2)}, u32[]{:S(2)}) async-start(bf16[8,192,128]{2,1,0:T(8,128)(2,1)} %get-tuple-element.7), calls=%async_computation.1 | async-start | bytes 786432 | tf_op jit(solution)/shard_map/all_to_all | solution.py:241
  54.2 3.7 %collective-permute-start.4 = (bf16[4,128,128]{2,1,0:T(8,128)(2,1)S(1)}, bf16[4,128,128]{2,1,0:T(8,128)(2,1)S(1)}, u32[]{:S(2)}, u32[]{:S(2)}) collective-permute-start(bf16[4,128,128]{2,1,0:T(8,128)(2,1)S(1)} %get-tuple-element.8), channel_id=1, source_target_pairs={{0,6},{1,7},{2,0},{3,1},{4,2},{5,3},{6,4},{7,5},{8,14},{9,15},{10,... | collective-permute-start | bytes 393224 | tf_op jit(solution)/shard_map/ppermute | solution.py:236
  57.9 1.9 %collective-permute-start.3 = (bf16[4,128,128]{2,1,0:T(8,128)(2,1)S(1)}, bf16[4,128,128]{2,1,0:T(8,128)(2,1)S(1)}, u32[]{:S(2)}, u32[]{:S(2)}) collective-permute-start(bf16[4,128,128]{2,1,0:T(8,128)(2,1)S(1)} %get-tuple-element.8), channel_id=1, source_target_pairs={{0,4},{1,5},{2,6},{3,7},{4,0},{5,1},{6,2},{7,3},{8,12},{9,13},{10,... | collective-permute-start | bytes 393224 | tf_op jit(solution)/shard_map/ppermute | solution.py:236
  59.8 3.4 %collective-permute-start.2 = (bf16[4,128,128]{2,1,0:T(8,128)(2,1)S(1)}, bf16[4,128,128]{2,1,0:T(8,128)(2,1)S(1)}, u32[]{:S(2)}, u32[]{:S(2)}) collective-permute-start(bf16[4,128,128]{2,1,0:T(8,128)(2,1)S(1)} %get-tuple-element.8), channel_id=1, source_target_pairs={{0,2},{1,3},{2,4},{3,5},{4,6},{5,7},{6,0},{7,1},{8,10},{9,11},{10,... | collective-permute-start | bytes 393224 | tf_op jit(solution)/shard_map/ppermute | solution.py:236
  63.2 0.0 collective-permute-done.4
  63.2 3.0 %collective-permute-done.3 = bf16[4,128,128]{2,1,0:T(8,128)(2,1)S(1)} collective-permute-done((bf16[4,128,128]{2,1,0:T(8,128)(2,1)S(1)}, bf16[4,128,128]{2,1,0:T(8,128)(2,1)S(1)}, u32[]{:S(2)}, u32[]{:S(2)}) %collective-permute-start.3) | collective-permute-done | bytes 131104 | tf_op jit(solution)/shard_map/ppermute | solution.py:236
  66.2 2.8 %collective-permute-done.2 = bf16[4,128,128]{2,1,0:T(8,128)(2,1)S(1)} collective-permute-done((bf16[4,128,128]{2,1,0:T(8,128)(2,1)S(1)}, bf16[4,128,128]{2,1,0:T(8,128)(2,1)S(1)}, u32[]{:S(2)}, u32[]{:S(2)}) %collective-permute-start.2) | collective-permute-done | bytes 131104 | tf_op jit(solution)/shard_map/ppermute | solution.py:236
  69.1 0.1 pad_maximum_fusion.own_ref
  69.1 1.9 %collective-permute-start.5 = (bf16[4,4,128,128]{3,2,1,0:T(8,128)(2,1)S(1)}, bf16[4,4,128,128]{3,2,1,0:T(8,128)(2,1)S(1)}, u32[]{:S(2)}, u32[]{:S(2)}) collective-permute-start(bf16[4,4,128,128]{3,2,1,0:T(8,128)(2,1)S(1)} %pad_maximum_fusion.own_ref), channel_id=1, source_target_pairs={{0,1},{1,0},{2,3},{3,2},{4,5},{5,4},{6,7},{7,6},{8,9},{9,8},{10,11... | collective-permute-start | bytes 1572872 | tf_op jit(solution)/shard_map/ppermute | solution.py:238
  71.1 0.1 pad_add_fusion.at_ref
  71.1 1.8 %collective-permute-done.5.oth_ref = bf16[4,4,128,128]{3,2,1,0:T(8,128)(2,1)S(1)} collective-permute-done((bf16[4,4,128,128]{3,2,1,0:T(8,128)(2,1)S(1)}, bf16[4,4,128,128]{3,2,1,0:T(8,128)(2,1)S(1)}, u32[]{:S(2)}, u32[]{:S(2)}) %collective-permute-start.5) | collective-permute-done | bytes 524320 | tf_op jit(solution)/shard_map/ppermute | solution.py:238
  72.9 5.7 %all-to-all-done.1.tan_ref = bf16[8,192,128]{2,1,0:T(8,128)(2,1)S(1)} async-done(((bf16[8,192,128]{2,1,0:T(8,128)(2,1)}), bf16[8,192,128]{2,1,0:T(8,128)(2,1)S(1)}, u32[]{:S(2)}, u32[]{:S(2)}) %all-to-all-start.1) | async-done | bytes 393248 | tf_op jit(solution)/shard_map/all_to_all | solution.py:241
  78.6 0.9 shard_map.88
  79.5 15.7 %collective-permute-start.6 = (bf16[2,192,128]{2,1,0:T(8,128)(2,1)S(1)}, bf16[2,192,128]{2,1,0:T(8,128)(2,1)S(1)}, u32[]{:S(2)}, u32[]{:S(2)}) collective-permute-start(bf16[2,192,128]{2,1,0:T(8,128)(2,1)S(1)} %shard_map.88), channel_id=1, source_target_pairs={{0,256},{1,769},{2,258},{3,771},{4,260},{5,773},{6,262},{7,775},{8... | collective-permute-start | bytes 294920 | tf_op jit(solution)/shard_map/ppermute | solution.py:260
  95.3 0.9 shard_map.87
  96.2 6.8 %collective-permute-done.6 = bf16[2,192,128]{2,1,0:T(8,128)(2,1)S(1)} collective-permute-done((bf16[2,192,128]{2,1,0:T(8,128)(2,1)S(1)}, bf16[2,192,128]{2,1,0:T(8,128)(2,1)S(1)}, u32[]{:S(2)}, u32[]{:S(2)}) %collective-permute-start.6) | collective-permute-done | bytes 98336 | tf_op jit(solution)/shard_map/ppermute | solution.py:260
  103.1 6.5 %collective-permute-start.7 = (bf16[192,128]{1,0:T(8,128)(2,1)S(1)}, bf16[192,128]{1,0:T(8,128)(2,1)S(1)}, u32[]{:S(2)}, u32[]{:S(2)}) collective-permute-start(bf16[192,128]{1,0:T(8,128)(2,1)S(1)} %fusion.4), channel_id=1, source_target_pairs={{0,768},{1,257},{2,770},{3,259},{4,772},{5,261},{6,774},{7,263},{8... | collective-permute-start | bytes 147464 | tf_op jit(solution)/shard_map/ppermute | solution.py:260
  109.6 10.8 %collective-permute-done.7 = bf16[192,128]{1,0:T(8,128)(2,1)S(1)} collective-permute-done((bf16[192,128]{1,0:T(8,128)(2,1)S(1)}, bf16[192,128]{1,0:T(8,128)(2,1)S(1)}, u32[]{:S(2)}, u32[]{:S(2)}) %collective-permute-start.7) | collective-permute-done | bytes 49184 | tf_op jit(solution)/shard_map/ppermute | solution.py:260
  120.3 0.6 fusion.3
  (3 shorter events, 0.0 us)
Async XLA Ops:
  29.2 6.6 %collective-permute-start = (bf16[16,256,128]{2,1,0:T(8,128)(2,1)S(1)}, bf16[16,256,128]{2,1,0:T(8,128)(2,1)S(1)}, u32[]{:S(2)}, u32[]{:S(2)}) collective-permute-start(bf16[16,256,128]{2,1,0:T(8,128)(2,1)S(1)} %all_to_all.10.rows_ref), channel_id=1, source_target_pairs={{0,1},{1,0},{2,3},{3,2},{4,5},{5,4},{6,7},{7,6},{8,9},{9,8},{10,11... | collective-permute-start | bytes 3145736 | tf_op jit(solution)/shard_map/ppermute | solution.py:191
  31.2 11.3 %collective-permute-start.1 = (bf16[4,128,128]{2,1,0:T(8,128)(2,1)S(1)}, bf16[4,128,128]{2,1,0:T(8,128)(2,1)S(1)}, u32[]{:S(2)}, u32[]{:S(2)}) collective-permute-start(bf16[4,128,128]{2,1,0:T(8,128)(2,1)S(1)} %shard_map.85), channel_id=1, source_target_pairs={{0,0},{1,160},{2,64},{3,224},{4,128},{5,32},{6,192},{7,96},{8,8},{... | collective-permute-start | bytes 393224 | tf_op jit(solution)/shard_map/ppermute | solution.py:204
  43.4 35.3 %all-to-all-start.1 = ((bf16[8,192,128]{2,1,0:T(8,128)(2,1)}), bf16[8,192,128]{2,1,0:T(8,128)(2,1)S(1)}, u32[]{:S(2)}, u32[]{:S(2)}) async-start(bf16[8,192,128]{2,1,0:T(8,128)(2,1)} %get-tuple-element.7), calls=%async_computation.1 | async-start | bytes 786432 | tf_op jit(solution)/shard_map/all_to_all | solution.py:241
  54.2 9.0 %collective-permute-start.4 = (bf16[4,128,128]{2,1,0:T(8,128)(2,1)S(1)}, bf16[4,128,128]{2,1,0:T(8,128)(2,1)S(1)}, u32[]{:S(2)}, u32[]{:S(2)}) collective-permute-start(bf16[4,128,128]{2,1,0:T(8,128)(2,1)S(1)} %get-tuple-element.8), channel_id=1, source_target_pairs={{0,6},{1,7},{2,0},{3,1},{4,2},{5,3},{6,4},{7,5},{8,14},{9,15},{10,... | collective-permute-start | bytes 393224 | tf_op jit(solution)/shard_map/ppermute | solution.py:236
  57.9 8.4 %collective-permute-start.3 = (bf16[4,128,128]{2,1,0:T(8,128)(2,1)S(1)}, bf16[4,128,128]{2,1,0:T(8,128)(2,1)S(1)}, u32[]{:S(2)}, u32[]{:S(2)}) collective-permute-start(bf16[4,128,128]{2,1,0:T(8,128)(2,1)S(1)} %get-tuple-element.8), channel_id=1, source_target_pairs={{0,4},{1,5},{2,6},{3,7},{4,0},{5,1},{6,2},{7,3},{8,12},{9,13},{10,... | collective-permute-start | bytes 393224 | tf_op jit(solution)/shard_map/ppermute | solution.py:236
  59.8 9.2 %collective-permute-start.2 = (bf16[4,128,128]{2,1,0:T(8,128)(2,1)S(1)}, bf16[4,128,128]{2,1,0:T(8,128)(2,1)S(1)}, u32[]{:S(2)}, u32[]{:S(2)}) collective-permute-start(bf16[4,128,128]{2,1,0:T(8,128)(2,1)S(1)} %get-tuple-element.8), channel_id=1, source_target_pairs={{0,2},{1,3},{2,4},{3,5},{4,6},{5,7},{6,0},{7,1},{8,10},{9,11},{10,... | collective-permute-start | bytes 393224 | tf_op jit(solution)/shard_map/ppermute | solution.py:236
  69.1 3.8 %collective-permute-start.5 = (bf16[4,4,128,128]{3,2,1,0:T(8,128)(2,1)S(1)}, bf16[4,4,128,128]{3,2,1,0:T(8,128)(2,1)S(1)}, u32[]{:S(2)}, u32[]{:S(2)}) collective-permute-start(bf16[4,4,128,128]{3,2,1,0:T(8,128)(2,1)S(1)} %pad_maximum_fusion.own_ref), channel_id=1, source_target_pairs={{0,1},{1,0},{2,3},{3,2},{4,5},{5,4},{6,7},{7,6},{8,9},{9,8},{10,11... | collective-permute-start | bytes 1572872 | tf_op jit(solution)/shard_map/ppermute | solution.py:238
  79.5 23.5 %collective-permute-start.6 = (bf16[2,192,128]{2,1,0:T(8,128)(2,1)S(1)}, bf16[2,192,128]{2,1,0:T(8,128)(2,1)S(1)}, u32[]{:S(2)}, u32[]{:S(2)}) collective-permute-start(bf16[2,192,128]{2,1,0:T(8,128)(2,1)S(1)} %shard_map.88), channel_id=1, source_target_pairs={{0,256},{1,769},{2,258},{3,771},{4,260},{5,773},{6,262},{7,775},{8... | collective-permute-start | bytes 294920 | tf_op jit(solution)/shard_map/ppermute | solution.py:260
  103.1 17.2 %collective-permute-start.7 = (bf16[192,128]{1,0:T(8,128)(2,1)S(1)}, bf16[192,128]{1,0:T(8,128)(2,1)S(1)}, u32[]{:S(2)}, u32[]{:S(2)}) collective-permute-start(bf16[192,128]{1,0:T(8,128)(2,1)S(1)} %fusion.4), channel_id=1, source_target_pairs={{0,768},{1,257},{2,770},{3,259},{4,772},{5,261},{6,774},{7,263},{8... | collective-permute-start | bytes 147464 | tf_op jit(solution)/shard_map/ppermute | solution.py:260

commit v8 on v7

--- a/solution.py
+++ b/solution.py
@@ -259,10 +259,12 @@
         ]
         return lax.ppermute(value, DPX, perm)
 
-    got = exchange(outer((1, 3), BF16), 1).astype(F32)
-    here, there = outer((0, 2), F32)
-    last = exchange((there + got[1]).astype(BF16), 2).astype(F32)
-    return (here + got[0] + last).astype(BF16)
+    passed = exchange(outer((3,), BF16), 1)
+    given = exchange(outer((1,), BF16), 1)
+    mine = outer((0, 2), F32)
+    last = exchange((mine[1:] + passed.astype(F32)).astype(BF16), 2)
+    total = mine[:1] + given.astype(F32) + last.astype(F32)
+    return total.astype(BF16)[0]
 
 
 def solution(mesh):

time: 121 us -> 119 us (0.983)
  the two profiles are of different devices: /device:TPU:2 before, /device:TPU:3 now
where the time goes in v8:
time: 119 us; the launch traced here: 118 us
  starting transfers between devices  69 us (58%)
  waiting for transfers between devices  20.3 us (17%)
  blocking collectives  17.5 us (15%)
  Pallas kernels  10.4 us (9%)
    ppermute x3, starting transfers between devices, exchange(): return lax.ppermute(value, DPX, perm)  29.4 us
    all_to_all x1, blocking collectives, on_device(): lax.all_to_all(send, 'expert', split_axis=0, concat_axis=0, tiled=True, a...  17.5 us
    ppermute x1, starting transfers between devices, on_device(): oth = lax.ppermute(own, 'expert', swap)  12.4 us
    ppermute x1, starting transfers between devices, on_device(): moved = lax.ppermute(picked, DPX, perm)  9.39 us
    all_to_all x1, starting transfers between devices, on_device(): lax.all_to_all(tangent, 'dp', split_axis=0, concat_axis=0, tiled=True, ax...  8 us
    ppermute x3, starting transfers between devices, on_device(): ring.append(lax.ppermute(mine, 'expert', perm))  7.19 us
    ppermute x3, waiting for transfers between devices, exchange(): return lax.ppermute(value, DPX, perm)  6.65 us
    ppermute x3, waiting for transfers between devices, on_device(): ring.append(lax.ppermute(mine, 'expert', perm))  6.53 us
  transfers between devices with their start and end apart: 10, of which 6 were waited for; matrix products, arithmetic and copies ran while one was open for 0% of the time, Pallas kernels for 6%

profile of v8, /device:TPU:3, one launch (start us, length us, event | category | flops | bytes accessed | tf_op | source)
XLA Modules:
  0.0 118.2 jit_solution(4828324076180896352)
XLA Ops:
  0.0 1.9 %shard_map.82 = bf16[16,256,128]{2,1,0:T(8,128)(2,1)S(1)} custom-call(s32[8,1024]{1,0:T(8,128)} %bitcast.16, f32[8,1024]{1,0:T(8,128)} %bitcast.17, bf16[1024,128]{1,0:T(8,128)(2,1)} %tok_hbm.1, bf16[1024,128]{1,0:T(8,128)(2,1)} %cot_hbm.1), custom_call_target="tpu_custom_call" | custom-call | flops 268435456 | bytes 2097152 | tf_op jit(solution)/shard_map/pallas_call | solution.py:172
  1.9 17.5 %all_to_all.10.rows_ref = bf16[16,256,128]{2,1,0:T(8,128)(2,1)S(1)} all-to-all(bf16[16,256,128]{2,1,0:T(8,128)(2,1)S(1)} %shard_map.82), channel_id=1, replica_groups={{0,2,4,6,8,10,12,14,16,18,20,22,24,26,28,30},{1,3,5,7,9,11,13,15,17,19,..., dimensions={0} | all-to-all | bytes 2097152 | tf_op jit(solution)/shard_map/all_to_all | solution.py:187
  19.3 12.4 %collective-permute-start = (bf16[16,256,128]{2,1,0:T(8,128)(2,1)S(1)}, bf16[16,256,128]{2,1,0:T(8,128)(2,1)S(1)}, u32[]{:S(2)}, u32[]{:S(2)}) collective-permute-start(bf16[16,256,128]{2,1,0:T(8,128)(2,1)S(1)} %all_to_all.10.rows_ref), channel_id=1, source_target_pairs={{0,1},{1,0},{2,3},{3,2},{4,5},{5,4},{6,7},{7,6},{8,9},{9,8},{10,11... | collective-permute-start | bytes 3145736 | tf_op jit(solution)/shard_map/ppermute | solution.py:191
  31.9 9.4 %collective-permute-start.1 = (bf16[4,128,128]{2,1,0:T(8,128)(2,1)S(1)}, bf16[4,128,128]{2,1,0:T(8,128)(2,1)S(1)}, u32[]{:S(2)}, u32[]{:S(2)}) collective-permute-start(bf16[4,128,128]{2,1,0:T(8,128)(2,1)S(1)} %shard_map.85), channel_id=1, source_target_pairs={{0,0},{1,160},{2,64},{3,224},{4,128},{5,32},{6,192},{7,96},{8,8},{... | collective-permute-start | bytes 393224 | tf_op jit(solution)/shard_map/ppermute | solution.py:204
  41.3 2.6 %shard_map.83.acc_ref = f32[4,192,128]{2,1,0:T(8,128)S(1)} custom-call(s32[1]{0:T(128)} %bitcast.1.c_ref, bf16[16,256,128]{2,1,0:T(8,128)(2,1)S(1)} %all_to_all.10.rows_ref, bf16[192,4096]{1,0:T(8,128)(2,1)} %g_hbm.3, bf16[192,4096]{1,0:T(8,128)(2,1)} %u_hbm.3, bf16[192,4096]{1,0:T(8,128)(2,1)} %p_hbm.3, bf16[192,4096]{1,0:T(8,128)(2,1)} %d_hbm.3), custom_call_target="tpu_custom_call" | custom-call | flops 402653184 | bytes 4194304 | tf_op jit(solution)/shard_map/pallas_call | solution.py:208
  43.9 0.0 collective-permute-done.rows_ref
  43.9 2.6 %shard_map.84.tan_ref = bf16[192,128]{1,0:T(8,128)(2,1)S(1)} custom-call(s32[1]{0:T(128)} %bitcast.1.c_ref, bf16[16,256,128]{2,1,0:T(8,128)(2,1)S(1)} %collective-permute-done.rows_ref, bf16[192,4096]{1,0:T(8,128)(2,1)} %g_hbm.3, bf16[192,4096]{1,0:T(8,128)(2,1)} %u_hbm.3, bf16[192,4096]{1,0:T(8,128)(2,1)} %p_hbm.3, bf16[192,4096]{1,0:T(8,128)(2,1)} %d_hbm.3, ...), custom_call_target="tpu_custom_call" | custom-call | flops 402653184 | bytes 4194304 | tf_op jit(solution)/shard_map/pallas_call | solution.py:216
  46.6 0.0 collective-permute-done.1.moved_ref
  46.6 0.8 shard_map.86
  47.4 8.0 %all-to-all-start.1 = ((bf16[8,192,128]{2,1,0:T(8,128)(2,1)}), bf16[8,192,128]{2,1,0:T(8,128)(2,1)S(1)}, u32[]{:S(2)}, u32[]{:S(2)}) async-start(bf16[8,192,128]{2,1,0:T(8,128)(2,1)} %get-tuple-element.7), calls=%async_computation.1 | async-start | bytes 786432 | tf_op jit(solution)/shard_map/all_to_all | solution.py:241
  55.4 1.9 %collective-permute-start.4 = (bf16[4,128,128]{2,1,0:T(8,128)(2,1)S(1)}, bf16[4,128,128]{2,1,0:T(8,128)(2,1)S(1)}, u32[]{:S(2)}, u32[]{:S(2)}) collective-permute-start(bf16[4,128,128]{2,1,0:T(8,128)(2,1)S(1)} %get-tuple-element.8), channel_id=1, source_target_pairs={{0,6},{1,7},{2,0},{3,1},{4,2},{5,3},{6,4},{7,5},{8,14},{9,15},{10,... | collective-permute-start | bytes 393224 | tf_op jit(solution)/shard_map/ppermute | solution.py:236
  57.3 1.9 %collective-permute-start.3 = (bf16[4,128,128]{2,1,0:T(8,128)(2,1)S(1)}, bf16[4,128,128]{2,1,0:T(8,128)(2,1)S(1)}, u32[]{:S(2)}, u32[]{:S(2)}) collective-permute-start(bf16[4,128,128]{2,1,0:T(8,128)(2,1)S(1)} %get-tuple-element.8), channel_id=1, source_target_pairs={{0,4},{1,5},{2,6},{3,7},{4,0},{5,1},{6,2},{7,3},{8,12},{9,13},{10,... | collective-permute-start | bytes 393224 | tf_op jit(solution)/shard_map/ppermute | solution.py:236
  59.2 3.4 %collective-permute-start.2 = (bf16[4,128,128]{2,1,0:T(8,128)(2,1)S(1)}, bf16[4,128,128]{2,1,0:T(8,128)(2,1)S(1)}, u32[]{:S(2)}, u32[]{:S(2)}) collective-permute-start(bf16[4,128,128]{2,1,0:T(8,128)(2,1)S(1)} %get-tuple-element.8), channel_id=1, source_target_pairs={{0,2},{1,3},{2,4},{3,5},{4,6},{5,7},{6,0},{7,1},{8,10},{9,11},{10,... | collective-permute-start | bytes 393224 | tf_op jit(solution)/shard_map/ppermute | solution.py:236
  62.6 0.1 collective-permute-done.4
  62.7 2.1 %collective-permute-done.3 = bf16[4,128,128]{2,1,0:T(8,128)(2,1)S(1)} collective-permute-done((bf16[4,128,128]{2,1,0:T(8,128)(2,1)S(1)}, bf16[4,128,128]{2,1,0:T(8,128)(2,1)S(1)}, u32[]{:S(2)}, u32[]{:S(2)}) %collective-permute-start.3) | collective-permute-done | bytes 131104 | tf_op jit(solution)/shard_map/ppermute | solution.py:236
  64.8 4.3 %collective-permute-done.2 = bf16[4,128,128]{2,1,0:T(8,128)(2,1)S(1)} collective-permute-done((bf16[4,128,128]{2,1,0:T(8,128)(2,1)S(1)}, bf16[4,128,128]{2,1,0:T(8,128)(2,1)S(1)}, u32[]{:S(2)}, u32[]{:S(2)}) %collective-permute-start.2) | collective-permute-done | bytes 131104 | tf_op jit(solution)/shard_map/ppermute | solution.py:236
  69.1 0.1 pad_maximum_fusion.own_ref
  69.2 2.5 %collective-permute-start.5 = (bf16[4,4,128,128]{3,2,1,0:T(8,128)(2,1)S(1)}, bf16[4,4,128,128]{3,2,1,0:T(8,128)(2,1)S(1)}, u32[]{:S(2)}, u32[]{:S(2)}) collective-permute-start(bf16[4,4,128,128]{3,2,1,0:T(8,128)(2,1)S(1)} %pad_maximum_fusion.own_ref), channel_id=1, source_target_pairs={{0,1},{1,0},{2,3},{3,2},{4,5},{5,4},{6,7},{7,6},{8,9},{9,8},{10,11... | collective-permute-start | bytes 1572872 | tf_op jit(solution)/shard_map/ppermute | solution.py:238
  71.7 0.1 pad_add_fusion.at_ref
  71.8 1.4 %collective-permute-done.5.oth_ref = bf16[4,4,128,128]{3,2,1,0:T(8,128)(2,1)S(1)} collective-permute-done((bf16[4,4,128,128]{3,2,1,0:T(8,128)(2,1)S(1)}, bf16[4,4,128,128]{3,2,1,0:T(8,128)(2,1)S(1)}, u32[]{:S(2)}, u32[]{:S(2)}) %collective-permute-start.5) | collective-permute-done | bytes 524320 | tf_op jit(solution)/shard_map/ppermute | solution.py:238
  73.2 5.7 %all-to-all-done.1.tan_ref = bf16[8,192,128]{2,1,0:T(8,128)(2,1)S(1)} async-done(((bf16[8,192,128]{2,1,0:T(8,128)(2,1)}), bf16[8,192,128]{2,1,0:T(8,128)(2,1)S(1)}, u32[]{:S(2)}, u32[]{:S(2)}) %all-to-all-start.1) | async-done | bytes 393248 | tf_op jit(solution)/shard_map/all_to_all | solution.py:241
  78.9 0.8 shard_map.89
  79.7 9.8 %collective-permute-start.7 = (bf16[1,192,128]{2,1,0:T(8,128)(2,1)S(1)}, bf16[1,192,128]{2,1,0:T(8,128)(2,1)S(1)}, u32[]{:S(2)}, u32[]{:S(2)}) collective-permute-start(bf16[1,192,128]{2,1,0:T(8,128)(2,1)S(1)} %shard_map.89), channel_id=1, source_target_pairs={{0,256},{1,769},{2,258},{3,771},{4,260},{5,773},{6,262},{7,775},{8... | collective-permute-start | bytes 147464 | tf_op jit(solution)/shard_map/ppermute | solution.py:260
  89.5 0.8 shard_map.88
  90.3 4.2 %collective-permute-start.6 = (bf16[1,192,128]{2,1,0:T(8,128)(2,1)S(1)}, bf16[1,192,128]{2,1,0:T(8,128)(2,1)S(1)}, u32[]{:S(2)}, u32[]{:S(2)}) collective-permute-start(bf16[1,192,128]{2,1,0:T(8,128)(2,1)S(1)} %shard_map.88), channel_id=1, source_target_pairs={{0,256},{1,769},{2,258},{3,771},{4,260},{5,773},{6,262},{7,775},{8... | collective-permute-start | bytes 147464 | tf_op jit(solution)/shard_map/ppermute | solution.py:260
  94.5 0.9 shard_map.87
  95.5 0.0 collective-permute-done.7
  95.5 15.4 %collective-permute-start.8 = (bf16[1,192,128]{2,1,0:T(8,128)(2,1)S(1)}, bf16[1,192,128]{2,1,0:T(8,128)(2,1)S(1)}, u32[]{:S(2)}, u32[]{:S(2)}) collective-permute-start(bf16[1,192,128]{2,1,0:T(8,128)(2,1)S(1)} %fusion), channel_id=1, source_target_pairs={{0,768},{1,257},{2,770},{3,259},{4,772},{5,261},{6,774},{7,263},{8... | collective-permute-start | bytes 147464 | tf_op jit(solution)/shard_map/ppermute | solution.py:260
  110.9 0.0 collective-permute-done.6
  111.0 6.6 %collective-permute-done.8 = bf16[1,192,128]{2,1,0:T(8,128)(2,1)S(1)} collective-permute-done((bf16[1,192,128]{2,1,0:T(8,128)(2,1)S(1)}, bf16[1,192,128]{2,1,0:T(8,128)(2,1)S(1)}, u32[]{:S(2)}, u32[]{:S(2)}) %collective-permute-start.8) | collective-permute-done | bytes 49184 | tf_op jit(solution)/shard_map/ppermute | solution.py:260
  117.6 0.6 fusion.3
  (2 shorter events, 0.0 us)
Async XLA Ops:
  19.3 24.6 %collective-permute-start = (bf16[16,256,128]{2,1,0:T(8,128)(2,1)S(1)}, bf16[16,256,128]{2,1,0:T(8,128)(2,1)S(1)}, u32[]{:S(2)}, u32[]{:S(2)}) collective-permute-start(bf16[16,256,128]{2,1,0:T(8,128)(2,1)S(1)} %all_to_all.10.rows_ref), channel_id=1, source_target_pairs={{0,1},{1,0},{2,3},{3,2},{4,5},{5,4},{6,7},{7,6},{8,9},{9,8},{10,11... | collective-permute-start | bytes 3145736 | tf_op jit(solution)/shard_map/ppermute | solution.py:191
  31.9 14.7 %collective-permute-start.1 = (bf16[4,128,128]{2,1,0:T(8,128)(2,1)S(1)}, bf16[4,128,128]{2,1,0:T(8,128)(2,1)S(1)}, u32[]{:S(2)}, u32[]{:S(2)}) collective-permute-start(bf16[4,128,128]{2,1,0:T(8,128)(2,1)S(1)} %shard_map.85), channel_id=1, source_target_pairs={{0,0},{1,160},{2,64},{3,224},{4,128},{5,32},{6,192},{7,96},{8,8},{... | collective-permute-start | bytes 393224 | tf_op jit(solution)/shard_map/ppermute | solution.py:204
  47.4 31.5 %all-to-all-start.1 = ((bf16[8,192,128]{2,1,0:T(8,128)(2,1)}), bf16[8,192,128]{2,1,0:T(8,128)(2,1)S(1)}, u32[]{:S(2)}, u32[]{:S(2)}) async-start(bf16[8,192,128]{2,1,0:T(8,128)(2,1)} %get-tuple-element.7), calls=%async_computation.1 | async-start | bytes 786432 | tf_op jit(solution)/shard_map/all_to_all | solution.py:241
  55.4 7.3 %collective-permute-start.4 = (bf16[4,128,128]{2,1,0:T(8,128)(2,1)S(1)}, bf16[4,128,128]{2,1,0:T(8,128)(2,1)S(1)}, u32[]{:S(2)}, u32[]{:S(2)}) collective-permute-start(bf16[4,128,128]{2,1,0:T(8,128)(2,1)S(1)} %get-tuple-element.8), channel_id=1, source_target_pairs={{0,6},{1,7},{2,0},{3,1},{4,2},{5,3},{6,4},{7,5},{8,14},{9,15},{10,... | collective-permute-start | bytes 393224 | tf_op jit(solution)/shard_map/ppermute | solution.py:236
  57.3 7.5 %collective-permute-start.3 = (bf16[4,128,128]{2,1,0:T(8,128)(2,1)S(1)}, bf16[4,128,128]{2,1,0:T(8,128)(2,1)S(1)}, u32[]{:S(2)}, u32[]{:S(2)}) collective-permute-start(bf16[4,128,128]{2,1,0:T(8,128)(2,1)S(1)} %get-tuple-element.8), channel_id=1, source_target_pairs={{0,4},{1,5},{2,6},{3,7},{4,0},{5,1},{6,2},{7,3},{8,12},{9,13},{10,... | collective-permute-start | bytes 393224 | tf_op jit(solution)/shard_map/ppermute | solution.py:236
  59.2 9.9 %collective-permute-start.2 = (bf16[4,128,128]{2,1,0:T(8,128)(2,1)S(1)}, bf16[4,128,128]{2,1,0:T(8,128)(2,1)S(1)}, u32[]{:S(2)}, u32[]{:S(2)}) collective-permute-start(bf16[4,128,128]{2,1,0:T(8,128)(2,1)S(1)} %get-tuple-element.8), channel_id=1, source_target_pairs={{0,2},{1,3},{2,4},{3,5},{4,6},{5,7},{6,0},{7,1},{8,10},{9,11},{10,... | collective-permute-start | bytes 393224 | tf_op jit(solution)/shard_map/ppermute | solution.py:236
  69.2 4.0 %collective-permute-start.5 = (bf16[4,4,128,128]{3,2,1,0:T(8,128)(2,1)S(1)}, bf16[4,4,128,128]{3,2,1,0:T(8,128)(2,1)S(1)}, u32[]{:S(2)}, u32[]{:S(2)}) collective-permute-start(bf16[4,4,128,128]{3,2,1,0:T(8,128)(2,1)S(1)} %pad_maximum_fusion.own_ref), channel_id=1, source_target_pairs={{0,1},{1,0},{2,3},{3,2},{4,5},{5,4},{6,7},{7,6},{8,9},{9,8},{10,11... | collective-permute-start | bytes 1572872 | tf_op jit(solution)/shard_map/ppermute | solution.py:238
  79.7 15.7 %collective-permute-start.7 = (bf16[1,192,128]{2,1,0:T(8,128)(2,1)S(1)}, bf16[1,192,128]{2,1,0:T(8,128)(2,1)S(1)}, u32[]{:S(2)}, u32[]{:S(2)}) collective-permute-start(bf16[1,192,128]{2,1,0:T(8,128)(2,1)S(1)} %shard_map.89), channel_id=1, source_target_pairs={{0,256},{1,769},{2,258},{3,771},{4,260},{5,773},{6,262},{7,775},{8... | collective-permute-start | bytes 147464 | tf_op jit(solution)/shard_map/ppermute | solution.py:260
  90.3 20.6 %collective-permute-start.6 = (bf16[1,192,128]{2,1,0:T(8,128)(2,1)S(1)}, bf16[1,192,128]{2,1,0:T(8,128)(2,1)S(1)}, u32[]{:S(2)}, u32[]{:S(2)}) collective-permute-start(bf16[1,192,128]{2,1,0:T(8,128)(2,1)S(1)} %shard_map.88), channel_id=1, source_target_pairs={{0,256},{1,769},{2,258},{3,771},{4,260},{5,773},{6,262},{7,775},{8... | collective-permute-start | bytes 147464 | tf_op jit(solution)/shard_map/ppermute | solution.py:260
  95.5 22.1 %collective-permute-start.8 = (bf16[1,192,128]{2,1,0:T(8,128)(2,1)S(1)}, bf16[1,192,128]{2,1,0:T(8,128)(2,1)S(1)}, u32[]{:S(2)}, u32[]{:S(2)}) collective-permute-start(bf16[1,192,128]{2,1,0:T(8,128)(2,1)S(1)} %fusion), channel_id=1, source_target_pairs={{0,768},{1,257},{2,770},{3,259},{4,772},{5,261},{6,774},{7,263},{8... | collective-permute-start | bytes 147464 | tf_op jit(solution)/shard_map/ppermute | solution.py:260

commit v9 on v8

--- a/solution.py
+++ b/solution.py
@@ -117,15 +117,14 @@
 
 
 def outer_kernel(flips, at_ref, tan_ref, own_ref, oth_ref, out_ref):
-    x, c, zhi = at_ref[0], at_ref[1], at_ref[2]
+    x, c, zhi, turn = at_ref[0], at_ref[1], at_ref[2], at_ref[3]
     for n, flip in enumerate(flips):
         dest = flipped(zhi, flip, c)
         acc = None
         for dx in range(WIN):
             chip = (x - dx + WIN) % WIN
-            lhs = jnp.concatenate(
-                [tan_ref[2 * chip + c], tan_ref[2 * chip + 1 - c]], axis=1
-            )
+            blocks = [(turn - chip - core) % WIN * 2 + core for core in (c, 1 - c)]
+            lhs = jnp.concatenate([tan_ref[b] for b in blocks], axis=1)
             rhs = jnp.concatenate([own_ref[dx, dest], oth_ref[dx, dest]], axis=1)
             part = lax.dot_general(
                 lhs, rhs, (((1,), (1,)), ((), ())), preferred_element_type=F32
@@ -166,7 +165,10 @@
     z, h = lax.axis_index("dp"), lax.axis_index("expert")
     x, c = (h // 2) % WIN, h % 2
     hid, feats = gate_proj.shape[0], tokens.shape[1]
-    at = jnp.stack([x, c, z // ZLO, (x + z % ZLO // 2 + z % 2 + 2 * c) % WIN]).astype(jnp.int32)
+    low = z % ZLO
+    turn = low // 2 - 2 * (low % 2) + 2 * WIN
+    pick = (x + low // 2 + low % 2 + 2 * c) % WIN
+    at = jnp.stack([x, c, z // ZLO, turn, pick]).astype(jnp.int32)
     rows, cols = tokens.shape[0], gate_proj.shape[1]
 
     send = call(
@@ -192,11 +194,13 @@
 
     picked = call(
         pick_kernel, sds((WIN, feats, CAP), BF16), [SMEM, VMEM], 0, 1 << 18
-    )(at[3:], own)
+    )(at[4:], own)
     perm = [
         (
             i * 32 + k,
-            (i // 8 * 8 + (k // 2 + i % 8 // 2 + i % 2 + 2 * (k % 2)) % 4 * 2 + k % 2) * 32 + k // 8 * 8 + i % 8,
+            (i // 8 * 8 + (k // 2 + i % 8 // 2 + i % 2 + 2 * (k % 2)) % 4 * 2 + k % 2) * 32
+            + k // 2 * 2
+            + i % 2,
         )
         for i in range(ZN)
         for k in range(32)
@@ -249,7 +253,7 @@
             [SMEM] + [VMEM] * 3,
             2 * len(flips) * hid * 1024 * CAP,
             2 << 20,
-        )(at[:3], tangents, own_t, oth_t)
+        )(at[:4], tangents, own_t, oth_t)
 
     def exchange(value, flip):
         perm = [

time: 119 us -> 115 us (0.966)
  the two profiles are of different devices: /device:TPU:3 before, /device:TPU:32 now
where the time goes in v9:
time: 115 us
  starting transfers between devices  62.5 us (54%)
  blocking collectives  24 us (21%)
  waiting for transfers between devices  16.8 us (15%)
  Pallas kernels  10.4 us (9%)
    ppermute x3, starting transfers between devices, exchange(): return lax.ppermute(value, DPX, perm)  31.3 us
    all_to_all x1, blocking collectives, on_device(): lax.all_to_all(send, 'expert', split_axis=0, concat_axis=0, tiled=True, a...  24 us
    all_to_all x1, starting transfers between devices, on_device(): lax.all_to_all(tangent, 'dp', split_axis=0, concat_axis=0, tiled=True, ax...  15.1 us
    ppermute x3, starting transfers between devices, on_device(): ring.append(lax.ppermute(mine, 'expert', perm))  8.26 us
    ppermute x3, waiting for transfers between devices, on_device(): ring.append(lax.ppermute(mine, 'expert', perm))  6.14 us
    ppermute x3, waiting for transfers between devices, exchange(): return lax.ppermute(value, DPX, perm)  5.12 us
    ppermute x1, starting transfers between devices, on_device(): moved = lax.ppermute(picked, DPX, perm)  3.93 us
    pallas_call x1, Pallas kernels, on_device(): call(own_kernel, sds((4, hid, CAP), F32), [SMEM, VMEM] + [HBM] * 4, 4 * h...  2.62 us
  transfers between devices with their start and end apart: 10, of which 7 were waited for; matrix products, arithmetic and copies ran while one was open for 0% of the time, Pallas kernels for 6%

profile of v9, /device:TPU:32, one launch (start us, length us, event | category | flops | bytes accessed | tf_op | source)
XLA Modules:
  0.0 114.8 jit_solution(17432479537583816737)
XLA Ops:
  0.0 1.9 %shard_map.82 = bf16[16,256,128]{2,1,0:T(8,128)(2,1)S(1)} custom-call(s32[8,1024]{1,0:T(8,128)} %bitcast.17, f32[8,1024]{1,0:T(8,128)} %bitcast.18, bf16[1024,128]{1,0:T(8,128)(2,1)} %tok_hbm.1, bf16[1024,128]{1,0:T(8,128)(2,1)} %cot_hbm.1), custom_call_target="tpu_custom_call" | custom-call | flops 268435456 | bytes 2097152 | tf_op jit(solution)/shard_map/pallas_call | solution.py:174
  1.9 24.0 %all_to_all.10.rows_ref = bf16[16,256,128]{2,1,0:T(8,128)(2,1)S(1)} all-to-all(bf16[16,256,128]{2,1,0:T(8,128)(2,1)S(1)} %shard_map.82), channel_id=1, replica_groups={{0,2,4,6,8,10,12,14,16,18,20,22,24,26,28,30},{1,3,5,7,9,11,13,15,17,19,..., dimensions={0} | all-to-all | bytes 2097152 | tf_op jit(solution)/shard_map/all_to_all | solution.py:189
  25.8 1.9 %collective-permute-start = (bf16[16,256,128]{2,1,0:T(8,128)(2,1)S(1)}, bf16[16,256,128]{2,1,0:T(8,128)(2,1)S(1)}, u32[]{:S(2)}, u32[]{:S(2)}) collective-permute-start(bf16[16,256,128]{2,1,0:T(8,128)(2,1)S(1)} %all_to_all.10.rows_ref), channel_id=1, source_target_pairs={{0,1},{1,0},{2,3},{3,2},{4,5},{5,4},{6,7},{7,6},{8,9},{9,8},{10,11... | collective-permute-start | bytes 3145736 | tf_op jit(solution)/shard_map/ppermute | solution.py:193
  27.9 3.9 %collective-permute-start.1 = (bf16[4,128,128]{2,1,0:T(8,128)(2,1)S(1)}, bf16[4,128,128]{2,1,0:T(8,128)(2,1)S(1)}, u32[]{:S(2)}, u32[]{:S(2)}) collective-permute-start(bf16[4,128,128]{2,1,0:T(8,128)(2,1)S(1)} %shard_map.85), channel_id=1, source_target_pairs={{0,0},{1,160},{2,66},{3,226},{4,132},{5,36},{6,198},{7,102},{8,8},... | collective-permute-start | bytes 393224 | tf_op jit(solution)/shard_map/ppermute | solution.py:208
  31.8 2.6 %shard_map.83.acc_ref = f32[4,192,128]{2,1,0:T(8,128)S(1)} custom-call(s32[1]{0:T(128)} %bitcast.1.c_ref, bf16[16,256,128]{2,1,0:T(8,128)(2,1)S(1)} %all_to_all.10.rows_ref, bf16[192,4096]{1,0:T(8,128)(2,1)} %g_hbm.3, bf16[192,4096]{1,0:T(8,128)(2,1)} %u_hbm.3, bf16[192,4096]{1,0:T(8,128)(2,1)} %p_hbm.3, bf16[192,4096]{1,0:T(8,128)(2,1)} %d_hbm.3), custom_call_target="tpu_custom_call" | custom-call | flops 402653184 | bytes 4194304 | tf_op jit(solution)/shard_map/pallas_call | solution.py:212
  34.4 0.0 collective-permute-done.rows_ref
  34.5 2.6 %shard_map.84.tan_ref = bf16[192,128]{1,0:T(8,128)(2,1)S(1)} custom-call(s32[1]{0:T(128)} %bitcast.1.c_ref, bf16[16,256,128]{2,1,0:T(8,128)(2,1)S(1)} %collective-permute-done.rows_ref, bf16[192,4096]{1,0:T(8,128)(2,1)} %g_hbm.3, bf16[192,4096]{1,0:T(8,128)(2,1)} %u_hbm.3, bf16[192,4096]{1,0:T(8,128)(2,1)} %p_hbm.3, bf16[192,4096]{1,0:T(8,128)(2,1)} %d_hbm.3, ...), custom_call_target="tpu_custom_call" | custom-call | flops 402653184 | bytes 4194304 | tf_op jit(solution)/shard_map/pallas_call | solution.py:220
  37.1 1.3 %collective-permute-done.1.moved_ref = bf16[4,128,128]{2,1,0:T(8,128)(2,1)S(1)} collective-permute-done((bf16[4,128,128]{2,1,0:T(8,128)(2,1)S(1)}, bf16[4,128,128]{2,1,0:T(8,128)(2,1)S(1)}, u32[]{:S(2)}, u32[]{:S(2)}) %collective-permute-start.1) | collective-permute-done | bytes 131104 | tf_op jit(solution)/shard_map/ppermute | solution.py:208
  38.4 0.8 shard_map.86
  39.2 15.1 %all-to-all-start.1 = ((bf16[8,192,128]{2,1,0:T(8,128)(2,1)}), bf16[8,192,128]{2,1,0:T(8,128)(2,1)S(1)}, u32[]{:S(2)}, u32[]{:S(2)}) async-start(bf16[8,192,128]{2,1,0:T(8,128)(2,1)} %get-tuple-element.7), calls=%async_computation.1 | async-start | bytes 786432 | tf_op jit(solution)/shard_map/all_to_all | solution.py:245
  54.3 3.1 %collective-permute-start.4 = (bf16[4,128,128]{2,1,0:T(8,128)(2,1)S(1)}, bf16[4,128,128]{2,1,0:T(8,128)(2,1)S(1)}, u32[]{:S(2)}, u32[]{:S(2)}) collective-permute-start(bf16[4,128,128]{2,1,0:T(8,128)(2,1)S(1)} %get-tuple-element.8), channel_id=1, source_target_pairs={{0,6},{1,7},{2,0},{3,1},{4,2},{5,3},{6,4},{7,5},{8,14},{9,15},{10,... | collective-permute-start | bytes 393224 | tf_op jit(solution)/shard_map/ppermute | solution.py:240
  57.4 3.2 %collective-permute-start.3 = (bf16[4,128,128]{2,1,0:T(8,128)(2,1)S(1)}, bf16[4,128,128]{2,1,0:T(8,128)(2,1)S(1)}, u32[]{:S(2)}, u32[]{:S(2)}) collective-permute-start(bf16[4,128,128]{2,1,0:T(8,128)(2,1)S(1)} %get-tuple-element.8), channel_id=1, source_target_pairs={{0,4},{1,5},{2,6},{3,7},{4,0},{5,1},{6,2},{7,3},{8,12},{9,13},{10,... | collective-permute-start | bytes 393224 | tf_op jit(solution)/shard_map/ppermute | solution.py:240
  60.7 1.9 %collective-permute-start.2 = (bf16[4,128,128]{2,1,0:T(8,128)(2,1)S(1)}, bf16[4,128,128]{2,1,0:T(8,128)(2,1)S(1)}, u32[]{:S(2)}, u32[]{:S(2)}) collective-permute-start(bf16[4,128,128]{2,1,0:T(8,128)(2,1)S(1)} %get-tuple-element.8), channel_id=1, source_target_pairs={{0,2},{1,3},{2,4},{3,5},{4,6},{5,7},{6,0},{7,1},{8,10},{9,11},{10,... | collective-permute-start | bytes 393224 | tf_op jit(solution)/shard_map/ppermute | solution.py:240
  62.6 0.0 collective-permute-done.4
  62.6 4.4 %collective-permute-done.3 = bf16[4,128,128]{2,1,0:T(8,128)(2,1)S(1)} collective-permute-done((bf16[4,128,128]{2,1,0:T(8,128)(2,1)S(1)}, bf16[4,128,128]{2,1,0:T(8,128)(2,1)S(1)}, u32[]{:S(2)}, u32[]{:S(2)}) %collective-permute-start.3) | collective-permute-done | bytes 131104 | tf_op jit(solution)/shard_map/ppermute | solution.py:240
  67.0 1.8 %collective-permute-done.2 = bf16[4,128,128]{2,1,0:T(8,128)(2,1)S(1)} collective-permute-done((bf16[4,128,128]{2,1,0:T(8,128)(2,1)S(1)}, bf16[4,128,128]{2,1,0:T(8,128)(2,1)S(1)}, u32[]{:S(2)}, u32[]{:S(2)}) %collective-permute-start.2) | collective-permute-done | bytes 131104 | tf_op jit(solution)/shard_map/ppermute | solution.py:240
  68.7 0.1 pad_maximum_fusion.own_ref
  68.8 1.9 %collective-permute-start.5 = (bf16[4,4,128,128]{3,2,1,0:T(8,128)(2,1)S(1)}, bf16[4,4,128,128]{3,2,1,0:T(8,128)(2,1)S(1)}, u32[]{:S(2)}, u32[]{:S(2)}) collective-permute-start(bf16[4,4,128,128]{3,2,1,0:T(8,128)(2,1)S(1)} %pad_maximum_fusion.own_ref), channel_id=1, source_target_pairs={{0,1},{1,0},{2,3},{3,2},{4,5},{5,4},{6,7},{7,6},{8,9},{9,8},{10,11... | collective-permute-start | bytes 1572872 | tf_op jit(solution)/shard_map/ppermute | solution.py:242
  70.8 0.1 pad_add_fusion.at_ref
  70.8 1.8 %collective-permute-done.5.oth_ref = bf16[4,4,128,128]{3,2,1,0:T(8,128)(2,1)S(1)} collective-permute-done((bf16[4,4,128,128]{3,2,1,0:T(8,128)(2,1)S(1)}, bf16[4,4,128,128]{3,2,1,0:T(8,128)(2,1)S(1)}, u32[]{:S(2)}, u32[]{:S(2)}) %collective-permute-start.5) | collective-permute-done | bytes 524320 | tf_op jit(solution)/shard_map/ppermute | solution.py:242
  72.6 2.4 %all-to-all-done.1.tan_ref = bf16[8,192,128]{2,1,0:T(8,128)(2,1)S(1)} async-done(((bf16[8,192,128]{2,1,0:T(8,128)(2,1)}), bf16[8,192,128]{2,1,0:T(8,128)(2,1)S(1)}, u32[]{:S(2)}, u32[]{:S(2)}) %all-to-all-start.1) | async-done | bytes 393248 | tf_op jit(solution)/shard_map/all_to_all | solution.py:245
  75.0 0.8 shard_map.89
  75.9 15.7 %collective-permute-start.7 = (bf16[1,192,128]{2,1,0:T(8,128)(2,1)S(1)}, bf16[1,192,128]{2,1,0:T(8,128)(2,1)S(1)}, u32[]{:S(2)}, u32[]{:S(2)}) collective-permute-start(bf16[1,192,128]{2,1,0:T(8,128)(2,1)S(1)} %shard_map.89), channel_id=1, source_target_pairs={{0,256},{1,769},{2,258},{3,771},{4,260},{5,773},{6,262},{7,775},{8... | collective-permute-start | bytes 147464 | tf_op jit(solution)/shard_map/ppermute | solution.py:264
  91.6 0.8 shard_map.88
  92.4 1.9 %collective-permute-start.6 = (bf16[1,192,128]{2,1,0:T(8,128)(2,1)S(1)}, bf16[1,192,128]{2,1,0:T(8,128)(2,1)S(1)}, u32[]{:S(2)}, u32[]{:S(2)}) collective-permute-start(bf16[1,192,128]{2,1,0:T(8,128)(2,1)S(1)} %shard_map.88), channel_id=1, source_target_pairs={{0,256},{1,769},{2,258},{3,771},{4,260},{5,773},{6,262},{7,775},{8... | collective-permute-start | bytes 147464 | tf_op jit(solution)/shard_map/ppermute | solution.py:264
  94.3 0.9 shard_map.87
  95.3 0.0 collective-permute-done.7
  95.3 13.7 %collective-permute-start.8 = (bf16[1,192,128]{2,1,0:T(8,128)(2,1)S(1)}, bf16[1,192,128]{2,1,0:T(8,128)(2,1)S(1)}, u32[]{:S(2)}, u32[]{:S(2)}) collective-permute-start(bf16[1,192,128]{2,1,0:T(8,128)(2,1)S(1)} %fusion), channel_id=1, source_target_pairs={{0,768},{1,257},{2,770},{3,259},{4,772},{5,261},{6,774},{7,263},{8... | collective-permute-start | bytes 147464 | tf_op jit(solution)/shard_map/ppermute | solution.py:264
  109.0 2.2 %collective-permute-done.6 = bf16[1,192,128]{2,1,0:T(8,128)(2,1)S(1)} collective-permute-done((bf16[1,192,128]{2,1,0:T(8,128)(2,1)S(1)}, bf16[1,192,128]{2,1,0:T(8,128)(2,1)S(1)}, u32[]{:S(2)}, u32[]{:S(2)}) %collective-permute-start.6) | collective-permute-done | bytes 49184 | tf_op jit(solution)/shard_map/ppermute | solution.py:264
  111.2 2.9 %collective-permute-done.8 = bf16[1,192,128]{2,1,0:T(8,128)(2,1)S(1)} collective-permute-done((bf16[1,192,128]{2,1,0:T(8,128)(2,1)S(1)}, bf16[1,192,128]{2,1,0:T(8,128)(2,1)S(1)}, u32[]{:S(2)}, u32[]{:S(2)}) %collective-permute-start.8) | collective-permute-done | bytes 49184 | tf_op jit(solution)/shard_map/ppermute | solution.py:264
  114.1 0.6 fusion.3
  (2 shorter events, 0.0 us)
Async XLA Ops:
  25.8 8.6 %collective-permute-start = (bf16[16,256,128]{2,1,0:T(8,128)(2,1)S(1)}, bf16[16,256,128]{2,1,0:T(8,128)(2,1)S(1)}, u32[]{:S(2)}, u32[]{:S(2)}) collective-permute-start(bf16[16,256,128]{2,1,0:T(8,128)(2,1)S(1)} %all_to_all.10.rows_ref), channel_id=1, source_target_pairs={{0,1},{1,0},{2,3},{3,2},{4,5},{5,4},{6,7},{7,6},{8,9},{9,8},{10,11... | collective-permute-start | bytes 3145736 | tf_op jit(solution)/shard_map/ppermute | solution.py:193
  27.9 10.5 %collective-permute-start.1 = (bf16[4,128,128]{2,1,0:T(8,128)(2,1)S(1)}, bf16[4,128,128]{2,1,0:T(8,128)(2,1)S(1)}, u32[]{:S(2)}, u32[]{:S(2)}) collective-permute-start(bf16[4,128,128]{2,1,0:T(8,128)(2,1)S(1)} %shard_map.85), channel_id=1, source_target_pairs={{0,0},{1,160},{2,66},{3,226},{4,132},{5,36},{6,198},{7,102},{8,8},... | collective-permute-start | bytes 393224 | tf_op jit(solution)/shard_map/ppermute | solution.py:208
  39.2 35.9 %all-to-all-start.1 = ((bf16[8,192,128]{2,1,0:T(8,128)(2,1)}), bf16[8,192,128]{2,1,0:T(8,128)(2,1)S(1)}, u32[]{:S(2)}, u32[]{:S(2)}) async-start(bf16[8,192,128]{2,1,0:T(8,128)(2,1)} %get-tuple-element.7), calls=%async_computation.1 | async-start | bytes 786432 | tf_op jit(solution)/shard_map/all_to_all | solution.py:245
  54.3 8.3 %collective-permute-start.4 = (bf16[4,128,128]{2,1,0:T(8,128)(2,1)S(1)}, bf16[4,128,128]{2,1,0:T(8,128)(2,1)S(1)}, u32[]{:S(2)}, u32[]{:S(2)}) collective-permute-start(bf16[4,128,128]{2,1,0:T(8,128)(2,1)S(1)} %get-tuple-element.8), channel_id=1, source_target_pairs={{0,6},{1,7},{2,0},{3,1},{4,2},{5,3},{6,4},{7,5},{8,14},{9,15},{10,... | collective-permute-start | bytes 393224 | tf_op jit(solution)/shard_map/ppermute | solution.py:240
  57.4 9.5 %collective-permute-start.3 = (bf16[4,128,128]{2,1,0:T(8,128)(2,1)S(1)}, bf16[4,128,128]{2,1,0:T(8,128)(2,1)S(1)}, u32[]{:S(2)}, u32[]{:S(2)}) collective-permute-start(bf16[4,128,128]{2,1,0:T(8,128)(2,1)S(1)} %get-tuple-element.8), channel_id=1, source_target_pairs={{0,4},{1,5},{2,6},{3,7},{4,0},{5,1},{6,2},{7,3},{8,12},{9,13},{10,... | collective-permute-start | bytes 393224 | tf_op jit(solution)/shard_map/ppermute | solution.py:240
  60.7 8.1 %collective-permute-start.2 = (bf16[4,128,128]{2,1,0:T(8,128)(2,1)S(1)}, bf16[4,128,128]{2,1,0:T(8,128)(2,1)S(1)}, u32[]{:S(2)}, u32[]{:S(2)}) collective-permute-start(bf16[4,128,128]{2,1,0:T(8,128)(2,1)S(1)} %get-tuple-element.8), channel_id=1, source_target_pairs={{0,2},{1,3},{2,4},{3,5},{4,6},{5,7},{6,0},{7,1},{8,10},{9,11},{10,... | collective-permute-start | bytes 393224 | tf_op jit(solution)/shard_map/ppermute | solution.py:240
  68.8 3.8 %collective-permute-start.5 = (bf16[4,4,128,128]{3,2,1,0:T(8,128)(2,1)S(1)}, bf16[4,4,128,128]{3,2,1,0:T(8,128)(2,1)S(1)}, u32[]{:S(2)}, u32[]{:S(2)}) collective-permute-start(bf16[4,4,128,128]{3,2,1,0:T(8,128)(2,1)S(1)} %pad_maximum_fusion.own_ref), channel_id=1, source_target_pairs={{0,1},{1,0},{2,3},{3,2},{4,5},{5,4},{6,7},{7,6},{8,9},{9,8},{10,11... | collective-permute-start | bytes 1572872 | tf_op jit(solution)/shard_map/ppermute | solution.py:242
  75.9 19.4 %collective-permute-start.7 = (bf16[1,192,128]{2,1,0:T(8,128)(2,1)S(1)}, bf16[1,192,128]{2,1,0:T(8,128)(2,1)S(1)}, u32[]{:S(2)}, u32[]{:S(2)}) collective-permute-start(bf16[1,192,128]{2,1,0:T(8,128)(2,1)S(1)} %shard_map.89), channel_id=1, source_target_pairs={{0,256},{1,769},{2,258},{3,771},{4,260},{5,773},{6,262},{7,775},{8... | collective-permute-start | bytes 147464 | tf_op jit(solution)/shard_map/ppermute | solution.py:264
  92.4 18.8 %collective-permute-start.6 = (bf16[1,192,128]{2,1,0:T(8,128)(2,1)S(1)}, bf16[1,192,128]{2,1,0:T(8,128)(2,1)S(1)}, u32[]{:S(2)}, u32[]{:S(2)}) collective-permute-start(bf16[1,192,128]{2,1,0:T(8,128)(2,1)S(1)} %shard_map.88), channel_id=1, source_target_pairs={{0,256},{1,769},{2,258},{3,771},{4,260},{5,773},{6,262},{7,775},{8... | collective-permute-start | bytes 147464 | tf_op jit(solution)/shard_map/ppermute | solution.py:264
  95.3 18.8 %collective-permute-start.8 = (bf16[1,192,128]{2,1,0:T(8,128)(2,1)S(1)}, bf16[1,192,128]{2,1,0:T(8,128)(2,1)S(1)}, u32[]{:S(2)}, u32[]{:S(2)}) collective-permute-start(bf16[1,192,128]{2,1,0:T(8,128)(2,1)S(1)} %fusion), channel_id=1, source_target_pairs={{0,768},{1,257},{2,770},{3,259},{4,772},{5,261},{6,774},{7,263},{8... | collective-permute-start | bytes 147464 | tf_op jit(solution)/shard_map/ppermute | solution.py:264

commit v10 on v9

--- a/solution.py
+++ b/solution.py
@@ -14,6 +14,7 @@
 DPX = ("dp", "expert")
 SMEM = pl.BlockSpec(memory_space=pltpu.SMEM)
 VMEM = pl.BlockSpec(memory_space=pltpu.VMEM)
+ANY = pl.BlockSpec(memory_space=pl.ANY)
 HBM = pl.BlockSpec(memory_space=pltpu.HBM)
 DMA = pltpu.SemaphoreType.DMA
 
@@ -110,10 +111,15 @@
     out_ref[...] = (backward * linear * curvature * probe_pre).astype(BF16)
 
 
-def fan_kernel(tan_ref, moved_ref, out_ref, mine_ref):
-    for i in range(ZLO):
-        out_ref[i] = tan_ref[...]
-    mine_ref[...] = moved_ref[...]
+def fan_kernel(tan_ref, moved_ref, out_ref, mine_ref, sems):
+    del moved_ref, mine_ref
+    copies = [
+        pltpu.make_async_copy(tan_ref, out_ref.at[i], sems.at[i]) for i in range(ZLO)
+    ]
+    for copy in copies:
+        copy.start()
+    for copy in copies:
+        copy.wait()
 
 
 def outer_kernel(flips, at_ref, tan_ref, own_ref, oth_ref, out_ref):
@@ -229,9 +235,12 @@
     tangent, mine = call(
         fan_kernel,
         [sds((ZLO, hid, CAP), BF16), sds((WIN, feats, CAP), BF16)],
-        [VMEM, VMEM],
+        [VMEM, ANY],
         0,
         1 << 19,
+        [DMA((ZLO,))],
+        out_specs=[ANY, ANY],
+        input_output_aliases={1: 1},
     )(tangent, moved)
 
     ring = [mine]

time: 115 us -> 115 us (level)
  no operation moved by 1% of the time
where the time goes in v10:
time: 115 us
  starting transfers between devices  62.5 us (54%)
  blocking collectives  24 us (21%)
  waiting for transfers between devices  16.8 us (15%)
  Pallas kernels  10.4 us (9%)
    ppermute x3, starting transfers between devices, exchange(): return lax.ppermute(value, DPX, perm)  31.3 us
    all_to_all x1, blocking collectives, on_device(): lax.all_to_all(send, 'expert', split_axis=0, concat_axis=0, tiled=True, a...  24 us
    all_to_all x1, starting transfers between devices, on_device(): lax.all_to_all(tangent, 'dp', split_axis=0, concat_axis=0, tiled=True, ax...  15.1 us
    ppermute x3, starting transfers between devices, on_device(): ring.append(lax.ppermute(mine, 'expert', perm))  8.26 us
    ppermute x3, waiting for transfers between devices, on_device(): ring.append(lax.ppermute(mine, 'expert', perm))  6.14 us
    ppermute x3, waiting for transfers between devices, exchange(): return lax.ppermute(value, DPX, perm)  5.12 us
    ppermute x1, starting transfers between devices, on_device(): moved = lax.ppermute(picked, DPX, perm)  3.93 us
    pallas_call x1, Pallas kernels, on_device(): call(own_kernel, sds((4, hid, CAP), F32), [SMEM, VMEM] + [HBM] * 4, 4 * h...  2.62 us
  transfers between devices with their start and end apart: 10, of which 7 were waited for; matrix products, arithmetic and copies ran while one was open for 0% of the time, Pallas kernels for 6%

profile of v10, /device:TPU:32, one launch (start us, length us, event | category | flops | bytes accessed | tf_op | source)
XLA Modules:
  0.0 114.8 jit_solution(5174962702573094911)
XLA Ops:
  0.0 1.9 %shard_map.82 = bf16[16,256,128]{2,1,0:T(8,128)(2,1)S(1)} custom-call(s32[8,1024]{1,0:T(8,128)} %bitcast.17, f32[8,1024]{1,0:T(8,128)} %bitcast.18, bf16[1024,128]{1,0:T(8,128)(2,1)} %tok_hbm.1, bf16[1024,128]{1,0:T(8,128)(2,1)} %cot_hbm.1), custom_call_target="tpu_custom_call" | custom-call | flops 268435456 | bytes 2097152 | tf_op jit(solution)/shard_map/pallas_call | solution.py:180
  1.9 24.0 %all_to_all.10.rows_ref = bf16[16,256,128]{2,1,0:T(8,128)(2,1)S(1)} all-to-all(bf16[16,256,128]{2,1,0:T(8,128)(2,1)S(1)} %shard_map.82), channel_id=1, replica_groups={{0,2,4,6,8,10,12,14,16,18,20,22,24,26,28,30},{1,3,5,7,9,11,13,15,17,19,..., dimensions={0} | all-to-all | bytes 2097152 | tf_op jit(solution)/shard_map/all_to_all | solution.py:195
  25.8 1.9 %collective-permute-start = (bf16[16,256,128]{2,1,0:T(8,128)(2,1)S(1)}, bf16[16,256,128]{2,1,0:T(8,128)(2,1)S(1)}, u32[]{:S(2)}, u32[]{:S(2)}) collective-permute-start(bf16[16,256,128]{2,1,0:T(8,128)(2,1)S(1)} %all_to_all.10.rows_ref), channel_id=1, source_target_pairs={{0,1},{1,0},{2,3},{3,2},{4,5},{5,4},{6,7},{7,6},{8,9},{9,8},{10,11... | collective-permute-start | bytes 3145736 | tf_op jit(solution)/shard_map/ppermute | solution.py:199
  27.9 3.9 %collective-permute-start.1 = (bf16[4,128,128]{2,1,0:T(8,128)(2,1)S(1)}, bf16[4,128,128]{2,1,0:T(8,128)(2,1)S(1)}, u32[]{:S(2)}, u32[]{:S(2)}) collective-permute-start(bf16[4,128,128]{2,1,0:T(8,128)(2,1)S(1)} %shard_map.85), channel_id=1, source_target_pairs={{0,0},{1,160},{2,66},{3,226},{4,132},{5,36},{6,198},{7,102},{8,8},... | collective-permute-start | bytes 393224 | tf_op jit(solution)/shard_map/ppermute | solution.py:214
  31.8 2.6 %shard_map.83.acc_ref = f32[4,192,128]{2,1,0:T(8,128)S(1)} custom-call(s32[1]{0:T(128)} %bitcast.1.c_ref, bf16[16,256,128]{2,1,0:T(8,128)(2,1)S(1)} %all_to_all.10.rows_ref, bf16[192,4096]{1,0:T(8,128)(2,1)} %g_hbm.3, bf16[192,4096]{1,0:T(8,128)(2,1)} %u_hbm.3, bf16[192,4096]{1,0:T(8,128)(2,1)} %p_hbm.3, bf16[192,4096]{1,0:T(8,128)(2,1)} %d_hbm.3), custom_call_target="tpu_custom_call" | custom-call | flops 402653184 | bytes 4194304 | tf_op jit(solution)/shard_map/pallas_call | solution.py:218
  34.4 0.0 collective-permute-done.rows_ref
  34.5 2.6 %shard_map.84.tan_ref = bf16[192,128]{1,0:T(8,128)(2,1)S(1)} custom-call(s32[1]{0:T(128)} %bitcast.1.c_ref, bf16[16,256,128]{2,1,0:T(8,128)(2,1)S(1)} %collective-permute-done.rows_ref, bf16[192,4096]{1,0:T(8,128)(2,1)} %g_hbm.3, bf16[192,4096]{1,0:T(8,128)(2,1)} %u_hbm.3, bf16[192,4096]{1,0:T(8,128)(2,1)} %p_hbm.3, bf16[192,4096]{1,0:T(8,128)(2,1)} %d_hbm.3, ...), custom_call_target="tpu_custom_call" | custom-call | flops 402653184 | bytes 4194304 | tf_op jit(solution)/shard_map/pallas_call | solution.py:226
  37.1 1.3 %collective-permute-done.1.moved_ref = bf16[4,128,128]{2,1,0:T(8,128)(2,1)S(1)} collective-permute-done((bf16[4,128,128]{2,1,0:T(8,128)(2,1)S(1)}, bf16[4,128,128]{2,1,0:T(8,128)(2,1)S(1)}, u32[]{:S(2)}, u32[]{:S(2)}) %collective-permute-start.1) | collective-permute-done | bytes 131104 | tf_op jit(solution)/shard_map/ppermute | solution.py:214
  38.4 0.8 shard_map.86
  39.2 15.1 %all-to-all-start.1 = ((bf16[8,192,128]{2,1,0:T(8,128)(2,1)}), bf16[8,192,128]{2,1,0:T(8,128)(2,1)S(1)}, u32[]{:S(2)}, u32[]{:S(2)}) async-start(bf16[8,192,128]{2,1,0:T(8,128)(2,1)} %get-tuple-element.7), calls=%async_computation.1 | async-start | bytes 786432 | tf_op jit(solution)/shard_map/all_to_all | solution.py:254
  54.3 3.1 %collective-permute-start.4 = (bf16[4,128,128]{2,1,0:T(8,128)(2,1)S(1)}, bf16[4,128,128]{2,1,0:T(8,128)(2,1)S(1)}, u32[]{:S(2)}, u32[]{:S(2)}) collective-permute-start(bf16[4,128,128]{2,1,0:T(8,128)(2,1)S(1)} %get-tuple-element.8), channel_id=1, source_target_pairs={{0,6},{1,7},{2,0},{3,1},{4,2},{5,3},{6,4},{7,5},{8,14},{9,15},{10,... | collective-permute-start | bytes 393224 | tf_op jit(solution)/shard_map/ppermute | solution.py:249
  57.5 3.2 %collective-permute-start.3 = (bf16[4,128,128]{2,1,0:T(8,128)(2,1)S(1)}, bf16[4,128,128]{2,1,0:T(8,128)(2,1)S(1)}, u32[]{:S(2)}, u32[]{:S(2)}) collective-permute-start(bf16[4,128,128]{2,1,0:T(8,128)(2,1)S(1)} %get-tuple-element.8), channel_id=1, source_target_pairs={{0,4},{1,5},{2,6},{3,7},{4,0},{5,1},{6,2},{7,3},{8,12},{9,13},{10,... | collective-permute-start | bytes 393224 | tf_op jit(solution)/shard_map/ppermute | solution.py:249
  60.7 1.9 %collective-permute-start.2 = (bf16[4,128,128]{2,1,0:T(8,128)(2,1)S(1)}, bf16[4,128,128]{2,1,0:T(8,128)(2,1)S(1)}, u32[]{:S(2)}, u32[]{:S(2)}) collective-permute-start(bf16[4,128,128]{2,1,0:T(8,128)(2,1)S(1)} %get-tuple-element.8), channel_id=1, source_target_pairs={{0,2},{1,3},{2,4},{3,5},{4,6},{5,7},{6,0},{7,1},{8,10},{9,11},{10,... | collective-permute-start | bytes 393224 | tf_op jit(solution)/shard_map/ppermute | solution.py:249
  62.6 0.0 collective-permute-done.4
  62.6 4.4 %collective-permute-done.3 = bf16[4,128,128]{2,1,0:T(8,128)(2,1)S(1)} collective-permute-done((bf16[4,128,128]{2,1,0:T(8,128)(2,1)S(1)}, bf16[4,128,128]{2,1,0:T(8,128)(2,1)S(1)}, u32[]{:S(2)}, u32[]{:S(2)}) %collective-permute-start.3) | collective-permute-done | bytes 131104 | tf_op jit(solution)/shard_map/ppermute | solution.py:249
  67.0 1.8 %collective-permute-done.2 = bf16[4,128,128]{2,1,0:T(8,128)(2,1)S(1)} collective-permute-done((bf16[4,128,128]{2,1,0:T(8,128)(2,1)S(1)}, bf16[4,128,128]{2,1,0:T(8,128)(2,1)S(1)}, u32[]{:S(2)}, u32[]{:S(2)}) %collective-permute-start.2) | collective-permute-done | bytes 131104 | tf_op jit(solution)/shard_map/ppermute | solution.py:249
  68.8 0.1 pad_maximum_fusion.own_ref
  68.8 1.9 %collective-permute-start.5 = (bf16[4,4,128,128]{3,2,1,0:T(8,128)(2,1)S(1)}, bf16[4,4,128,128]{3,2,1,0:T(8,128)(2,1)S(1)}, u32[]{:S(2)}, u32[]{:S(2)}) collective-permute-start(bf16[4,4,128,128]{3,2,1,0:T(8,128)(2,1)S(1)} %pad_maximum_fusion.own_ref), channel_id=1, source_target_pairs={{0,1},{1,0},{2,3},{3,2},{4,5},{5,4},{6,7},{7,6},{8,9},{9,8},{10,11... | collective-permute-start | bytes 1572872 | tf_op jit(solution)/shard_map/ppermute | solution.py:251
  70.8 0.1 pad_add_fusion.at_ref
  70.9 1.8 %collective-permute-done.5.oth_ref = bf16[4,4,128,128]{3,2,1,0:T(8,128)(2,1)S(1)} collective-permute-done((bf16[4,4,128,128]{3,2,1,0:T(8,128)(2,1)S(1)}, bf16[4,4,128,128]{3,2,1,0:T(8,128)(2,1)S(1)}, u32[]{:S(2)}, u32[]{:S(2)}) %collective-permute-start.5) | collective-permute-done | bytes 524320 | tf_op jit(solution)/shard_map/ppermute | solution.py:251
  72.6 2.4 %all-to-all-done.1.tan_ref = bf16[8,192,128]{2,1,0:T(8,128)(2,1)S(1)} async-done(((bf16[8,192,128]{2,1,0:T(8,128)(2,1)}), bf16[8,192,128]{2,1,0:T(8,128)(2,1)S(1)}, u32[]{:S(2)}, u32[]{:S(2)}) %all-to-all-start.1) | async-done | bytes 393248 | tf_op jit(solution)/shard_map/all_to_all | solution.py:254
  75.1 0.8 shard_map.89
  75.9 15.7 %collective-permute-start.7 = (bf16[1,192,128]{2,1,0:T(8,128)(2,1)S(1)}, bf16[1,192,128]{2,1,0:T(8,128)(2,1)S(1)}, u32[]{:S(2)}, u32[]{:S(2)}) collective-permute-start(bf16[1,192,128]{2,1,0:T(8,128)(2,1)S(1)} %shard_map.89), channel_id=1, source_target_pairs={{0,256},{1,769},{2,258},{3,771},{4,260},{5,773},{6,262},{7,775},{8... | collective-permute-start | bytes 147464 | tf_op jit(solution)/shard_map/ppermute | solution.py:273
  91.6 0.8 shard_map.88
  92.4 1.9 %collective-permute-start.6 = (bf16[1,192,128]{2,1,0:T(8,128)(2,1)S(1)}, bf16[1,192,128]{2,1,0:T(8,128)(2,1)S(1)}, u32[]{:S(2)}, u32[]{:S(2)}) collective-permute-start(bf16[1,192,128]{2,1,0:T(8,128)(2,1)S(1)} %shard_map.88), channel_id=1, source_target_pairs={{0,256},{1,769},{2,258},{3,771},{4,260},{5,773},{6,262},{7,775},{8... | collective-permute-start | bytes 147464 | tf_op jit(solution)/shard_map/ppermute | solution.py:273
  94.4 0.9 shard_map.87
  95.3 0.0 collective-permute-done.7
  95.3 13.7 %collective-permute-start.8 = (bf16[1,192,128]{2,1,0:T(8,128)(2,1)S(1)}, bf16[1,192,128]{2,1,0:T(8,128)(2,1)S(1)}, u32[]{:S(2)}, u32[]{:S(2)}) collective-permute-start(bf16[1,192,128]{2,1,0:T(8,128)(2,1)S(1)} %fusion), channel_id=1, source_target_pairs={{0,768},{1,257},{2,770},{3,259},{4,772},{5,261},{6,774},{7,263},{8... | collective-permute-start | bytes 147464 | tf_op jit(solution)/shard_map/ppermute | solution.py:273
  109.0 2.7 %collective-permute-done.6 = bf16[1,192,128]{2,1,0:T(8,128)(2,1)S(1)} collective-permute-done((bf16[1,192,128]{2,1,0:T(8,128)(2,1)S(1)}, bf16[1,192,128]{2,1,0:T(8,128)(2,1)S(1)}, u32[]{:S(2)}, u32[]{:S(2)}) %collective-permute-start.6) | collective-permute-done | bytes 49184 | tf_op jit(solution)/shard_map/ppermute | solution.py:273
  111.7 2.4 %collective-permute-done.8 = bf16[1,192,128]{2,1,0:T(8,128)(2,1)S(1)} collective-permute-done((bf16[1,192,128]{2,1,0:T(8,128)(2,1)S(1)}, bf16[1,192,128]{2,1,0:T(8,128)(2,1)S(1)}, u32[]{:S(2)}, u32[]{:S(2)}) %collective-permute-start.8) | collective-permute-done | bytes 49184 | tf_op jit(solution)/shard_map/ppermute | solution.py:273
  114.1 0.6 fusion.3
  (2 shorter events, 0.0 us)
Async XLA Ops:
  25.8 8.6 %collective-permute-start = (bf16[16,256,128]{2,1,0:T(8,128)(2,1)S(1)}, bf16[16,256,128]{2,1,0:T(8,128)(2,1)S(1)}, u32[]{:S(2)}, u32[]{:S(2)}) collective-permute-start(bf16[16,256,128]{2,1,0:T(8,128)(2,1)S(1)} %all_to_all.10.rows_ref), channel_id=1, source_target_pairs={{0,1},{1,0},{2,3},{3,2},{4,5},{5,4},{6,7},{7,6},{8,9},{9,8},{10,11... | collective-permute-start | bytes 3145736 | tf_op jit(solution)/shard_map/ppermute | solution.py:199
  27.9 10.5 %collective-permute-start.1 = (bf16[4,128,128]{2,1,0:T(8,128)(2,1)S(1)}, bf16[4,128,128]{2,1,0:T(8,128)(2,1)S(1)}, u32[]{:S(2)}, u32[]{:S(2)}) collective-permute-start(bf16[4,128,128]{2,1,0:T(8,128)(2,1)S(1)} %shard_map.85), channel_id=1, source_target_pairs={{0,0},{1,160},{2,66},{3,226},{4,132},{5,36},{6,198},{7,102},{8,8},... | collective-permute-start | bytes 393224 | tf_op jit(solution)/shard_map/ppermute | solution.py:214
  39.2 35.9 %all-to-all-start.1 = ((bf16[8,192,128]{2,1,0:T(8,128)(2,1)}), bf16[8,192,128]{2,1,0:T(8,128)(2,1)S(1)}, u32[]{:S(2)}, u32[]{:S(2)}) async-start(bf16[8,192,128]{2,1,0:T(8,128)(2,1)} %get-tuple-element.7), calls=%async_computation.1 | async-start | bytes 786432 | tf_op jit(solution)/shard_map/all_to_all | solution.py:254
  54.3 8.3 %collective-permute-start.4 = (bf16[4,128,128]{2,1,0:T(8,128)(2,1)S(1)}, bf16[4,128,128]{2,1,0:T(8,128)(2,1)S(1)}, u32[]{:S(2)}, u32[]{:S(2)}) collective-permute-start(bf16[4,128,128]{2,1,0:T(8,128)(2,1)S(1)} %get-tuple-element.8), channel_id=1, source_target_pairs={{0,6},{1,7},{2,0},{3,1},{4,2},{5,3},{6,4},{7,5},{8,14},{9,15},{10,... | collective-permute-start | bytes 393224 | tf_op jit(solution)/shard_map/ppermute | solution.py:249
  57.5 9.5 %collective-permute-start.3 = (bf16[4,128,128]{2,1,0:T(8,128)(2,1)S(1)}, bf16[4,128,128]{2,1,0:T(8,128)(2,1)S(1)}, u32[]{:S(2)}, u32[]{:S(2)}) collective-permute-start(bf16[4,128,128]{2,1,0:T(8,128)(2,1)S(1)} %get-tuple-element.8), channel_id=1, source_target_pairs={{0,4},{1,5},{2,6},{3,7},{4,0},{5,1},{6,2},{7,3},{8,12},{9,13},{10,... | collective-permute-start | bytes 393224 | tf_op jit(solution)/shard_map/ppermute | solution.py:249
  60.7 8.1 %collective-permute-start.2 = (bf16[4,128,128]{2,1,0:T(8,128)(2,1)S(1)}, bf16[4,128,128]{2,1,0:T(8,128)(2,1)S(1)}, u32[]{:S(2)}, u32[]{:S(2)}) collective-permute-start(bf16[4,128,128]{2,1,0:T(8,128)(2,1)S(1)} %get-tuple-element.8), channel_id=1, source_target_pairs={{0,2},{1,3},{2,4},{3,5},{4,6},{5,7},{6,0},{7,1},{8,10},{9,11},{10,... | collective-permute-start | bytes 393224 | tf_op jit(solution)/shard_map/ppermute | solution.py:249
  68.8 3.8 %collective-permute-start.5 = (bf16[4,4,128,128]{3,2,1,0:T(8,128)(2,1)S(1)}, bf16[4,4,128,128]{3,2,1,0:T(8,128)(2,1)S(1)}, u32[]{:S(2)}, u32[]{:S(2)}) collective-permute-start(bf16[4,4,128,128]{3,2,1,0:T(8,128)(2,1)S(1)} %pad_maximum_fusion.own_ref), channel_id=1, source_target_pairs={{0,1},{1,0},{2,3},{3,2},{4,5},{5,4},{6,7},{7,6},{8,9},{9,8},{10,11... | collective-permute-start | bytes 1572872 | tf_op jit(solution)/shard_map/ppermute | solution.py:251
  75.9 19.4 %collective-permute-start.7 = (bf16[1,192,128]{2,1,0:T(8,128)(2,1)S(1)}, bf16[1,192,128]{2,1,0:T(8,128)(2,1)S(1)}, u32[]{:S(2)}, u32[]{:S(2)}) collective-permute-start(bf16[1,192,128]{2,1,0:T(8,128)(2,1)S(1)} %shard_map.89), channel_id=1, source_target_pairs={{0,256},{1,769},{2,258},{3,771},{4,260},{5,773},{6,262},{7,775},{8... | collective-permute-start | bytes 147464 | tf_op jit(solution)/shard_map/ppermute | solution.py:273
  92.4 19.3 %collective-permute-start.6 = (bf16[1,192,128]{2,1,0:T(8,128)(2,1)S(1)}, bf16[1,192,128]{2,1,0:T(8,128)(2,1)S(1)}, u32[]{:S(2)}, u32[]{:S(2)}) collective-permute-start(bf16[1,192,128]{2,1,0:T(8,128)(2,1)S(1)} %shard_map.88), channel_id=1, source_target_pairs={{0,256},{1,769},{2,258},{3,771},{4,260},{5,773},{6,262},{7,775},{8... | collective-permute-start | bytes 147464 | tf_op jit(solution)/shard_map/ppermute | solution.py:273
  95.3 18.8 %collective-permute-start.8 = (bf16[1,192,128]{2,1,0:T(8,128)(2,1)S(1)}, bf16[1,192,128]{2,1,0:T(8,128)(2,1)S(1)}, u32[]{:S(2)}, u32[]{:S(2)}) collective-permute-start(bf16[1,192,128]{2,1,0:T(8,128)(2,1)S(1)} %fusion), channel_id=1, source_target_pairs={{0,768},{1,257},{2,770},{3,259},{4,772},{5,261},{6,774},{7,263},{8... | collective-permute-start | bytes 147464 | tf_op jit(solution)/shard_map/ppermute | solution.py:273

commit v11 on v10

--- a/solution.py
+++ b/solution.py
@@ -123,15 +123,14 @@
 
 
 def outer_kernel(flips, at_ref, tan_ref, own_ref, oth_ref, out_ref):
-    x, c, zhi, turn = at_ref[0], at_ref[1], at_ref[2], at_ref[3]
+    c, zhi, turn = at_ref[0], at_ref[1], at_ref[2]
     for n, flip in enumerate(flips):
         dest = flipped(zhi, flip, c)
         acc = None
-        for dx in range(WIN):
-            chip = (x - dx + WIN) % WIN
+        for chip in range(WIN):
             blocks = [(turn - chip - core) % WIN * 2 + core for core in (c, 1 - c)]
             lhs = jnp.concatenate([tan_ref[b] for b in blocks], axis=1)
-            rhs = jnp.concatenate([own_ref[dx, dest], oth_ref[dx, dest]], axis=1)
+            rhs = jnp.concatenate([own_ref[chip, dest], oth_ref[chip, dest]], axis=1)
             part = lax.dot_general(
                 lhs, rhs, (((1,), (1,)), ((), ())), preferred_element_type=F32
             )
@@ -243,11 +242,8 @@
         input_output_aliases={1: 1},
     )(tangent, moved)
 
-    ring = [mine]
-    for dx in range(1, WIN):
-        perm = [(k, k // 8 * 8 + (k // 2 % 4 + dx) % 4 * 2 + k % 2) for k in range(32)]
-        ring.append(lax.ppermute(mine, "expert", perm))
-    own_t = jnp.stack(ring)
+    row = [[8 * y + c0 + 2 * i for i in range(WIN)] for y in range(WIN) for c0 in range(2)]
+    own_t = lax.all_gather(mine, "expert", axis_index_groups=row)
     oth_t = lax.ppermute(own_t, "expert", swap)
 
     near = [[8 * a + b for b in range(8)] for a in range(4)]
@@ -262,7 +258,7 @@
             [SMEM] + [VMEM] * 3,
             2 * len(flips) * hid * 1024 * CAP,
             2 << 20,
-        )(at[:4], tangents, own_t, oth_t)
+        )(at[1:4], tangents, own_t, oth_t)
 
     def exchange(value, flip):
         perm = [

time: 115 us -> 115 us (level)
  the two profiles are of different devices: /device:TPU:32 before, /device:TPU:6 now
where the time goes in v11:
time: 115 us; the launch traced here: 114 us
  starting transfers between devices  50 us (43%)
  blocking collectives  39.4 us (34%)
  waiting for transfers between devices  13.4 us (12%)
  Pallas kernels  10.4 us (9%)
    ppermute x3, starting transfers between devices, exchange(): return lax.ppermute(value, DPX, perm)  29.5 us
    all_to_all x1, blocking collectives, on_device(): lax.all_to_all(send, 'expert', split_axis=0, concat_axis=0, tiled=True, a...  26 us
    all_gather x1, blocking collectives, on_device(): own_t = lax.all_gather(mine, 'expert', axis_index_groups=row)  13.4 us
    all_to_all x1, starting transfers between devices, on_device(): lax.all_to_all(tangent, 'dp', split_axis=0, concat_axis=0, tiled=True, ax...  9.15 us
    ppermute x1, starting transfers between devices, on_device(): moved = lax.ppermute(picked, DPX, perm)  7.59 us
    ppermute x3, waiting for transfers between devices, exchange(): return lax.ppermute(value, DPX, perm)  6.73 us
    all_to_all x1, waiting for transfers between devices, on_device(): lax.all_to_all(tangent, 'dp', split_axis=0, concat_axis=0, tiled=True, ax...  4.91 us
    pallas_call x1, Pallas kernels, on_device(): call(own_kernel, sds((4, hid, CAP), F32), [SMEM, VMEM] + [HBM] * 4, 4 * h...  2.62 us
  transfers between devices with their start and end apart: 7, of which 4 were waited for; matrix products, arithmetic and copies ran while one was open for 0% of the time, Pallas kernels for 6%

profile of v11, /device:TPU:6, one launch (start us, length us, event | category | flops | bytes accessed | tf_op | source)
XLA Modules:
  0.0 114.2 jit_solution(4028359303511267695)
XLA Ops:
  0.0 1.9 %shard_map.82 = bf16[16,256,128]{2,1,0:T(8,128)(2,1)S(1)} custom-call(s32[8,1024]{1,0:T(8,128)} %bitcast.13, f32[8,1024]{1,0:T(8,128)} %bitcast.14, bf16[1024,128]{1,0:T(8,128)(2,1)} %tok_hbm.1, bf16[1024,128]{1,0:T(8,128)(2,1)} %cot_hbm.1), custom_call_target="tpu_custom_call" | custom-call | flops 268435456 | bytes 2097152 | tf_op jit(solution)/shard_map/pallas_call | solution.py:179
  1.9 26.0 %all_to_all.10.rows_ref = bf16[16,256,128]{2,1,0:T(8,128)(2,1)S(1)} all-to-all(bf16[16,256,128]{2,1,0:T(8,128)(2,1)S(1)} %shard_map.82), channel_id=1, replica_groups={{0,2,4,6,8,10,12,14,16,18,20,22,24,26,28,30},{1,3,5,7,9,11,13,15,17,19,..., dimensions={0} | all-to-all | bytes 2097152 | tf_op jit(solution)/shard_map/all_to_all | solution.py:194
  27.8 1.9 %collective-permute-start = (bf16[16,256,128]{2,1,0:T(8,128)(2,1)S(1)}, bf16[16,256,128]{2,1,0:T(8,128)(2,1)S(1)}, u32[]{:S(2)}, u32[]{:S(2)}) collective-permute-start(bf16[16,256,128]{2,1,0:T(8,128)(2,1)S(1)} %all_to_all.10.rows_ref), channel_id=1, source_target_pairs={{0,1},{1,0},{2,3},{3,2},{4,5},{5,4},{6,7},{7,6},{8,9},{9,8},{10,11... | collective-permute-start | bytes 3145736 | tf_op jit(solution)/shard_map/ppermute | solution.py:198
  29.9 7.6 %collective-permute-start.1 = (bf16[4,128,128]{2,1,0:T(8,128)(2,1)S(1)}, bf16[4,128,128]{2,1,0:T(8,128)(2,1)S(1)}, u32[]{:S(2)}, u32[]{:S(2)}) collective-permute-start(bf16[4,128,128]{2,1,0:T(8,128)(2,1)S(1)} %shard_map.85), channel_id=1, source_target_pairs={{0,0},{1,160},{2,66},{3,226},{4,132},{5,36},{6,198},{7,102},{8,8},... | collective-permute-start | bytes 393224 | tf_op jit(solution)/shard_map/ppermute | solution.py:213
  37.5 2.6 %shard_map.83.acc_ref = f32[4,192,128]{2,1,0:T(8,128)S(1)} custom-call(s32[1]{0:T(128)} %bitcast.c_ref, bf16[16,256,128]{2,1,0:T(8,128)(2,1)S(1)} %all_to_all.10.rows_ref, bf16[192,4096]{1,0:T(8,128)(2,1)} %g_hbm.3, bf16[192,4096]{1,0:T(8,128)(2,1)} %u_hbm.3, bf16[192,4096]{1,0:T(8,128)(2,1)} %p_hbm.3, bf16[192,4096]{1,0:T(8,128)(2,1)} %d_hbm.3), custom_call_target="tpu_custom_call" | custom-call | flops 402653184 | bytes 4194304 | tf_op jit(solution)/shard_map/pallas_call | solution.py:217
  40.1 0.0 collective-permute-done.rows_ref
  40.1 2.6 %shard_map.84.tan_ref = bf16[192,128]{1,0:T(8,128)(2,1)S(1)} custom-call(s32[1]{0:T(128)} %bitcast.c_ref, bf16[16,256,128]{2,1,0:T(8,128)(2,1)S(1)} %collective-permute-done.rows_ref, bf16[192,4096]{1,0:T(8,128)(2,1)} %g_hbm.3, bf16[192,4096]{1,0:T(8,128)(2,1)} %u_hbm.3, bf16[192,4096]{1,0:T(8,128)(2,1)} %p_hbm.3, bf16[192,4096]{1,0:T(8,128)(2,1)} %d_hbm.3, ...), custom_call_target="tpu_custom_call" | custom-call | flops 402653184 | bytes 4194304 | tf_op jit(solution)/shard_map/pallas_call | solution.py:225
  42.7 0.0 collective-permute-done.1.moved_ref
  42.7 0.8 shard_map.86
  43.5 9.1 %all-to-all-start.1 = ((bf16[8,192,128]{2,1,0:T(8,128)(2,1)}), bf16[8,192,128]{2,1,0:T(8,128)(2,1)S(1)}, u32[]{:S(2)}, u32[]{:S(2)}) async-start(bf16[8,192,128]{2,1,0:T(8,128)(2,1)} %get-tuple-element.7), calls=%async_computation.1 | async-start | bytes 786432 | tf_op jit(solution)/shard_map/all_to_all | solution.py:250
  52.7 13.4 %all-gather = bf16[16,128,128]{2,1,0:T(8,128)(2,1)S(1)} all-gather(bf16[4,128,128]{2,1,0:T(8,128)(2,1)S(1)} %get-tuple-element.8), channel_id=2, replica_groups={{0,2,4,6},{1,3,5,7},{8,10,12,14},{9,11,13,15},{16,18,20,22},{17,19,21,2..., dimensions={0}, use_global_device_ids=true | all-gather | bytes 655360 | tf_op jit(solution)/shard_map/all_gather | solution.py:246
  66.1 1.9 %collective-permute-start.2 = (bf16[4,4,128,128]{3,2,1,0:T(8,128)(2,1)S(1)}, bf16[4,4,128,128]{3,2,1,0:T(8,128)(2,1)S(1)}, u32[]{:S(2)}, u32[]{:S(2)}) collective-permute-start(bf16[4,4,128,128]{3,2,1,0:T(8,128)(2,1)S(1)} %bitcast.9), channel_id=1, source_target_pairs={{0,1},{1,0},{2,3},{3,2},{4,5},{5,4},{6,7},{7,6},{8,9},{9,8},{10,11... | collective-permute-start | bytes 1572872 | tf_op jit(solution)/shard_map/ppermute | solution.py:247
  68.0 0.1 pad_add_fusion.at_ref
  68.1 1.8 %collective-permute-done.2.oth_ref = bf16[4,4,128,128]{3,2,1,0:T(8,128)(2,1)S(1)} collective-permute-done((bf16[4,4,128,128]{3,2,1,0:T(8,128)(2,1)S(1)}, bf16[4,4,128,128]{3,2,1,0:T(8,128)(2,1)S(1)}, u32[]{:S(2)}, u32[]{:S(2)}) %collective-permute-start.2) | collective-permute-done | bytes 524320 | tf_op jit(solution)/shard_map/ppermute | solution.py:247
  69.9 4.9 %all-to-all-done.1.tan_ref = bf16[8,192,128]{2,1,0:T(8,128)(2,1)S(1)} async-done(((bf16[8,192,128]{2,1,0:T(8,128)(2,1)}), bf16[8,192,128]{2,1,0:T(8,128)(2,1)S(1)}, u32[]{:S(2)}, u32[]{:S(2)}) %all-to-all-start.1) | async-done | bytes 393248 | tf_op jit(solution)/shard_map/all_to_all | solution.py:250
  74.8 0.8 shard_map.89
  75.6 15.7 %collective-permute-start.4 = (bf16[1,192,128]{2,1,0:T(8,128)(2,1)S(1)}, bf16[1,192,128]{2,1,0:T(8,128)(2,1)S(1)}, u32[]{:S(2)}, u32[]{:S(2)}) collective-permute-start(bf16[1,192,128]{2,1,0:T(8,128)(2,1)S(1)} %shard_map.89), channel_id=1, source_target_pairs={{0,256},{1,769},{2,258},{3,771},{4,260},{5,773},{6,262},{7,775},{8... | collective-permute-start | bytes 147464 | tf_op jit(solution)/shard_map/ppermute | solution.py:269
  91.3 0.8 shard_map.88
  92.2 1.9 %collective-permute-start.3 = (bf16[1,192,128]{2,1,0:T(8,128)(2,1)S(1)}, bf16[1,192,128]{2,1,0:T(8,128)(2,1)S(1)}, u32[]{:S(2)}, u32[]{:S(2)}) collective-permute-start(bf16[1,192,128]{2,1,0:T(8,128)(2,1)S(1)} %shard_map.88), channel_id=1, source_target_pairs={{0,256},{1,769},{2,258},{3,771},{4,260},{5,773},{6,262},{7,775},{8... | collective-permute-start | bytes 147464 | tf_op jit(solution)/shard_map/ppermute | solution.py:269
  94.1 0.9 shard_map.87
  95.0 0.1 collective-permute-done.4
  95.1 11.8 %collective-permute-start.5 = (bf16[1,192,128]{2,1,0:T(8,128)(2,1)S(1)}, bf16[1,192,128]{2,1,0:T(8,128)(2,1)S(1)}, u32[]{:S(2)}, u32[]{:S(2)}) collective-permute-start(bf16[1,192,128]{2,1,0:T(8,128)(2,1)S(1)} %fusion), channel_id=1, source_target_pairs={{0,768},{1,257},{2,770},{3,259},{4,772},{5,261},{6,774},{7,263},{8... | collective-permute-start | bytes 147464 | tf_op jit(solution)/shard_map/ppermute | solution.py:269
  106.9 6.7 %collective-permute-done.3 = bf16[1,192,128]{2,1,0:T(8,128)(2,1)S(1)} collective-permute-done((bf16[1,192,128]{2,1,0:T(8,128)(2,1)S(1)}, bf16[1,192,128]{2,1,0:T(8,128)(2,1)S(1)}, u32[]{:S(2)}, u32[]{:S(2)}) %collective-permute-start.3) | collective-permute-done | bytes 49184 | tf_op jit(solution)/shard_map/ppermute | solution.py:269
  113.6 0.0 collective-permute-done.5
  113.6 0.6 fusion.3
  (2 shorter events, 0.0 us)
Async XLA Ops:
  27.8 12.3 %collective-permute-start = (bf16[16,256,128]{2,1,0:T(8,128)(2,1)S(1)}, bf16[16,256,128]{2,1,0:T(8,128)(2,1)S(1)}, u32[]{:S(2)}, u32[]{:S(2)}) collective-permute-start(bf16[16,256,128]{2,1,0:T(8,128)(2,1)S(1)} %all_to_all.10.rows_ref), channel_id=1, source_target_pairs={{0,1},{1,0},{2,3},{3,2},{4,5},{5,4},{6,7},{7,6},{8,9},{9,8},{10,11... | collective-permute-start | bytes 3145736 | tf_op jit(solution)/shard_map/ppermute | solution.py:198
  29.9 12.9 %collective-permute-start.1 = (bf16[4,128,128]{2,1,0:T(8,128)(2,1)S(1)}, bf16[4,128,128]{2,1,0:T(8,128)(2,1)S(1)}, u32[]{:S(2)}, u32[]{:S(2)}) collective-permute-start(bf16[4,128,128]{2,1,0:T(8,128)(2,1)S(1)} %shard_map.85), channel_id=1, source_target_pairs={{0,0},{1,160},{2,66},{3,226},{4,132},{5,36},{6,198},{7,102},{8,8},... | collective-permute-start | bytes 393224 | tf_op jit(solution)/shard_map/ppermute | solution.py:213
  43.5 31.2 %all-to-all-start.1 = ((bf16[8,192,128]{2,1,0:T(8,128)(2,1)}), bf16[8,192,128]{2,1,0:T(8,128)(2,1)S(1)}, u32[]{:S(2)}, u32[]{:S(2)}) async-start(bf16[8,192,128]{2,1,0:T(8,128)(2,1)} %get-tuple-element.7), calls=%async_computation.1 | async-start | bytes 786432 | tf_op jit(solution)/shard_map/all_to_all | solution.py:250
  66.1 3.8 %collective-permute-start.2 = (bf16[4,4,128,128]{3,2,1,0:T(8,128)(2,1)S(1)}, bf16[4,4,128,128]{3,2,1,0:T(8,128)(2,1)S(1)}, u32[]{:S(2)}, u32[]{:S(2)}) collective-permute-start(bf16[4,4,128,128]{3,2,1,0:T(8,128)(2,1)S(1)} %bitcast.9), channel_id=1, source_target_pairs={{0,1},{1,0},{2,3},{3,2},{4,5},{5,4},{6,7},{7,6},{8,9},{9,8},{10,11... | collective-permute-start | bytes 1572872 | tf_op jit(solution)/shard_map/ppermute | solution.py:247
  75.6 19.5 %collective-permute-start.4 = (bf16[1,192,128]{2,1,0:T(8,128)(2,1)S(1)}, bf16[1,192,128]{2,1,0:T(8,128)(2,1)S(1)}, u32[]{:S(2)}, u32[]{:S(2)}) collective-permute-start(bf16[1,192,128]{2,1,0:T(8,128)(2,1)S(1)} %shard_map.89), channel_id=1, source_target_pairs={{0,256},{1,769},{2,258},{3,771},{4,260},{5,773},{6,262},{7,775},{8... | collective-permute-start | bytes 147464 | tf_op jit(solution)/shard_map/ppermute | solution.py:269
  92.2 21.4 %collective-permute-start.3 = (bf16[1,192,128]{2,1,0:T(8,128)(2,1)S(1)}, bf16[1,192,128]{2,1,0:T(8,128)(2,1)S(1)}, u32[]{:S(2)}, u32[]{:S(2)}) collective-permute-start(bf16[1,192,128]{2,1,0:T(8,128)(2,1)S(1)} %shard_map.88), channel_id=1, source_target_pairs={{0,256},{1,769},{2,258},{3,771},{4,260},{5,773},{6,262},{7,775},{8... | collective-permute-start | bytes 147464 | tf_op jit(solution)/shard_map/ppermute | solution.py:269
  95.1 18.5 %collective-permute-start.5 = (bf16[1,192,128]{2,1,0:T(8,128)(2,1)S(1)}, bf16[1,192,128]{2,1,0:T(8,128)(2,1)S(1)}, u32[]{:S(2)}, u32[]{:S(2)}) collective-permute-start(bf16[1,192,128]{2,1,0:T(8,128)(2,1)S(1)} %fusion), channel_id=1, source_target_pairs={{0,768},{1,257},{2,770},{3,259},{4,772},{5,261},{6,774},{7,263},{8... | collective-permute-start | bytes 147464 | tf_op jit(solution)/shard_map/ppermute | solution.py:269
